TPU v7x, 32 devices: a whole 2x2x4 slice. The times are simulated.
32 devices in a mesh: grp: 4 (over x, core), rep: 8 (over z, y).
Axes of the slice: x: 2, y: 2, z: 4, core: 2. Of those that a mesh axis runs over, the one named last changes fastest.
Arguments:
- blocks: bfloat16 [64, 64, 4096], P(('grp', 'rep')), may hold values from 0 to 10
- coords: int32 [64, 3], P(('grp', 'rep')), may hold values from 0 to 63, as said below
- factor_a: float32 [2048, 128], P(('grp', 'rep')), may hold values from 0 to 1
- factor_b: bfloat16 [4096, 128], P('grp'), may hold values from 0.049804688 to 1
- factor_c: bfloat16 [4096, 128], P('grp'), may hold values from 0.049804688 to 1
Outputs:
- updated_a: float32 [2048, 128], P(('grp', 'rep'))
Inputs may be any that keep to these rules, and one draw needn't show every extreme that they name: Row n of coords holds first, second and third coordinates below 32, 64, 64. Among the 2 blocks of one device, for each mode, the values coordinate // 8 (first mode) or coordinate // 16 (second and third) take any one value at most 2 times.
All inputs are finite; a program needn't handle non-finite values.
Results may differ from a plain program's by a relative error of at most 0.00072.
Values may be sent and summed in bfloat16 or wider, within the bound.
No kernel may reach another device: no remote copies, remote signals or barrier semaphores. Data moves between devices by JAX's collectives and lax.ppermute only.
A program may use at most 64 MiB of HBM per device.

v0:
```python
import jax
import jax.numpy as jnp
from jax import lax
from jax.sharding import PartitionSpec as P

R = 128
BS = 64
CAP = 2


def slot_of(owner):
    count = owner.shape[0]
    same_peer = owner[:, None] == owner[None, :]
    earlier = jnp.arange(count)[None, :] < jnp.arange(count)[:, None]
    return jnp.sum(jnp.logical_and(same_peer, earlier), axis=1)


def gram_of(factor):
    dims = (((0,), (0,)), ((), ()))
    return lax.dot_general(factor, factor, dims, preferred_element_type=jnp.float32)


def body(blocks, coords, factor_a, factor_b, factor_c):
    n_grp = lax.axis_size("grp")
    n_rep = lax.axis_size("rep")
    nblk_here = blocks.shape[0]
    jb_here = factor_b.shape[0] // BS
    ab_here = factor_a.shape[0] // BS
    part_here = ab_here * n_rep
    first_row = coords[:, 0]
    second_row = coords[:, 1]
    third_row = coords[:, 2]
    peer_b = second_row // jb_here
    peer_c = third_row // jb_here
    slot_b = slot_of(peer_b)
    slot_c = slot_of(peer_c) + CAP
    wanted = jnp.zeros((n_grp, 2 * CAP), jnp.int32)
    wanted = wanted.at[peer_b, slot_b].set(second_row % jb_here)
    wanted = wanted.at[peer_c, slot_c].set(third_row % jb_here + jb_here)
    lookup_rows = jnp.concatenate([factor_b, factor_c], 0).reshape(2 * jb_here, BS, R)
    fetched = lax.all_to_all(
        lookup_rows[lax.all_to_all(wanted, "grp", split_axis=0, concat_axis=0, tiled=True)],
        "grp",
        split_axis=0,
        concat_axis=0,
        tiled=True,
    )
    left_rows = fetched[peer_b, slot_b]
    right_rows = fetched[peer_c, slot_c]
    gram_b, gram_c = lax.psum((gram_of(factor_b), gram_of(factor_c)), "grp")
    khatri = (
        left_rows.astype(jnp.float32)[:, :, None, :] * right_rows.astype(jnp.float32)[:, None, :, :]
    )
    khatri = khatri.astype(jnp.bfloat16).reshape(nblk_here, BS * BS, R)
    partial_rows = jnp.einsum("bix,bxr->bir", blocks, khatri, preferred_element_type=jnp.float32)
    peer_a = first_row // part_here
    slot_a = slot_of(peer_a)
    outgoing = jnp.zeros((n_grp, CAP, BS, R), jnp.float32).at[peer_a, slot_a].set(partial_rows)
    target_ids = (
        jnp.zeros((n_grp, CAP), jnp.float32)
        .at[peer_a, slot_a]
        .set((first_row % part_here).astype(jnp.float32))
    )
    arrived, arrived_ids = (
        lax.all_to_all(outgoing, "grp", split_axis=0, concat_axis=0, tiled=True),
        lax.all_to_all(target_ids, "grp", split_axis=0, concat_axis=0, tiled=True),
    )
    dense_rows = jnp.zeros((part_here, BS, R), jnp.float32)
    dense_rows = dense_rows.at[arrived_ids.reshape(-1).astype(jnp.int32)].add(
        arrived.reshape(-1, BS, R)
    )
    mttkrp = lax.psum_scatter(
        dense_rows.reshape(part_here * BS, R), "rep", scatter_dimension=0, tiled=True
    )
    norm_b = jnp.sqrt(jnp.diagonal(gram_b))
    norm_c = jnp.sqrt(jnp.diagonal(gram_c))
    gram = (
        gram_b
        / (norm_b[:, None] * norm_b[None, :])
        * (gram_c / (norm_c[:, None] * norm_c[None, :]))
    )
    target = mttkrp / (norm_b * norm_c)[None, :]

    def sweep(owner_step, factor):
        for within in range(8):
            column = owner_step * 8 + within
            g_column = lax.dynamic_slice_in_dim(gram, column, 1, 1)
            predicted = jnp.dot(factor, g_column, precision=lax.Precision.HIGHEST)
            m_column = lax.dynamic_slice_in_dim(target, column, 1, 1)
            a_column = lax.dynamic_slice_in_dim(factor, column, 1, 1)
            pivot = lax.dynamic_slice_in_dim(g_column, column, 1, 0)
            updated = jnp.maximum(a_column + (m_column - predicted) / pivot, 0.0)
            factor = lax.dynamic_update_slice_in_dim(factor, updated, column, 1)
        return factor

    return lax.fori_loop(0, R // 8, sweep, factor_a)


def solution(mesh):
    placed = (
        P(("grp", "rep"), None, None),
        P(("grp", "rep"), None),
        P(("grp", "rep"), None),
        P("grp", None),
        P("grp", None),
    )
    return jax.shard_map(
        body, mesh=mesh, in_specs=placed, out_specs=P(("grp", "rep"), None), check_vma=False
    )
```

profile of v0, /device:TPU:0, one launch (start us, length us, event | category | flops | bytes accessed | tf_op | source)
XLA Modules:
  0.0 242.7 jit_solution(8180300417385501319)
XLA Ops:
  7.4 0.9 fusion.47
  9.5 1.9 scatter_fusion.1
  11.4 1.9 scatter_fusion.2
  13.3 4.2 %all-to-all-start.1 = ((s32[4,1,4]{2,1,0:T(1,128)}), s32[4,1,4]{2,1,0:T(1,128)S(1)}, u32[]{:S(2)}, u32[]{:S(2)}) async-start(s32[4,1,4]{2,1,0:T(1,128)} %bitcast.49), calls=%async_computation.1 | async-start | bytes 4096 | tf_op jit(solution)/shard_map/all_to_all | solution.py:42
  17.7 0.9 fusion.49
  20.1 1.2 all-to-all-done.1
  21.3 3.2 %all-to-all-start = ((f32[4,1,2]{2,1,0:T(1,128)}), f32[4,1,2]{2,1,0:T(1,128)S(1)}, u32[]{:S(2)}, u32[]{:S(2)}) async-start(f32[4,1,2]{2,1,0:T(1,128)} %copy.31), calls=%async_computation | async-start | bytes 4096 | tf_op jit(solution)/shard_map/all_to_all | solution.py:66
  24.6 1.3 gather_fusion
  25.9 2.3 all-to-all-done
  28.2 3.4 %all-to-all-start.2 = ((bf16[4,4,64,128]{3,2,1,0:T(8,128)(2,1)}), bf16[4,4,64,128]{3,2,1,0:T(8,128)(2,1)S(1)}, u32[]{:S(2)}, u32[]{:S(2)}) async-start(bf16[4,4,64,128]{3,2,1,0:T(8,128)(2,1)} %bitcast.51), calls=%async_computation.2 | async-start | bytes 524288 | tf_op jit(solution)/shard_map/all_to_all | solution.py:41
  31.6 0.9 fusion.50
  32.7 4.8 %all-to-all-done.2 = bf16[4,4,64,128]{3,2,1,0:T(8,128)(2,1)S(1)} async-done(((bf16[4,4,64,128]{3,2,1,0:T(8,128)(2,1)}), bf16[4,4,64,128]{3,2,1,0:T(8,128)(2,1)S(1)}, u32[]{:S(2)}, u32[]{:S(2)}) %all-to-all-start.2) | async-done | bytes 262176 | tf_op jit(solution)/shard_map/all_to_all | solution.py:41
  40.6 1.9 scatter_fusion.3
  42.5 3.4 %all-to-all-start.3 = ((f32[4,2,64,128]{3,2,1,0:T(8,128)}), f32[4,2,64,128]{3,2,1,0:T(8,128)S(1)}, u32[]{:S(2)}, u32[]{:S(2)}) async-start(f32[4,2,64,128]{3,2,1,0:T(8,128)} %scatter_fusion.3), calls=%async_computation.3 | async-start | bytes 524288 | tf_op jit(solution)/shard_map/all_to_all | solution.py:65
  46.0 6.1 %all-to-all-done.3 = f32[4,2,64,128]{3,2,1,0:T(8,128)S(1)} async-done(((f32[4,2,64,128]{3,2,1,0:T(8,128)}), f32[4,2,64,128]{3,2,1,0:T(8,128)S(1)}, u32[]{:S(2)}, u32[]{:S(2)}) %all-to-all-start.3) | async-done | bytes 262176 | tf_op jit(solution)/shard_map/all_to_all | solution.py:65
  52.1 0.9 scatter_fusion.4
  53.8 14.8 %all-reduce.3.cloned.1.call-done = (f32[128,128]{1,0:T(8,128)}, f32[128,128]{1,0:T(8,128)}) async-done(((f32[128,128]{1,0:T(8,128)}, f32[128,128]{1,0:T(8,128)}), (f32[128,128]{1,0:T(8,128)}, f32[128,128]{1,0:T(8,128)})) %all-reduce.3.cloned.1.call-update) | async-done | bytes 131088 | tf_op jit(solution)/shard_map/psum | solution.py:50
  68.6 1.9 gather_fusion.3
  70.5 1.9 gather_fusion.4
  72.5 1.0 divide_multiply_fusion
  73.5 42.4 %reduce-scatter.2.cloned.1.call-done = f32[64,128]{1,0:T(8,128)} async-done(((f32[512,128]{1,0:T(8,128)}), f32[64,128]{1,0:T(8,128)}) %reduce-scatter.2.cloned.1.call-update) | async-done | bytes 32784 | tf_op jit(solution)/shard_map/reduce_scatter | solution.py:72
  116.8 117.7 %while.16 = (s32[]{:T(128)}, f32[64,128]{0,1:T(8,128)S(1)}, f32[64,128]{0,1:T(8,128)S(1)}, f32[128,128]{0,1:T(8,128)S(1)}, s32[]{:T(128)}, /*index=5*/s32[]{:T(1...) while((s32[]{:T(128)}, f32[64,128]{0,1:T(8,128)S(1)}, ...), condition=%wide.region_12.13_spmd, body=%wide.region_11.12_spmd.sunk | while | flops 788522 | bytes 551765 | solution.py:96
  117.6 0.8 fusion.94
  119.2 0.9 fusion.96
  125.0 0.8 fusion.94
  126.6 0.9 fusion.96
  132.3 0.8 fusion.94
  133.9 0.9 fusion.96
  139.7 0.8 fusion.94
  141.3 0.9 fusion.96
  147.0 0.8 fusion.94
  148.7 0.9 fusion.96
  156.0 0.9 fusion.96
  163.4 0.9 fusion.96
  169.1 0.8 fusion.94
  170.7 0.9 fusion.96
  178.1 0.9 fusion.96
  183.8 0.8 fusion.94
  185.5 0.9 fusion.96
  191.2 0.8 fusion.94
  192.8 0.9 fusion.96
  200.2 0.9 fusion.96
  205.9 0.8 fusion.94
  207.5 0.9 fusion.96
  214.9 0.9 fusion.96
  222.3 0.9 fusion.96
  228.0 0.8 fusion.94
  229.6 0.9 fusion.96
  (301 shorter events, 102.2 us)
Async XLA Ops:
  7.4 32.0 %copy-start = (bf16[2,64,4096]{2,1,0:T(8,128)(2,1)S(1)}, bf16[2,64,4096]{2,1,0:T(8,128)(2,1)}, u32[]{:S(2)}) copy-start(bf16[2,64,4096]{2,1,0:T(8,128)(2,1)} %param.7) | copy-start | bytes 3145732
  7.4 10.3 %copy-start.1 = (bf16[1024,128]{1,0:T(8,128)(2,1)S(1)}, bf16[1024,128]{1,0:T(8,128)(2,1)}, u32[]{:S(2)}) copy-start(bf16[1024,128]{1,0:T(8,128)(2,1)} %param.10) | copy-start | bytes 786436
  7.4 11.2 %copy-start.2 = (bf16[1024,128]{1,0:T(8,128)(2,1)S(1)}, bf16[1024,128]{1,0:T(8,128)(2,1)}, u32[]{:S(2)}) copy-start(bf16[1024,128]{1,0:T(8,128)(2,1)} %param.11) | copy-start | bytes 786436
  13.3 8.0 %all-to-all-start.1 = ((s32[4,1,4]{2,1,0:T(1,128)}), s32[4,1,4]{2,1,0:T(1,128)S(1)}, u32[]{:S(2)}, u32[]{:S(2)}) async-start(s32[4,1,4]{2,1,0:T(1,128)} %bitcast.49), calls=%async_computation.1 | async-start | bytes 4096 | tf_op jit(solution)/shard_map/all_to_all | solution.py:42
  18.6 14.0 %copy-start.4 = (f32[64,128]{1,0:T(8,128)S(1)}, f32[64,128]{1,0:T(8,128)}, u32[]{:S(2)}) copy-start(f32[64,128]{1,0:T(8,128)} %param.9) | copy-start | bytes 98308
  21.3 6.9 %all-to-all-start = ((f32[4,1,2]{2,1,0:T(1,128)}), f32[4,1,2]{2,1,0:T(1,128)S(1)}, u32[]{:S(2)}, u32[]{:S(2)}) async-start(f32[4,1,2]{2,1,0:T(1,128)} %copy.31), calls=%async_computation | async-start | bytes 4096 | tf_op jit(solution)/shard_map/all_to_all | solution.py:66
  28.2 9.4 %all-to-all-start.2 = ((bf16[4,4,64,128]{3,2,1,0:T(8,128)(2,1)}), bf16[4,4,64,128]{3,2,1,0:T(8,128)(2,1)S(1)}, u32[]{:S(2)}, u32[]{:S(2)}) async-start(bf16[4,4,64,128]{3,2,1,0:T(8,128)(2,1)} %bitcast.51), calls=%async_computation.2 | async-start | bytes 524288 | tf_op jit(solution)/shard_map/all_to_all | solution.py:41
  31.6 37.0 %all-reduce.3.cloned.1.call-start = ((), (), s32[]{:S(2)}) async-start(), calls=%async_computation.6 | async-start | bytes 262144 | tf_op jit(solution)/shard_map/psum | solution.py:50
  42.5 9.6 %all-to-all-start.3 = ((f32[4,2,64,128]{3,2,1,0:T(8,128)}), f32[4,2,64,128]{3,2,1,0:T(8,128)S(1)}, u32[]{:S(2)}, u32[]{:S(2)}) async-start(f32[4,2,64,128]{3,2,1,0:T(8,128)} %scatter_fusion.3), calls=%async_computation.3 | async-start | bytes 524288 | tf_op jit(solution)/shard_map/all_to_all | solution.py:65
  45.9 70.0 %reduce-scatter.2.cloned.1.call-start = ((), (), s32[]{:S(2)}) async-start(), calls=%async_computation.5 | async-start | bytes 294912 | tf_op jit(solution)/shard_map/reduce_scatter | solution.py:72
  53.0 0.7 copy-start.3
Sparse Core Ops, SparseCore 0:
  34.8 33.7 all-reduce.2
Sparse Core Ops, SparseCore 1:
  53.8 62.1 reduce-scatter.1
where the time goes:
time: 245 us; the launch traced here: 243 us
  matrix products  103 us (42%)
  waiting for transfers between devices  71.6 us (29%)
  local copies, waits for them, and re-layouts  32.4 us (13%)
  between operations  15.1 us (6%)
  starting transfers between devices  14.3 us (6%)
  other arithmetic  4.02 us (2%)
    dot_general x128, matrix products, sweep(): predicted = jnp.dot(factor, g_column, precision=lax.Precision.HIGHEST)  101 us
    reduce_scatter x1, waiting for transfers between devices, body(): lax.psum_scatter(dense_rows.reshape(part_here * BS, R), 'rep', scatter_di...  42.4 us
    psum x1, waiting for transfers between devices, body(): gram_b, gram_c = lax.psum((gram_of(factor_b), gram_of(factor_c)), 'grp')  14.8 us
    dynamic_slice x16, local copies, waits for them, and re-layouts, sweep(): pivot = lax.dynamic_slice_in_dim(g_column, column, 1, 0)  11.2 us
    all_to_all x1, waiting for transfers between devices, body(): lax.all_to_all(outgoing, 'grp', split_axis=0, concat_axis=0, tiled=True)  6.11 us
  transfers between devices with their start and end apart: 6, of which 6 were waited for; matrix products, arithmetic and copies ran while one was open for 7% of the time, Pallas kernels for 0%

commit v1 on v0

v1 whole, which is shorter than its diff:
```python
import functools

import jax
import jax.numpy as jnp
from jax import lax
from jax.experimental import pallas as pl
from jax.experimental.pallas import tpu as pltpu
from jax.sharding import PartitionSpec as P

BS = 64
TILE = 8
CORES = 2
EXACT = lax.Precision.HIGHEST
VMEM = pl.BlockSpec(memory_space=pltpu.VMEM)
SMEM = pl.BlockSpec(memory_space=pltpu.SMEM)
ANY = pl.BlockSpec(memory_space=pl.ANY)


def shift_grp(value, n_grp, chips, swap):
    n_x = n_grp // CORES
    pairs = [
        (x * CORES + c, ((x + chips) % n_x) * CORES + (c ^ swap))
        for x in range(n_x)
        for c in range(CORES)
    ]
    return lax.ppermute(value, "grp", pairs)


def gather_kernel(n_ask, nblk, jb, here_ref, *refs):
    asks, (own_b, own_c, mate_b, mate_c) = refs[:n_ask], refs[n_ask : n_ask + 4]
    outs, sems = refs[n_ask + 4 : -1], refs[-1]
    core = lax.rem(here_ref[0], CORES)
    copies = []
    for a in range(n_ask):
        for mode, (own, mate) in enumerate(((own_b, mate_b), (own_c, mate_c))):
            for n in range(nblk):
                slot = mode * nblk + n
                local = lax.rem(asks[a][n, 1 + mode], CORES * jb)
                row = pl.multiple_of(lax.rem(local, jb) * BS, BS)
                is_own = lax.div(local, jb) == core
                dst, sem = outs[a].at[slot], sems.at[a * 2 * nblk + slot]
                from_own = pltpu.make_async_copy(own.at[pl.ds(row, BS)], dst, sem)
                from_mate = pltpu.make_async_copy(mate.at[pl.ds(row, BS)], dst, sem)
                pl.when(is_own)(from_own.start)
                pl.when(jnp.logical_not(is_own))(from_mate.start)
                copies.append(from_own)
    for copy in copies:
        copy.wait()


def gram_kernel(own_b, mate_b, own_c, mate_c, out_ref):
    dims = (((0,), (0,)), ((), ()))
    for mode, pair in enumerate(((own_b, mate_b), (own_c, mate_c))):
        total = 0.0
        for ref in pair:
            total += lax.dot_general(ref[...], ref[...], dims, preferred_element_type=jnp.float32)
        out_ref[mode] = total


def partial_kernel(n_x, nblk, jb, here_ref, ask_ref, *refs):
    found, blocks_ref, out_ref = refs[:n_x], refs[n_x], refs[n_x + 1]
    my_x = lax.div(here_ref[0], CORES)

    def rows_of(n, mode):
        chip = lax.div(ask_ref[n, 1 + mode], CORES * jb)
        slot = mode * nblk + n
        rows = found[0][slot]
        for d in range(1, n_x):
            rows = jnp.where(chip == lax.rem(my_x + d, n_x), found[d][slot], rows)
        return rows.astype(jnp.float32)

    step = 8
    for n in range(nblk):
        left, right = rows_of(n, 0), rows_of(n, 1)
        rank = left.shape[1]
        total = jnp.zeros((BS, rank), jnp.float32)
        for j in range(0, BS, step):
            khatri = (left[j : j + step, None, :] * right[None, :, :]).astype(jnp.bfloat16)
            total += jnp.dot(
                blocks_ref[n, :, j * BS : (j + step) * BS],
                khatri.reshape(step * BS, rank),
                preferred_element_type=jnp.float32,
            )
        out_ref[n, :BS] = total
        out_ref[n, BS:] = jnp.full((TILE, rank), ask_ref[n, 0].astype(jnp.float32))


def dispatch_kernel(nblk, n_rep, ab, here_ref, *refs):
    arrived, out_ref = refs[:-1], refs[-1]
    first = here_ref[0] * (n_rep * ab)

    def fill(owner, sub):
        target = (first + owner * ab + sub).astype(jnp.float32)
        total = None
        for ref in arrived:
            for n in range(nblk):
                term = jnp.where(ref[n, BS : BS + 1] == target, ref[n, :BS], 0.0)
                total = term if total is None else total + term
        out_ref[owner, sub * BS : (sub + 1) * BS] = total

    for sub in range(ab):
        if n_rep <= 8:
            for owner in range(n_rep):
                fill(owner, sub)
        else:
            pl.loop(0, n_rep)(functools.partial(fill, sub=sub))


def prepare_kernel(n_x, *refs):
    grams, a_ref, low_ref, pre_ref, scale_ref = refs[:n_x], *refs[n_x:]
    gram_b, gram_c = grams[0][0], grams[0][1]
    for ref in grams[1:]:
        gram_b += ref[0]
        gram_c += ref[1]
    shape = gram_b.shape
    at_row = lax.broadcasted_iota(jnp.int32, shape, 0)
    at_col = lax.broadcasted_iota(jnp.int32, shape, 1)

    def diagonal(square, axis):
        return jnp.sum(jnp.where(at_row == at_col, square, 0.0), axis=axis, keepdims=True)

    norm_b_row, norm_b_col = jnp.sqrt(diagonal(gram_b, 0)), jnp.sqrt(diagonal(gram_b, 1))
    norm_c_row, norm_c_col = jnp.sqrt(diagonal(gram_c, 0)), jnp.sqrt(diagonal(gram_c, 1))
    gram = gram_b / (norm_b_col * norm_b_row) * (gram_c / (norm_c_col * norm_c_row))
    pivot = diagonal(gram, 1)
    steps = gram.T / pivot
    low_ref[...] = jnp.where(at_col < at_row, steps, 0.0)
    later = jnp.where(at_col > at_row, steps, 0.0)
    pre_ref[...] = lax.dot_general(
        later, a_ref[...], (((1,), (1,)), ((), ())), precision=EXACT, preferred_element_type=jnp.float32
    )
    scale_ref[...] = jnp.broadcast_to(1.0 / (norm_b_col * norm_c_col * pivot), scale_ref.shape)


def sweep_kernel(n_rep, low_ref, pre_ref, scale_ref, sums_ref, out_ref):
    rank, rows = pre_ref.shape
    if n_rep <= 8:
        total = sums_ref[0]
        for i in range(1, n_rep):
            total += sums_ref[i]
    else:
        total = lax.fori_loop(1, n_rep, lambda i, acc: acc + sums_ref[i], sums_ref[0])
    start = total.T * scale_ref[...] - pre_ref[...]
    count = rank // TILE
    rest = [start[t * TILE : (t + 1) * TILE] for t in range(count)]
    for k in range(count):
        for s in range(TILE):
            column = k * TILE + s
            done = jnp.broadcast_to(jnp.maximum(rest[k], 0.0)[s : s + 1], (TILE, rows))
            for t in range(k if s < TILE - 1 else k + 1, count):
                weight = low_ref[t * TILE : (t + 1) * TILE, column : column + 1]
                rest[t] = rest[t] - weight * done
        rest[k] = jnp.maximum(rest[k], 0.0)
    out_ref[...] = jnp.concatenate(rest, 0).T


def body(blocks, coords, factor_a, factor_b, factor_c):
    n_grp = lax.axis_size("grp")
    n_rep = lax.axis_size("rep")
    n_x = n_grp // CORES
    nblk = blocks.shape[0]
    rank = factor_a.shape[1]
    jb = factor_b.shape[0] // BS
    ab = factor_a.shape[0] // BS
    here = lax.axis_index("grp").astype(jnp.int32).reshape(1)

    asks = [coords] + [shift_grp(coords, n_grp, d, 0) for d in range(1, n_x)]
    mate_b = shift_grp(factor_b, n_grp, 0, 1)
    mate_c = shift_grp(factor_c, n_grp, 0, 1)

    rows_shape = jax.ShapeDtypeStruct((2 * nblk, BS, rank), factor_b.dtype)
    answers = pl.pallas_call(
        functools.partial(gather_kernel, n_x, nblk, jb),
        out_shape=[rows_shape] * n_x,
        in_specs=[SMEM] * (1 + n_x) + [ANY] * 4,
        out_specs=[VMEM] * n_x,
        scratch_shapes=[pltpu.SemaphoreType.DMA((n_x * 2 * nblk,))],
        name="gather_rows",
    )(here, *asks, factor_b, factor_c, mate_b, mate_c)
    found = [answers[0]] + [shift_grp(answers[d], n_grp, -d, 0) for d in range(1, n_x)]

    chip_gram = pl.pallas_call(
        gram_kernel,
        out_shape=jax.ShapeDtypeStruct((2, rank, rank), jnp.float32),
        in_specs=[VMEM] * 4,
        out_specs=VMEM,
        name="chip_gram",
    )(factor_b, mate_b, factor_c, mate_c)
    grams = [chip_gram] + [shift_grp(chip_gram, n_grp, d, 0) for d in range(1, n_x)]

    partial = pl.pallas_call(
        functools.partial(partial_kernel, n_x, nblk, jb),
        out_shape=jax.ShapeDtypeStruct((nblk, BS + TILE, rank), jnp.float32),
        in_specs=[SMEM] * 2 + [VMEM] * (n_x + 1),
        out_specs=VMEM,
        name="block_products",
    )(here, coords, *found, blocks)
    arrived = [
        shift_grp(partial, n_grp, d, swap) if d or swap else partial
        for d in range(n_x)
        for swap in range(CORES)
    ]

    dense = pl.pallas_call(
        functools.partial(dispatch_kernel, nblk, n_rep, ab),
        out_shape=jax.ShapeDtypeStruct((n_rep, ab * BS, rank), jnp.float32),
        in_specs=[SMEM] + [VMEM] * n_grp,
        out_specs=VMEM,
        name="sum_by_owner",
    )(here, *arrived)
    sums = lax.all_to_all(dense, "rep", split_axis=0, concat_axis=0, tiled=True)

    low, pre, scale = pl.pallas_call(
        functools.partial(prepare_kernel, n_x),
        out_shape=[
            jax.ShapeDtypeStruct((rank, rank), jnp.float32),
            jax.ShapeDtypeStruct((rank, ab * BS), jnp.float32),
            jax.ShapeDtypeStruct((rank, ab * BS), jnp.float32),
        ],
        in_specs=[VMEM] * (n_x + 1),
        out_specs=[VMEM] * 3,
        name="prepare_sweep",
    )(*grams, factor_a)
    return pl.pallas_call(
        functools.partial(sweep_kernel, n_rep),
        out_shape=jax.ShapeDtypeStruct(factor_a.shape, jnp.float32),
        in_specs=[VMEM] * 4,
        out_specs=VMEM,
        name="sweep",
    )(low, pre, scale, sums)


def solution(mesh):
    placed = (
        P(("grp", "rep"), None, None),
        P(("grp", "rep"), None),
        P(("grp", "rep"), None),
        P("grp", None),
        P("grp", None),
    )
    return jax.shard_map(
        body, mesh=mesh, in_specs=placed, out_specs=P(("grp", "rep"), None), check_vma=False
    )
```

time: 245 us -> 46.5 us (0.19)
  matrix products: 103 us -> 0 us
  waiting for transfers between devices: 71.6 us -> 13.2 us
  local copies, waits for them, and re-layouts: 32.4 us -> 3.99 us
  between operations: 15.1 us -> 0.04 us
  Pallas kernels: 0 us -> 14.2 us
  other arithmetic: 4.02 us -> 0 us
    dot_general x131 -> x0, matrix products: 103 us -> none  [the longest x128 101 us: sweep(): predicted = jnp.dot(factor, g_column, precision=lax.Precision.HIGHEST)]
    reduce_scatter x1 -> x0, waiting for transfers between devices: 42.4 us -> none  [body(): lax.psum_scatter(dense_rows.reshape(part_here * BS, R), 'rep', scatter_di...]
    psum x1 -> x0, waiting for transfers between devices: 14.8 us -> none  [body(): gram_b, gram_c = lax.psum((gram_of(factor_b), gram_of(factor_c)), 'grp')]
    all_to_all x4 -> x1, waiting for transfers between devices: 14.4 us -> 0.01 us  [body(): sums = lax.all_to_all(dense, 'rep', split_axis=0, concat_axis=0, tiled=True)]
    pallas_call x0 -> x6, Pallas kernels: none -> 14.2 us  [the longest x1 3.19 us: body(): pl.pallas_call(functools.partial(sweep_kernel, n_rep), out_shape=jax.Shap...]
    ppermute x0 -> x8, waiting for transfers between devices: none -> 13.2 us  [shift_grp(): return lax.ppermute(value, 'grp', pairs)]
    dynamic_slice x16 -> x0, local copies, waits for them, and re-layouts: 11.2 us -> none  [sweep(): pivot = lax.dynamic_slice_in_dim(g_column, column, 1, 0)]
    ppermute x0 -> x8, starting transfers between devices: none -> 8.13 us  [shift_grp(): return lax.ppermute(value, 'grp', pairs)]
  transfers between devices with their start and end apart: 6 -> 9, of which waited for: 6 -> 5; matrix products, arithmetic and copies ran while one was open for 7% -> 0% of each run, Pallas kernels for 0% -> 9%
where the time goes in v1:
time: 46.5 us; the launch traced here: 46 us
  starting transfers between devices  14.7 us (32%)
  Pallas kernels  14.2 us (31%)
  waiting for transfers between devices  13.2 us (28%)
  local copies, waits for them, and re-layouts  3.99 us (9%)
    ppermute x8, waiting for transfers between devices, shift_grp(): return lax.ppermute(value, 'grp', pairs)  13.2 us
    ppermute x8, starting transfers between devices, shift_grp(): return lax.ppermute(value, 'grp', pairs)  8.13 us
    all_to_all x1, starting transfers between devices, body(): sums = lax.all_to_all(dense, 'rep', split_axis=0, concat_axis=0, tiled=True)  6.54 us
    unnamed x18, local copies, waits for them, and re-layouts  3.99 us
    pallas_call x1, Pallas kernels, body(): pl.pallas_call(functools.partial(sweep_kernel, n_rep), out_shape=jax.Shap...  3.19 us
    pallas_call x1, Pallas kernels, body(): pl.pallas_call(functools.partial(partial_kernel, n_x, nblk, jb), out_shap...  2.46 us
    pallas_call x1, Pallas kernels, body(): pl.pallas_call(gram_kernel, out_shape=jax.ShapeDtypeStruct((2, rank, rank...  2.32 us
    pallas_call x1, Pallas kernels, body(): pl.pallas_call(functools.partial(gather_kernel, n_x, nblk, jb), out_shape...  2.27 us
  transfers between devices with their start and end apart: 9, of which 5 were waited for; matrix products, arithmetic and copies ran while one was open for 0% of the time, Pallas kernels for 9%

profile of v1, /device:TPU:0, one launch (start us, length us, event | category | flops | bytes accessed | tf_op | source)
XLA Modules:
  0.0 46.0 jit_solution(9373522206112024285)
XLA Ops:
  0.0 0.5 collective-permute-start
  0.5 0.1 collective-permute-start.1
  0.5 2.9 %collective-permute-start.3 = (s32[2,3]{1,0:T(2,128)}, s32[2,3]{1,0:T(2,128)S(1)}, u32[]{:S(2)}, u32[]{:S(2)}) collective-permute-start(s32[2,3]{1,0:T(2,128)} %ask_ref.1), channel_id=1, source_target_pairs={{0,16},{8,24},{16,0},{24,8},{1,17},{9,25},{17,1},{25,9},{2,18},{10... | collective-permute-start | bytes 80 | tf_op jit(solution)/shard_map/ppermute | solution.py:26
  3.5 1.8 %collective-permute-done.3.refs_1_ = s32[2,3]{1,0:T(2,128)S(1)} collective-permute-done((s32[2,3]{1,0:T(2,128)}, s32[2,3]{1,0:T(2,128)S(1)}, u32[]{:S(2)}, u32[]{:S(2)}) %collective-permute-start.3) | collective-permute-done | bytes 56 | tf_op jit(solution)/shard_map/ppermute | solution.py:26
  5.2 0.0 copy-start.8
  5.2 0.0 collective-permute-done.mate_b.refs_4_
  5.2 0.0 copy-start.1
  5.2 0.0 collective-permute-done.1.mate_c.refs_5_
  5.2 0.0 copy-start.2
  5.2 0.5 %copy-done.8 = s32[2,3]{1,0:T(2,128)} copy-done((s32[2,3]{1,0:T(2,128)}, s32[2,3]{1,0:T(2,128)S(1)}, u32[]{:S(2)}) %copy-start.8) | copy-done | bytes 48
  5.8 0.1 copy-done.1
  5.9 0.1 copy-done.2
  6.0 2.3 %gather_rows.1 = (bf16[4,64,128]{2,1,0:T(8,128)(2,1)}, bf16[4,64,128]{2,1,0:T(8,128)(2,1)}) custom-call(s32[1]{0:T(128)} %bitcast.here_ref, s32[2,3]{1,0:T(2,128)} %ask_ref.1, s32[2,3]{1,0:T(2,128)} %copy-done.8, bf16[1024,128]{1,0:T(8,128)(2,1)} %refs_2_.4, bf16[1024,128]{1,0:T(8,128)(2,1)} %refs_3_.1, bf16[1024,128]{1,0:T(8,128)(2,1)} %copy-done.1, ...), custom_call_target="tpu_custom_call" | custom-call | tf_op jit(solution)/shard_map/gather_rows/pallas_call | solution.py:172
  8.3 2.1 %collective-permute-start.4 = (bf16[4,64,128]{2,1,0:T(8,128)(2,1)}, bf16[4,64,128]{2,1,0:T(8,128)(2,1)S(1)}, u32[]{:S(2)}, u32[]{:S(2)}) collective-permute-start(bf16[4,64,128]{2,1,0:T(8,128)(2,1)} %get-tuple-element.14), channel_id=1, source_target_pairs={{0,16},{8,24},{16,0},{24,8},{1,17},{9,25},{17,1},{25,9},{2,18},{10... | collective-permute-start | bytes 196616 | tf_op jit(solution)/shard_map/ppermute | solution.py:26
  10.4 2.5 %collective-permute-done.4.refs_1_ = bf16[4,64,128]{2,1,0:T(8,128)(2,1)S(1)} collective-permute-done((bf16[4,64,128]{2,1,0:T(8,128)(2,1)}, bf16[4,64,128]{2,1,0:T(8,128)(2,1)S(1)}, u32[]{:S(2)}, u32[]{:S(2)}) %collective-permute-start.4) | collective-permute-done | bytes 65568 | tf_op jit(solution)/shard_map/ppermute | solution.py:26
  12.8 0.0 copy-start.7
  12.8 0.6 %copy-done.7 = bf16[4,64,128]{2,1,0:T(8,128)(2,1)} copy-done((bf16[4,64,128]{2,1,0:T(8,128)(2,1)}, bf16[4,64,128]{2,1,0:T(8,128)(2,1)S(1)}, u32[]{:S(2)}) %copy-start.7) | copy-done | bytes 65560
  13.4 2.5 %block_products.1.refs_0_ = f32[2,72,128]{2,1,0:T(8,128)} custom-call(s32[1]{0:T(128)} %bitcast.here_ref, s32[2,3]{1,0:T(2,128)} %ask_ref.1, bf16[4,64,128]{2,1,0:T(8,128)(2,1)} %get-tuple-element.13.refs_0_, bf16[4,64,128]{2,1,0:T(8,128)(2,1)} %copy-done.7, bf16[2,64,4096]{2,1,0:T(8,128)(2,1)} %refs_2_.5), custom_call_target="tpu_custom_call" | custom-call | tf_op jit(solution)/shard_map/block_products/pallas_call | solution.py:191
  15.9 0.0 collective-permute-start.7
  15.9 2.0 %collective-permute-start.6 = (f32[2,72,128]{2,1,0:T(8,128)}, f32[2,72,128]{2,1,0:T(8,128)S(1)}, u32[]{:S(2)}, u32[]{:S(2)}) collective-permute-start(f32[2,72,128]{2,1,0:T(8,128)} %block_products.1.refs_0_), channel_id=1, source_target_pairs={{0,16},{8,24},{16,0},{24,8},{1,17},{9,25},{17,1},{25,9},{2,18},{10... | collective-permute-start | bytes 221192 | tf_op jit(solution)/shard_map/ppermute | solution.py:26
  18.0 0.1 collective-permute-start.5
  18.0 2.1 %collective-permute-done.7.refs_3_ = f32[2,72,128]{2,1,0:T(8,128)S(1)} collective-permute-done((f32[2,72,128]{2,1,0:T(8,128)}, f32[2,72,128]{2,1,0:T(8,128)S(1)}, u32[]{:S(2)}, u32[]{:S(2)}) %collective-permute-start.7) | collective-permute-done | bytes 73760 | tf_op jit(solution)/shard_map/ppermute | solution.py:26
  20.2 0.0 copy-start.4
  20.2 1.9 %collective-permute-done.6.refs_2_ = f32[2,72,128]{2,1,0:T(8,128)S(1)} collective-permute-done((f32[2,72,128]{2,1,0:T(8,128)}, f32[2,72,128]{2,1,0:T(8,128)S(1)}, u32[]{:S(2)}, u32[]{:S(2)}) %collective-permute-start.6) | collective-permute-done | bytes 73760 | tf_op jit(solution)/shard_map/ppermute | solution.py:26
  22.1 0.0 copy-start.5
  22.1 0.0 collective-permute-done.5.refs_1_
  22.1 0.0 copy-done.4
  22.1 0.6 %copy-done.5 = f32[2,72,128]{2,1,0:T(8,128)} copy-done((f32[2,72,128]{2,1,0:T(8,128)}, f32[2,72,128]{2,1,0:T(8,128)S(1)}, u32[]{:S(2)}) %copy-start.5) | copy-done | bytes 73752
  22.7 0.0 copy-start.6
  22.7 0.6 %copy-done.6 = f32[2,72,128]{2,1,0:T(8,128)} copy-done((f32[2,72,128]{2,1,0:T(8,128)}, f32[2,72,128]{2,1,0:T(8,128)S(1)}, u32[]{:S(2)}) %copy-start.6) | copy-done | bytes 73752
  23.3 1.9 %sum_by_owner.1 = f32[8,64,128]{2,1,0:T(8,128)} custom-call(s32[1]{0:T(128)} %bitcast.here_ref, f32[2,72,128]{2,1,0:T(8,128)} %block_products.1.refs_0_, f32[2,72,128]{2,1,0:T(8,128)} %copy-done.6, f32[2,72,128]{2,1,0:T(8,128)} %copy-done.5, f32[2,72,128]{2,1,0:T(8,128)} %copy-done.4), custom_call_target="tpu_custom_call" | custom-call | tf_op jit(solution)/shard_map/sum_by_owner/pallas_call | solution.py:204
  25.2 6.5 %all-to-all-start = ((f32[8,64,128]{2,1,0:T(8,128)}), f32[8,64,128]{2,1,0:T(8,128)S(1)}, u32[]{:S(2)}, u32[]{:S(2)}) async-start(f32[8,64,128]{2,1,0:T(8,128)} %sum_by_owner.1), calls=%async_computation | async-start | bytes 524288 | tf_op jit(solution)/shard_map/all_to_all | solution.py:211
  31.7 2.3 %chip_gram.1.refs_0_ = f32[2,128,128]{2,1,0:T(8,128)} custom-call(bf16[1024,128]{1,0:T(8,128)(2,1)} %refs_2_.4, bf16[1024,128]{1,0:T(8,128)(2,1)} %copy-done.1, bf16[1024,128]{1,0:T(8,128)(2,1)} %refs_3_.1, bf16[1024,128]{1,0:T(8,128)(2,1)} %copy-done.2), custom_call_target="tpu_custom_call" | custom-call | tf_op jit(solution)/shard_map/chip_gram/pallas_call | solution.py:182
  34.1 0.5 %collective-permute-start.2 = (f32[2,128,128]{2,1,0:T(8,128)}, f32[2,128,128]{2,1,0:T(8,128)S(1)}, u32[]{:S(2)}, u32[]{:S(2)}) collective-permute-start(f32[2,128,128]{2,1,0:T(8,128)} %chip_gram.1.refs_0_), channel_id=1, source_target_pairs={{0,16},{8,24},{16,0},{24,8},{1,17},{9,25},{17,1},{25,9},{2,18},{10... | collective-permute-start | bytes 393224 | tf_op jit(solution)/shard_map/ppermute | solution.py:26
  34.5 4.9 %collective-permute-done.2.refs_1_ = f32[2,128,128]{2,1,0:T(8,128)S(1)} collective-permute-done((f32[2,128,128]{2,1,0:T(8,128)}, f32[2,128,128]{2,1,0:T(8,128)S(1)}, u32[]{:S(2)}, u32[]{:S(2)}) %collective-permute-start.2) | collective-permute-done | bytes 131104 | tf_op jit(solution)/shard_map/ppermute | solution.py:26
  39.5 0.0 copy-start.3
  39.5 0.6 %copy-done.3 = f32[2,128,128]{2,1,0:T(8,128)} copy-done((f32[2,128,128]{2,1,0:T(8,128)}, f32[2,128,128]{2,1,0:T(8,128)S(1)}, u32[]{:S(2)}) %copy-start.3) | copy-done | bytes 131096
  40.1 2.0 %prepare_sweep.1 = (f32[128,128]{1,0:T(8,128)}, f32[128,64]{1,0:T(8,128)}, f32[128,64]{1,0:T(8,128)}) custom-call(f32[2,128,128]{2,1,0:T(8,128)} %chip_gram.1.refs_0_, f32[2,128,128]{2,1,0:T(8,128)} %copy-done.3, f32[64,128]{1,0:T(8,128)} %refs_2_.3), custom_call_target="tpu_custom_call" | custom-call | tf_op jit(solution)/shard_map/prepare_sweep/pallas_call | solution.py:213
  42.1 0.0 all-to-all-done.sums_ref
  42.2 0.0 copy-start
  42.2 0.7 %copy-done = f32[8,64,128]{2,1,0:T(8,128)} copy-done((f32[8,64,128]{2,1,0:T(8,128)}, f32[8,64,128]{2,1,0:T(8,128)S(1)}, u32[]{:S(2)}) %copy-start) | copy-done | bytes 262168
  42.9 3.2 %sweep.1 = f32[64,128]{1,0:T(8,128)} custom-call(f32[128,128]{1,0:T(8,128)} %get-tuple-element.10.low_ref, f32[128,64]{1,0:T(8,128)} %get-tuple-element.11.pre_ref, f32[128,64]{1,0:T(8,128)} %get-tuple-element.12.scale_ref, f32[8,64,128]{2,1,0:T(8,128)} %copy-done), custom_call_target="tpu_custom_call" | custom-call | tf_op jit(solution)/shard_map/sweep/pallas_call | solution.py:224
Async XLA Ops:
  0.0 5.2 %collective-permute-start = (bf16[1024,128]{1,0:T(8,128)(2,1)}, bf16[1024,128]{1,0:T(8,128)(2,1)S(1)}, u32[]{:S(2)}, u32[]{:S(2)}) collective-permute-start(bf16[1024,128]{1,0:T(8,128)(2,1)} %refs_2_.4), channel_id=1, source_target_pairs={{0,8},{8,0},{16,24},{24,16},{1,9},{9,1},{17,25},{25,17},{2,10},{10... | collective-permute-start | bytes 786440 | tf_op jit(solution)/shard_map/ppermute | solution.py:26
  0.5 4.8 %collective-permute-start.1 = (bf16[1024,128]{1,0:T(8,128)(2,1)}, bf16[1024,128]{1,0:T(8,128)(2,1)S(1)}, u32[]{:S(2)}, u32[]{:S(2)}) collective-permute-start(bf16[1024,128]{1,0:T(8,128)(2,1)} %refs_3_.1), channel_id=1, source_target_pairs={{0,8},{8,0},{16,24},{24,16},{1,9},{9,1},{17,25},{25,17},{2,10},{10... | collective-permute-start | bytes 786440 | tf_op jit(solution)/shard_map/ppermute | solution.py:26
  0.5 4.7 %collective-permute-start.3 = (s32[2,3]{1,0:T(2,128)}, s32[2,3]{1,0:T(2,128)S(1)}, u32[]{:S(2)}, u32[]{:S(2)}) collective-permute-start(s32[2,3]{1,0:T(2,128)} %ask_ref.1), channel_id=1, source_target_pairs={{0,16},{8,24},{16,0},{24,8},{1,17},{9,25},{17,1},{25,9},{2,18},{10... | collective-permute-start | bytes 80 | tf_op jit(solution)/shard_map/ppermute | solution.py:26
  5.2 0.6 %copy-start.8 = (s32[2,3]{1,0:T(2,128)}, s32[2,3]{1,0:T(2,128)S(1)}, u32[]{:S(2)}) copy-start(s32[2,3]{1,0:T(2,128)S(1)} %collective-permute-done.3.refs_1_) | copy-start | bytes 76
  5.2 0.7 %copy-start.1 = (bf16[1024,128]{1,0:T(8,128)(2,1)}, bf16[1024,128]{1,0:T(8,128)(2,1)S(1)}, u32[]{:S(2)}) copy-start(bf16[1024,128]{1,0:T(8,128)(2,1)S(1)} %collective-permute-done.mate_b.refs_4_) | copy-start | bytes 786436
  5.2 0.8 %copy-start.2 = (bf16[1024,128]{1,0:T(8,128)(2,1)}, bf16[1024,128]{1,0:T(8,128)(2,1)S(1)}, u32[]{:S(2)}) copy-start(bf16[1024,128]{1,0:T(8,128)(2,1)S(1)} %collective-permute-done.1.mate_c.refs_5_) | copy-start | bytes 786436
  8.3 4.5 %collective-permute-start.4 = (bf16[4,64,128]{2,1,0:T(8,128)(2,1)}, bf16[4,64,128]{2,1,0:T(8,128)(2,1)S(1)}, u32[]{:S(2)}, u32[]{:S(2)}) collective-permute-start(bf16[4,64,128]{2,1,0:T(8,128)(2,1)} %get-tuple-element.14), channel_id=1, source_target_pairs={{0,16},{8,24},{16,0},{24,8},{1,17},{9,25},{17,1},{25,9},{2,18},{10... | collective-permute-start | bytes 196616 | tf_op jit(solution)/shard_map/ppermute | solution.py:26
  12.8 0.6 %copy-start.7 = (bf16[4,64,128]{2,1,0:T(8,128)(2,1)}, bf16[4,64,128]{2,1,0:T(8,128)(2,1)S(1)}, u32[]{:S(2)}) copy-start(bf16[4,64,128]{2,1,0:T(8,128)(2,1)S(1)} %collective-permute-done.4.refs_1_) | copy-start | bytes 196612
  15.9 4.3 %collective-permute-start.7 = (f32[2,72,128]{2,1,0:T(8,128)}, f32[2,72,128]{2,1,0:T(8,128)S(1)}, u32[]{:S(2)}, u32[]{:S(2)}) collective-permute-start(f32[2,72,128]{2,1,0:T(8,128)} %block_products.1.refs_0_), channel_id=1, source_target_pairs={{0,24},{8,16},{16,8},{24,0},{1,25},{9,17},{17,9},{25,1},{2,26},{10... | collective-permute-start | bytes 221192 | tf_op jit(solution)/shard_map/ppermute | solution.py:26
  15.9 6.2 %collective-permute-start.6 = (f32[2,72,128]{2,1,0:T(8,128)}, f32[2,72,128]{2,1,0:T(8,128)S(1)}, u32[]{:S(2)}, u32[]{:S(2)}) collective-permute-start(f32[2,72,128]{2,1,0:T(8,128)} %block_products.1.refs_0_), channel_id=1, source_target_pairs={{0,16},{8,24},{16,0},{24,8},{1,17},{9,25},{17,1},{25,9},{2,18},{10... | collective-permute-start | bytes 221192 | tf_op jit(solution)/shard_map/ppermute | solution.py:26
  18.0 4.1 %collective-permute-start.5 = (f32[2,72,128]{2,1,0:T(8,128)}, f32[2,72,128]{2,1,0:T(8,128)S(1)}, u32[]{:S(2)}, u32[]{:S(2)}) collective-permute-start(f32[2,72,128]{2,1,0:T(8,128)} %block_products.1.refs_0_), channel_id=1, source_target_pairs={{0,8},{8,0},{16,24},{24,16},{1,9},{9,1},{17,25},{25,17},{2,10},{10... | collective-permute-start | bytes 221192 | tf_op jit(solution)/shard_map/ppermute | solution.py:26
  20.2 1.9 %copy-start.4 = (f32[2,72,128]{2,1,0:T(8,128)}, f32[2,72,128]{2,1,0:T(8,128)S(1)}, u32[]{:S(2)}) copy-start(f32[2,72,128]{2,1,0:T(8,128)S(1)} %collective-permute-done.7.refs_3_) | copy-start | bytes 221188
  22.1 0.6 %copy-start.5 = (f32[2,72,128]{2,1,0:T(8,128)}, f32[2,72,128]{2,1,0:T(8,128)S(1)}, u32[]{:S(2)}) copy-start(f32[2,72,128]{2,1,0:T(8,128)S(1)} %collective-permute-done.6.refs_2_) | copy-start | bytes 221188
  22.7 0.6 %copy-start.6 = (f32[2,72,128]{2,1,0:T(8,128)}, f32[2,72,128]{2,1,0:T(8,128)S(1)}, u32[]{:S(2)}) copy-start(f32[2,72,128]{2,1,0:T(8,128)S(1)} %collective-permute-done.5.refs_1_) | copy-start | bytes 221188
  25.2 16.9 %all-to-all-start = ((f32[8,64,128]{2,1,0:T(8,128)}), f32[8,64,128]{2,1,0:T(8,128)S(1)}, u32[]{:S(2)}, u32[]{:S(2)}) async-start(f32[8,64,128]{2,1,0:T(8,128)} %sum_by_owner.1), calls=%async_computation | async-start | bytes 524288 | tf_op jit(solution)/shard_map/all_to_all | solution.py:211
  34.1 5.4 %collective-permute-start.2 = (f32[2,128,128]{2,1,0:T(8,128)}, f32[2,128,128]{2,1,0:T(8,128)S(1)}, u32[]{:S(2)}, u32[]{:S(2)}) collective-permute-start(f32[2,128,128]{2,1,0:T(8,128)} %chip_gram.1.refs_0_), channel_id=1, source_target_pairs={{0,16},{8,24},{16,0},{24,8},{1,17},{9,25},{17,1},{25,9},{2,18},{10... | collective-permute-start | bytes 393224 | tf_op jit(solution)/shard_map/ppermute | solution.py:26
  39.5 0.6 %copy-start.3 = (f32[2,128,128]{2,1,0:T(8,128)}, f32[2,128,128]{2,1,0:T(8,128)S(1)}, u32[]{:S(2)}) copy-start(f32[2,128,128]{2,1,0:T(8,128)S(1)} %collective-permute-done.2.refs_1_) | copy-start | bytes 393220
  42.2 0.7 %copy-start = (f32[8,64,128]{2,1,0:T(8,128)}, f32[8,64,128]{2,1,0:T(8,128)S(1)}, u32[]{:S(2)}) copy-start(f32[8,64,128]{2,1,0:T(8,128)S(1)} %all-to-all-done.sums_ref) | copy-start | bytes 786436

commit v2 on v1

v2 whole, which is shorter than its diff:
```python
import functools

import jax
import jax.numpy as jnp
from jax import lax
from jax.experimental import pallas as pl
from jax.experimental.pallas import tpu as pltpu
from jax.sharding import PartitionSpec as P

BS = 64
TILE = 8
CORES = 2
EXACT = lax.Precision.HIGHEST
VMEM = pl.BlockSpec(memory_space=pltpu.VMEM)
HBM = pl.BlockSpec(memory_space=pltpu.HBM)
SMEM = pl.BlockSpec(memory_space=pltpu.SMEM)


def moves(n_grp, n_rep, to):
    pairs = []
    for g in range(n_grp):
        for rep in range(n_rep):
            x, c, to_rep = to(g // CORES, g % CORES, rep)
            pairs.append((g * n_rep + rep, (x * CORES + c) * n_rep + to_rep))
    return pairs


def partner(index, offset, size):
    return index ^ offset if size & (size - 1) == 0 else (index + offset) % size


def here():
    grp = lax.axis_index("grp")
    return lax.div(grp, CORES), lax.rem(grp, CORES), lax.axis_index("rep")


def load_kernel(b_ref, c_ref, own_b, own_c, sems):
    copies = [
        pltpu.make_async_copy(src, dst, sems.at[i])
        for i, (src, dst) in enumerate(((b_ref, own_b), (c_ref, own_c)))
    ]
    for copy in copies:
        copy.start()
    for copy in copies:
        copy.wait()


def gram_kernel(own_b, mate_b, own_c, mate_c, out_ref):
    _, core, _ = here()
    dims = (((0,), (0,)), ((), ()))

    def fill(*shards):
        total = 0.0
        for ref in shards:
            total += lax.dot_general(ref[...], ref[...], dims, preferred_element_type=jnp.float32)
        out_ref[...] = total

    pl.when(core == 0)(lambda: fill(own_b, mate_b))
    pl.when(core != 0)(lambda: fill(own_c, mate_c))


def row_block(own, mate, local, core, jb):
    row = pl.multiple_of(lax.rem(local, jb) * BS, BS)
    return jnp.where(lax.div(local, jb) == core, own[pl.ds(row, BS)], mate[pl.ds(row, BS)])


def gather_kernel(n_ask, nblk, jb, *refs):
    asks, factors, outs = refs[:n_ask], refs[n_ask : n_ask + 4], refs[n_ask + 4 :]
    _, core, _ = here()
    for ask, out in zip(asks, outs):
        for mode in range(2):
            for n in range(nblk):
                local = lax.rem(ask[n, 1 + mode], CORES * jb)
                out[mode * nblk + n] = row_block(*factors[2 * mode : 2 * mode + 2], local, core, jb)


def local_kernel(n_x, nblk, jb, ask_ref, *refs):
    factors, (rows_ref, far_ref, first_ref) = refs[:4], refs[4:]
    my_x, core, _ = here()
    for mode in range(2):
        for n in range(nblk):
            slot = mode * nblk + n
            wanted = ask_ref[n, 1 + mode]
            local = lax.rem(wanted, CORES * jb)
            rows_ref[slot] = row_block(*factors[2 * mode : 2 * mode + 2], local, core, jb)
            far = lax.rem(lax.div(wanted, CORES * jb) - my_x + n_x, n_x)
            far_ref[slot] = jnp.full(far_ref.shape[1:], far, jnp.int32)
    for n in range(nblk):
        first_ref[n] = jnp.full(first_ref.shape[1:], ask_ref[n, 0].astype(jnp.float32))


def partial_kernel(n_x, nblk, rows_ref, far_ref, first_ref, *refs):
    found, blocks_ref, out_ref = refs[:-2], refs[-2], refs[-1]

    def rows_of(n, mode):
        slot = mode * nblk + n
        rows = rows_ref[slot].astype(jnp.float32)
        for d in range(1, n_x):
            rows = jnp.where(far_ref[slot, :1] == d, found[d - 1][slot].astype(jnp.float32), rows)
        return rows

    step = 8
    for n in range(nblk):
        left, right = rows_of(n, 0), rows_of(n, 1)
        rank = left.shape[1]
        total = jnp.zeros((BS, rank), jnp.float32)
        for j in range(0, BS, step):
            khatri = (left[j : j + step, None, :] * right[None, :, :]).astype(jnp.bfloat16)
            total += jnp.dot(
                blocks_ref[n, :, j * BS : (j + step) * BS],
                khatri.reshape(step * BS, rank),
                preferred_element_type=jnp.float32,
            )
        out_ref[n, :BS] = total
        out_ref[n, BS:] = first_ref[n]


def owner_kernel(n_rep, near, ab, count, *refs):
    arrived, outs = refs[:count], refs[count:]
    my_x, core, rep = here()
    line = n_rep // near
    at, side = lax.div(rep, near), lax.rem(rep, near)
    for offset, out in enumerate(outs):
        if line & (line - 1) == 0:
            to_at = lax.bitwise_xor(at, offset)
        else:
            to_at = lax.rem(at + offset, line)
        to_core = core if offset == 0 else 1 - core
        first = ((my_x * CORES + to_core) * n_rep + to_at * near + side) * ab
        for sub in range(ab):
            target = (first + sub).astype(jnp.float32)
            total = None
            for ref in arrived:
                for n in range(ref.shape[0]):
                    term = jnp.where(ref[n, BS : BS + 1] == target, ref[n, :BS], 0.0)
                    total = term if total is None else total + term
            out[sub * BS : (sub + 1) * BS] = total


def prepare_kernel(gram_b_ref, gram_c_ref, a_ref, low_ref, pre_ref, scale_ref):
    gram_b, gram_c = gram_b_ref[...], gram_c_ref[...]
    shape = gram_b.shape
    at_row = lax.broadcasted_iota(jnp.int32, shape, 0)
    at_col = lax.broadcasted_iota(jnp.int32, shape, 1)

    def diagonal(square, axis):
        return jnp.sum(jnp.where(at_row == at_col, square, 0.0), axis=axis, keepdims=True)

    norm_b_row, norm_b_col = jnp.sqrt(diagonal(gram_b, 0)), jnp.sqrt(diagonal(gram_b, 1))
    norm_c_row, norm_c_col = jnp.sqrt(diagonal(gram_c, 0)), jnp.sqrt(diagonal(gram_c, 1))
    gram = gram_b / (norm_b_col * norm_b_row) * (gram_c / (norm_c_col * norm_c_row))
    pivot = diagonal(gram, 1)
    steps = gram.T / pivot
    low_ref[...] = jnp.where(at_col < at_row, steps, 0.0)
    later = jnp.where(at_col > at_row, steps, 0.0)
    pre_ref[...] = lax.dot_general(
        later, a_ref[...], (((1,), (1,)), ((), ())), precision=EXACT, preferred_element_type=jnp.float32
    )
    scale_ref[...] = jnp.broadcast_to(1.0 / (norm_b_col * norm_c_col * pivot), scale_ref.shape)


def sweep_kernel(low_ref, pre_ref, scale_ref, *refs):
    sums, out_ref = refs[:-1], refs[-1]
    rank, rows = pre_ref.shape
    total = sums[0][...]
    for ref in sums[1:]:
        total += ref[...]
    start = total.T * scale_ref[...] - pre_ref[...]
    count = rank // TILE
    rest = [start[t * TILE : (t + 1) * TILE] for t in range(count)]
    for k in range(count):
        for s in range(TILE):
            column = k * TILE + s
            done = jnp.broadcast_to(jnp.maximum(rest[k], 0.0)[s : s + 1], (TILE, rows))
            for t in range(k if s < TILE - 1 else k + 1, count):
                weight = low_ref[t * TILE : (t + 1) * TILE, column : column + 1]
                rest[t] = rest[t] - weight * done
        rest[k] = jnp.maximum(rest[k], 0.0)
    out_ref[...] = jnp.concatenate(rest, 0).T


def body(blocks, coords, factor_a, factor_b, factor_c):
    n_grp = lax.axis_size("grp")
    n_rep = lax.axis_size("rep")
    n_x = n_grp // CORES
    near = 2 if n_rep % 2 == 0 else 1
    line = n_rep // near
    nblk = blocks.shape[0]
    rank = factor_a.shape[1]
    jb = factor_b.shape[0] // BS
    ab = factor_a.shape[0] // BS
    params = pltpu.CompilerParams(vmem_limit_bytes=16 * 2**20)

    def move(value, chips, swap, beside=0, along=0):
        def to(x, c, rep):
            to_rep = partner(rep // near, along, line) * near + ((rep + beside) % near)
            return (x + chips) % n_x, c ^ swap, to_rep

        return lax.ppermute(value, ("grp", "rep"), moves(n_grp, n_rep, to))

    asks = [move(coords, d, 1) for d in range(1, n_x)]
    mate_b = move(factor_b, 0, 1)
    mate_c = move(factor_c, 0, 1)
    own_b, own_c = pl.pallas_call(
        load_kernel,
        out_shape=[jax.ShapeDtypeStruct(factor_b.shape, factor_b.dtype)] * 2,
        in_specs=[HBM] * 2,
        out_specs=[VMEM] * 2,
        scratch_shapes=[pltpu.SemaphoreType.DMA((2,))],
        compiler_params=params,
        name="load_shards",
    )(factor_b, factor_c)
    factors = (own_b, mate_b, own_c, mate_c)

    chip_gram = pl.pallas_call(
        gram_kernel,
        out_shape=jax.ShapeDtypeStruct((rank, rank), jnp.float32),
        in_specs=[VMEM] * 4,
        out_specs=VMEM,
        compiler_params=params,
        name="chip_gram",
    )(*factors)
    asks, chip_gram = lax.optimization_barrier((asks, chip_gram))

    answers = pl.pallas_call(
        functools.partial(gather_kernel, n_x - 1, nblk, jb),
        out_shape=[jax.ShapeDtypeStruct((2 * nblk, BS, rank), factor_b.dtype)] * (n_x - 1),
        in_specs=[SMEM] * (n_x - 1) + [VMEM] * 4,
        out_specs=[VMEM] * (n_x - 1),
        compiler_params=params,
        name="gather_rows",
    )(*asks, *factors)
    answers, chip_gram = lax.optimization_barrier((answers, chip_gram))
    found = [move(answers[d - 1], -d, 1) for d in range(1, n_x)]
    gram = chip_gram
    for d in range(1, n_x):
        gram = gram + move(chip_gram, d, 0)

    local = pl.pallas_call(
        functools.partial(local_kernel, n_x, nblk, jb),
        out_shape=[
            jax.ShapeDtypeStruct((2 * nblk, BS, rank), factor_b.dtype),
            jax.ShapeDtypeStruct((2 * nblk, TILE, rank), jnp.int32),
            jax.ShapeDtypeStruct((nblk, TILE, rank), jnp.float32),
        ],
        in_specs=[SMEM] + [VMEM] * 4,
        out_specs=[VMEM] * 3,
        compiler_params=params,
        name="local_rows",
    )(coords, *factors)
    found, local = lax.optimization_barrier((found, local))

    partial = pl.pallas_call(
        functools.partial(partial_kernel, n_x, nblk),
        out_shape=jax.ShapeDtypeStruct((nblk, BS + TILE, rank), jnp.float32),
        in_specs=[VMEM] * (3 + n_x),
        out_specs=VMEM,
        compiler_params=params,
        name="block_products",
    )(*local, *found, blocks)
    others = [
        move(partial, d, 1, beside)
        for d in range(n_x)
        for beside in range(near)
        if d or beside
    ]
    prepared = pl.pallas_call(
        prepare_kernel,
        out_shape=[
            jax.ShapeDtypeStruct((rank, rank), jnp.float32),
            jax.ShapeDtypeStruct((rank, ab * BS), jnp.float32),
            jax.ShapeDtypeStruct((rank, ab * BS), jnp.float32),
        ],
        in_specs=[VMEM] * 3,
        out_specs=[VMEM] * 3,
        compiler_params=params,
        name="prepare_sweep",
    )(gram, move(gram, 0, 1), factor_a)
    arrived = [partial, move(partial, 0, 1), *others, *(move(value, 0, 1) for value in others)]

    sums = pl.pallas_call(
        functools.partial(owner_kernel, n_rep, near, ab, len(arrived)),
        out_shape=[jax.ShapeDtypeStruct(factor_a.shape, jnp.float32)] * line,
        in_specs=[VMEM] * len(arrived),
        out_specs=[VMEM] * line,
        compiler_params=params,
        name="sum_by_owner",
    )(*arrived)
    sums = [sums[0]] + [move(sums[d], 0, 1, 0, d) for d in range(1, line)]

    return pl.pallas_call(
        sweep_kernel,
        out_shape=jax.ShapeDtypeStruct(factor_a.shape, jnp.float32),
        in_specs=[VMEM] * (3 + line),
        out_specs=VMEM,
        compiler_params=params,
        name="sweep",
    )(*prepared, *sums)


def solution(mesh):
    placed = (
        P(("grp", "rep"), None, None),
        P(("grp", "rep"), None),
        P(("grp", "rep"), None),
        P("grp", None),
        P("grp", None),
    )
    return jax.shard_map(
        body, mesh=mesh, in_specs=placed, out_specs=P(("grp", "rep"), None), check_vma=False
    )
```

time: 46.5 us -> 30.7 us (0.66)
  Pallas kernels: 14.2 us -> 4.9 us
  waiting for transfers between devices: 13.2 us -> 9.18 us
  local copies, waits for them, and re-layouts: 3.99 us -> 1.92 us
    pallas_call x6 -> x8, Pallas kernels: 14.2 us -> 4.9 us  [the longest x1 2.13 us: body(): pl.pallas_call(sweep_kernel, out_shape=jax.ShapeDtypeStruct(factor_a.shap...]
    all_to_all x1 -> x0, starting transfers between devices: 6.54 us -> none  [body(): sums = lax.all_to_all(dense, 'rep', split_axis=0, concat_axis=0, tiled=True)]
    ppermute x8 -> x16, starting transfers between devices: 8.13 us -> 14.4 us  [move(): return lax.ppermute(value, ('grp', 'rep'), moves(n_grp, n_rep, to))]
    ppermute x8 -> x16, waiting for transfers between devices: 13.2 us -> 9.18 us  [move(): return lax.ppermute(value, ('grp', 'rep'), moves(n_grp, n_rep, to))]
    unnamed x18 -> x10, local copies, waits for them, and re-layouts: 3.99 us -> 1.92 us
  transfers between devices with their start and end apart: 9 -> 16, of which waited for: 5 -> 6; matrix products, arithmetic and copies ran while one was open for 0% -> 0% of each run, Pallas kernels for 9% -> 5%
where the time goes in v2:
time: 30.7 us; the launch traced here: 30.6 us
  starting transfers between devices  14.4 us (47%)
  waiting for transfers between devices  9.18 us (30%)
  Pallas kernels  4.9 us (16%)
  local copies, waits for them, and re-layouts  1.92 us (6%)
    ppermute x16, starting transfers between devices, move(): return lax.ppermute(value, ('grp', 'rep'), moves(n_grp, n_rep, to))  14.4 us
    ppermute x16, waiting for transfers between devices, move(): return lax.ppermute(value, ('grp', 'rep'), moves(n_grp, n_rep, to))  9.18 us
    pallas_call x1, Pallas kernels, body(): pl.pallas_call(sweep_kernel, out_shape=jax.ShapeDtypeStruct(factor_a.shap...  2.13 us
    unnamed x10, local copies, waits for them, and re-layouts  1.92 us
  transfers between devices with their start and end apart: 16, of which 6 were waited for; matrix products, arithmetic and copies ran while one was open for 0% of the time, Pallas kernels for 5%

profile of v2, /device:TPU:0, one launch (start us, length us, event | category | flops | bytes accessed | tf_op | source)
XLA Modules:
  0.0 30.6 jit_solution(4470899324327845146)
XLA Ops:
  0.0 0.5 %collective-permute-start.1 = (bf16[1024,128]{1,0:T(8,128)(2,1)}, bf16[1024,128]{1,0:T(8,128)(2,1)S(1)}, u32[]{:S(2)}, u32[]{:S(2)}) collective-permute-start(bf16[1024,128]{1,0:T(8,128)(2,1)} %b_ref.1), channel_id=1, source_target_pairs={{0,8},{1,9},{2,10},{3,11},{4,12},{5,13},{6,14},{7,15},{8,0},{9,1},... | collective-permute-start | bytes 786440 | tf_op jit(solution)/shard_map/ppermute | solution.py:199
  0.5 0.1 collective-permute-start.2
  0.5 2.5 %collective-permute-start = (s32[2,3]{1,0:T(2,128)}, s32[2,3]{1,0:T(2,128)S(1)}, u32[]{:S(2)}, u32[]{:S(2)}) collective-permute-start(s32[2,3]{1,0:T(2,128)} %ask_ref.1), channel_id=1, source_target_pairs={{0,24},{1,25},{2,26},{3,27},{4,28},{5,29},{6,30},{7,31},{8,16},{9,... | collective-permute-start | bytes 80 | tf_op jit(solution)/shard_map/ppermute | solution.py:199
  3.1 0.9 %copy-done.1 = bf16[1024,128]{1,0:T(8,128)(2,1)S(1)} copy-done((bf16[1024,128]{1,0:T(8,128)(2,1)S(1)}, bf16[1024,128]{1,0:T(8,128)(2,1)}, u32[]{:S(2)}) %copy-start.1) | copy-done | bytes 262168
  4.0 0.9 %copy-done.2 = bf16[1024,128]{1,0:T(8,128)(2,1)S(1)} copy-done((bf16[1024,128]{1,0:T(8,128)(2,1)S(1)}, bf16[1024,128]{1,0:T(8,128)(2,1)}, u32[]{:S(2)}) %copy-start.2) | copy-done | bytes 262168
  5.0 0.1 load_shards.1
  5.0 0.0 collective-permute-done.1.mate_b.refs_2_.refs_1_
  5.0 0.0 collective-permute-done.2.mate_c.refs_4_.refs_3_
  5.0 0.4 %chip_gram.1 = f32[128,128]{1,0:T(8,128)S(1)} custom-call(bf16[1024,128]{1,0:T(8,128)(2,1)S(1)} %get-tuple-element.25.own_b.refs_1_.refs_0_, bf16[1024,128]{1,0:T(8,128)(2,1)S(1)} %collective-permute-done.1.mate_b.refs_2_.refs_1_, bf16[1024,128]{1,0:T(8,128)(2,1)S(1)} %get-tuple-element.26.own_c.refs_3_.refs_2_, ...), custom_call_target="tpu_custom_call" | custom-call | tf_op jit(solution)/shard_map/chip_gram/pallas_call | solution.py:215
  5.4 0.0 copy-start.4
  5.4 0.0 copy-start
  5.4 0.0 collective-permute-done.refs_0_
  5.4 0.6 %gather_rows.1 = bf16[4,64,128]{2,1,0:T(8,128)(2,1)S(1)} custom-call(s32[2,3]{1,0:T(2,128)S(1)} %collective-permute-done.refs_0_, bf16[1024,128]{1,0:T(8,128)(2,1)S(1)} %get-tuple-element.25.own_b.refs_1_.refs_0_, bf16[1024,128]{1,0:T(8,128)(2,1)S(1)} %collective-permute-done.1.mate_b.refs_2_.refs_1_, ...), custom_call_target="tpu_custom_call" | custom-call | tf_op jit(solution)/shard_map/gather_rows/pallas_call | solution.py:225
  6.1 1.0 %collective-permute-start.5 = (bf16[4,64,128]{2,1,0:T(8,128)(2,1)S(1)}, bf16[4,64,128]{2,1,0:T(8,128)(2,1)S(1)}, u32[]{:S(2)}, u32[]{:S(2)}) collective-permute-start(bf16[4,64,128]{2,1,0:T(8,128)(2,1)S(1)} %gather_rows.1), channel_id=1, source_target_pairs={{0,24},{1,25},{2,26},{3,27},{4,28},{5,29},{6,30},{7,31},{8,16},{9,... | collective-permute-start | bytes 196616 | tf_op jit(solution)/shard_map/ppermute | solution.py:199
  7.0 0.0 copy-done.4
  7.0 0.6 %local_rows.1 = (bf16[4,64,128]{2,1,0:T(8,128)(2,1)S(1)}, s32[4,8,128]{2,1,0:T(8,128)S(1)}, f32[2,8,128]{2,1,0:T(8,128)S(1)}) custom-call(s32[2,3]{1,0:T(2,128)S(1)} %copy-done.4, bf16[1024,128]{1,0:T(8,128)(2,1)S(1)} %get-tuple-element.25.own_b.refs_1_.refs_0_, bf16[1024,128]{1,0:T(8,128)(2,1)S(1)} %collective-permute-done.1.mate_b.refs_2_.refs_1_, ...), custom_call_target="tpu_custom_call" | custom-call | tf_op jit(solution)/shard_map/local_rows/pallas_call | solution.py:239
  7.7 2.2 %collective-permute-done.5.refs_0_ = bf16[4,64,128]{2,1,0:T(8,128)(2,1)S(1)} collective-permute-done((bf16[4,64,128]{2,1,0:T(8,128)(2,1)S(1)}, bf16[4,64,128]{2,1,0:T(8,128)(2,1)S(1)}, u32[]{:S(2)}, u32[]{:S(2)}) %collective-permute-start.5) | collective-permute-done | bytes 65568 | tf_op jit(solution)/shard_map/ppermute | solution.py:199
  9.9 0.0 copy-done
  9.9 0.5 %block_products.1.refs_0_ = f32[2,72,128]{2,1,0:T(8,128)S(1)} custom-call(bf16[4,64,128]{2,1,0:T(8,128)(2,1)S(1)} %get-tuple-element.37.rows_ref, s32[4,8,128]{2,1,0:T(8,128)S(1)} %get-tuple-element.38.far_ref, f32[2,8,128]{2,1,0:T(8,128)S(1)} %get-tuple-element.39.first_ref, bf16[4,64,128]{2,1,0:T(8,128)(2,1)S(1)} %collective-permute-done.5.refs_0_, ...), custom_call_target="tpu_custom_call" | custom-call | tf_op jit(solution)/shard_map/block_products/pallas_call | solution.py:253
  10.4 2.3 %collective-permute-start.9 = (f32[2,72,128]{2,1,0:T(8,128)S(1)}, f32[2,72,128]{2,1,0:T(8,128)S(1)}, u32[]{:S(2)}, u32[]{:S(2)}) collective-permute-start(f32[2,72,128]{2,1,0:T(8,128)S(1)} %block_products.1.refs_0_), channel_id=1, source_target_pairs={{0,25},{1,24},{2,27},{3,26},{4,29},{5,28},{6,31},{7,30},{8,17},{9,... | collective-permute-start | bytes 221192 | tf_op jit(solution)/shard_map/ppermute | solution.py:199
  12.7 0.5 %collective-permute-start.8 = (f32[2,72,128]{2,1,0:T(8,128)S(1)}, f32[2,72,128]{2,1,0:T(8,128)S(1)}, u32[]{:S(2)}, u32[]{:S(2)}) collective-permute-start(f32[2,72,128]{2,1,0:T(8,128)S(1)} %block_products.1.refs_0_), channel_id=1, source_target_pairs={{0,24},{1,25},{2,26},{3,27},{4,28},{5,29},{6,30},{7,31},{8,16},{9,... | collective-permute-start | bytes 221192 | tf_op jit(solution)/shard_map/ppermute | solution.py:199
  13.2 0.6 %collective-permute-start.7 = (f32[2,72,128]{2,1,0:T(8,128)S(1)}, f32[2,72,128]{2,1,0:T(8,128)S(1)}, u32[]{:S(2)}, u32[]{:S(2)}) collective-permute-start(f32[2,72,128]{2,1,0:T(8,128)S(1)} %block_products.1.refs_0_), channel_id=1, source_target_pairs={{0,9},{1,8},{2,11},{3,10},{4,13},{5,12},{6,15},{7,14},{8,1},{9,0},... | collective-permute-start | bytes 221192 | tf_op jit(solution)/shard_map/ppermute | solution.py:199
  13.7 1.2 %collective-permute-start.3 = (f32[128,128]{1,0:T(8,128)S(1)}, f32[128,128]{1,0:T(8,128)S(1)}, u32[]{:S(2)}, u32[]{:S(2)}) collective-permute-start(f32[128,128]{1,0:T(8,128)S(1)} %chip_gram.1), channel_id=1, source_target_pairs={{0,16},{1,17},{2,18},{3,19},{4,20},{5,21},{6,22},{7,23},{8,24},{9,... | collective-permute-start | bytes 196616 | tf_op jit(solution)/shard_map/ppermute | solution.py:199
  15.0 0.2 collective-permute-start.6
  15.1 0.2 collective-permute-done.9.refs_4_
  15.4 0.8 %collective-permute-start.12 = (f32[2,72,128]{2,1,0:T(8,128)S(1)}, f32[2,72,128]{2,1,0:T(8,128)S(1)}, u32[]{:S(2)}, u32[]{:S(2)}) collective-permute-start(f32[2,72,128]{2,1,0:T(8,128)S(1)} %collective-permute-done.9.refs_4_), channel_id=1, source_target_pairs={{0,8},{1,9},{2,10},{3,11},{4,12},{5,13},{6,14},{7,15},{8,0},{9,1},... | collective-permute-start | bytes 221192 | tf_op jit(solution)/shard_map/ppermute | solution.py:199
  16.1 1.1 %collective-permute-done.8.refs_3_ = f32[2,72,128]{2,1,0:T(8,128)S(1)} collective-permute-done((f32[2,72,128]{2,1,0:T(8,128)S(1)}, f32[2,72,128]{2,1,0:T(8,128)S(1)}, u32[]{:S(2)}, u32[]{:S(2)}) %collective-permute-start.8) | collective-permute-done | bytes 73760 | tf_op jit(solution)/shard_map/ppermute | solution.py:199
  17.2 0.5 %collective-permute-start.11 = (f32[2,72,128]{2,1,0:T(8,128)S(1)}, f32[2,72,128]{2,1,0:T(8,128)S(1)}, u32[]{:S(2)}, u32[]{:S(2)}) collective-permute-start(f32[2,72,128]{2,1,0:T(8,128)S(1)} %collective-permute-done.8.refs_3_), channel_id=1, source_target_pairs={{0,8},{1,9},{2,10},{3,11},{4,12},{5,13},{6,14},{7,15},{8,0},{9,1},... | collective-permute-start | bytes 221192 | tf_op jit(solution)/shard_map/ppermute | solution.py:199
  17.7 0.0 collective-permute-done.7.refs_2_
  17.7 0.0 collective-permute-start.10
  17.8 1.2 %collective-permute-done.3 = f32[128,128]{1,0:T(8,128)S(1)} collective-permute-done((f32[128,128]{1,0:T(8,128)S(1)}, f32[128,128]{1,0:T(8,128)S(1)}, u32[]{:S(2)}, u32[]{:S(2)}) %collective-permute-start.3) | collective-permute-done | bytes 65568 | tf_op jit(solution)/shard_map/ppermute | solution.py:199
  19.0 0.0 copy-start.3
  19.0 0.1 collective-permute-start.4
  19.1 0.0 collective-permute-done.6.refs_1_
  19.1 0.0 collective-permute-done.12.refs_7_
  19.1 0.0 collective-permute-done.11.refs_6_
  19.1 0.0 collective-permute-done.10.refs_5_
  19.1 0.2 sum_by_owner.1
  19.3 1.7 %collective-permute-start.13 = (f32[64,128]{1,0:T(8,128)S(1)}, f32[64,128]{1,0:T(8,128)S(1)}, u32[]{:S(2)}, u32[]{:S(2)}) collective-permute-start(f32[64,128]{1,0:T(8,128)S(1)} %get-tuple-element.42), channel_id=1, source_target_pairs={{0,10},{1,11},{2,8},{3,9},{4,14},{5,15},{6,12},{7,13},{8,2},{9,3},... | collective-permute-start | bytes 98312 | tf_op jit(solution)/shard_map/ppermute | solution.py:199
  21.0 2.2 %collective-permute-start.14 = (f32[64,128]{1,0:T(8,128)S(1)}, f32[64,128]{1,0:T(8,128)S(1)}, u32[]{:S(2)}, u32[]{:S(2)}) collective-permute-start(f32[64,128]{1,0:T(8,128)S(1)} %get-tuple-element.43), channel_id=1, source_target_pairs={{0,12},{1,13},{2,14},{3,15},{4,8},{5,9},{6,10},{7,11},{8,4},{9,5},... | collective-permute-start | bytes 98312 | tf_op jit(solution)/shard_map/ppermute | solution.py:199
  23.3 0.3 collective-permute-start.15
  23.6 0.0 collective-permute-done.4.gram_c_ref
  23.6 0.0 copy-done.3
  23.6 0.4 %prepare_sweep.1 = (f32[128,128]{1,0:T(8,128)S(1)}, f32[128,64]{1,0:T(8,128)S(1)}, f32[128,64]{1,0:T(8,128)S(1)}) custom-call(f32[128,128]{1,0:T(8,128)S(1)} %add.3.gram_b_ref, f32[128,128]{1,0:T(8,128)S(1)} %collective-permute-done.4.gram_c_ref, f32[64,128]{1,0:T(8,128)S(1)} %copy-done.3), custom_call_target="tpu_custom_call" | custom-call | tf_op jit(solution)/shard_map/prepare_sweep/pallas_call | solution.py:267
  24.0 0.0 collective-permute-done.13.refs_1_
  24.0 2.1 %collective-permute-done.14.refs_2_ = f32[64,128]{1,0:T(8,128)S(1)} collective-permute-done((f32[64,128]{1,0:T(8,128)S(1)}, f32[64,128]{1,0:T(8,128)S(1)}, u32[]{:S(2)}, u32[]{:S(2)}) %collective-permute-start.14) | collective-permute-done | bytes 32800 | tf_op jit(solution)/shard_map/ppermute | solution.py:199
  26.2 2.3 %collective-permute-done.15.refs_3_ = f32[64,128]{1,0:T(8,128)S(1)} collective-permute-done((f32[64,128]{1,0:T(8,128)S(1)}, f32[64,128]{1,0:T(8,128)S(1)}, u32[]{:S(2)}, u32[]{:S(2)}) %collective-permute-start.15) | collective-permute-done | bytes 32800 | tf_op jit(solution)/shard_map/ppermute | solution.py:199
  28.4 2.1 %sweep.1 = f32[64,128]{1,0:T(8,128)} custom-call(f32[128,128]{1,0:T(8,128)S(1)} %get-tuple-element.30.low_ref, f32[128,64]{1,0:T(8,128)S(1)} %get-tuple-element.31.pre_ref, f32[128,64]{1,0:T(8,128)S(1)} %get-tuple-element.32.scale_ref, f32[64,128]{1,0:T(8,128)S(1)} %get-tuple-element.41.refs_0_, f32[64,128]{1,0:T(8,128)S(1)} %collective-permute-done.13.refs_1_, ...), custom_call_target="tpu_custom_call" | custom-call | tf_op jit(solution)/shard_map/sweep/pallas_call | solution.py:291
  (3 shorter events, 0.0 us)
Async XLA Ops:
  0.0 5.0 %collective-permute-start.1 = (bf16[1024,128]{1,0:T(8,128)(2,1)}, bf16[1024,128]{1,0:T(8,128)(2,1)S(1)}, u32[]{:S(2)}, u32[]{:S(2)}) collective-permute-start(bf16[1024,128]{1,0:T(8,128)(2,1)} %b_ref.1), channel_id=1, source_target_pairs={{0,8},{1,9},{2,10},{3,11},{4,12},{5,13},{6,14},{7,15},{8,0},{9,1},... | collective-permute-start | bytes 786440 | tf_op jit(solution)/shard_map/ppermute | solution.py:199
  0.5 4.6 %collective-permute-start.2 = (bf16[1024,128]{1,0:T(8,128)(2,1)}, bf16[1024,128]{1,0:T(8,128)(2,1)S(1)}, u32[]{:S(2)}, u32[]{:S(2)}) collective-permute-start(bf16[1024,128]{1,0:T(8,128)(2,1)} %c_ref.1), channel_id=1, source_target_pairs={{0,8},{1,9},{2,10},{3,11},{4,12},{5,13},{6,14},{7,15},{8,0},{9,1},... | collective-permute-start | bytes 786440 | tf_op jit(solution)/shard_map/ppermute | solution.py:199
  0.5 4.9 %collective-permute-start = (s32[2,3]{1,0:T(2,128)}, s32[2,3]{1,0:T(2,128)S(1)}, u32[]{:S(2)}, u32[]{:S(2)}) collective-permute-start(s32[2,3]{1,0:T(2,128)} %ask_ref.1), channel_id=1, source_target_pairs={{0,24},{1,25},{2,26},{3,27},{4,28},{5,29},{6,30},{7,31},{8,16},{9,... | collective-permute-start | bytes 80 | tf_op jit(solution)/shard_map/ppermute | solution.py:199
  3.1 0.9 %copy-start.1 = (bf16[1024,128]{1,0:T(8,128)(2,1)S(1)}, bf16[1024,128]{1,0:T(8,128)(2,1)}, u32[]{:S(2)}) copy-start(bf16[1024,128]{1,0:T(8,128)(2,1)} %b_ref.1) | copy-start | bytes 786436
  4.0 0.9 %copy-start.2 = (bf16[1024,128]{1,0:T(8,128)(2,1)S(1)}, bf16[1024,128]{1,0:T(8,128)(2,1)}, u32[]{:S(2)}) copy-start(bf16[1024,128]{1,0:T(8,128)(2,1)} %c_ref.1) | copy-start | bytes 786436
  5.4 1.6 %copy-start.4 = (s32[2,3]{1,0:T(2,128)S(1)}, s32[2,3]{1,0:T(2,128)}, u32[]{:S(2)}) copy-start(s32[2,3]{1,0:T(2,128)} %ask_ref.1) | copy-start | bytes 76
  5.4 4.4 %copy-start = (bf16[2,64,4096]{2,1,0:T(8,128)(2,1)S(1)}, bf16[2,64,4096]{2,1,0:T(8,128)(2,1)}, u32[]{:S(2)}) copy-start(bf16[2,64,4096]{2,1,0:T(8,128)(2,1)} %refs_1_.1) | copy-start | bytes 3145732
  6.1 3.8 %collective-permute-start.5 = (bf16[4,64,128]{2,1,0:T(8,128)(2,1)S(1)}, bf16[4,64,128]{2,1,0:T(8,128)(2,1)S(1)}, u32[]{:S(2)}, u32[]{:S(2)}) collective-permute-start(bf16[4,64,128]{2,1,0:T(8,128)(2,1)S(1)} %gather_rows.1), channel_id=1, source_target_pairs={{0,24},{1,25},{2,26},{3,27},{4,28},{5,29},{6,30},{7,31},{8,16},{9,... | collective-permute-start | bytes 196616 | tf_op jit(solution)/shard_map/ppermute | solution.py:199
  10.4 5.0 %collective-permute-start.9 = (f32[2,72,128]{2,1,0:T(8,128)S(1)}, f32[2,72,128]{2,1,0:T(8,128)S(1)}, u32[]{:S(2)}, u32[]{:S(2)}) collective-permute-start(f32[2,72,128]{2,1,0:T(8,128)S(1)} %block_products.1.refs_0_), channel_id=1, source_target_pairs={{0,25},{1,24},{2,27},{3,26},{4,29},{5,28},{6,31},{7,30},{8,17},{9,... | collective-permute-start | bytes 221192 | tf_op jit(solution)/shard_map/ppermute | solution.py:199
  12.7 4.5 %collective-permute-start.8 = (f32[2,72,128]{2,1,0:T(8,128)S(1)}, f32[2,72,128]{2,1,0:T(8,128)S(1)}, u32[]{:S(2)}, u32[]{:S(2)}) collective-permute-start(f32[2,72,128]{2,1,0:T(8,128)S(1)} %block_products.1.refs_0_), channel_id=1, source_target_pairs={{0,24},{1,25},{2,26},{3,27},{4,28},{5,29},{6,30},{7,31},{8,16},{9,... | collective-permute-start | bytes 221192 | tf_op jit(solution)/shard_map/ppermute | solution.py:199
  13.2 4.6 %collective-permute-start.7 = (f32[2,72,128]{2,1,0:T(8,128)S(1)}, f32[2,72,128]{2,1,0:T(8,128)S(1)}, u32[]{:S(2)}, u32[]{:S(2)}) collective-permute-start(f32[2,72,128]{2,1,0:T(8,128)S(1)} %block_products.1.refs_0_), channel_id=1, source_target_pairs={{0,9},{1,8},{2,11},{3,10},{4,13},{5,12},{6,15},{7,14},{8,1},{9,0},... | collective-permute-start | bytes 221192 | tf_op jit(solution)/shard_map/ppermute | solution.py:199
  13.7 5.2 %collective-permute-start.3 = (f32[128,128]{1,0:T(8,128)S(1)}, f32[128,128]{1,0:T(8,128)S(1)}, u32[]{:S(2)}, u32[]{:S(2)}) collective-permute-start(f32[128,128]{1,0:T(8,128)S(1)} %chip_gram.1), channel_id=1, source_target_pairs={{0,16},{1,17},{2,18},{3,19},{4,20},{5,21},{6,22},{7,23},{8,24},{9,... | collective-permute-start | bytes 196616 | tf_op jit(solution)/shard_map/ppermute | solution.py:199
  15.0 4.1 %collective-permute-start.6 = (f32[2,72,128]{2,1,0:T(8,128)S(1)}, f32[2,72,128]{2,1,0:T(8,128)S(1)}, u32[]{:S(2)}, u32[]{:S(2)}) collective-permute-start(f32[2,72,128]{2,1,0:T(8,128)S(1)} %block_products.1.refs_0_), channel_id=1, source_target_pairs={{0,8},{1,9},{2,10},{3,11},{4,12},{5,13},{6,14},{7,15},{8,0},{9,1},... | collective-permute-start | bytes 221192 | tf_op jit(solution)/shard_map/ppermute | solution.py:199
  15.4 3.7 %collective-permute-start.12 = (f32[2,72,128]{2,1,0:T(8,128)S(1)}, f32[2,72,128]{2,1,0:T(8,128)S(1)}, u32[]{:S(2)}, u32[]{:S(2)}) collective-permute-start(f32[2,72,128]{2,1,0:T(8,128)S(1)} %collective-permute-done.9.refs_4_), channel_id=1, source_target_pairs={{0,8},{1,9},{2,10},{3,11},{4,12},{5,13},{6,14},{7,15},{8,0},{9,1},... | collective-permute-start | bytes 221192 | tf_op jit(solution)/shard_map/ppermute | solution.py:199
  17.2 1.9 %collective-permute-start.11 = (f32[2,72,128]{2,1,0:T(8,128)S(1)}, f32[2,72,128]{2,1,0:T(8,128)S(1)}, u32[]{:S(2)}, u32[]{:S(2)}) collective-permute-start(f32[2,72,128]{2,1,0:T(8,128)S(1)} %collective-permute-done.8.refs_3_), channel_id=1, source_target_pairs={{0,8},{1,9},{2,10},{3,11},{4,12},{5,13},{6,14},{7,15},{8,0},{9,1},... | collective-permute-start | bytes 221192 | tf_op jit(solution)/shard_map/ppermute | solution.py:199
  17.7 1.4 %collective-permute-start.10 = (f32[2,72,128]{2,1,0:T(8,128)S(1)}, f32[2,72,128]{2,1,0:T(8,128)S(1)}, u32[]{:S(2)}, u32[]{:S(2)}) collective-permute-start(f32[2,72,128]{2,1,0:T(8,128)S(1)} %collective-permute-done.7.refs_2_), channel_id=1, source_target_pairs={{0,8},{1,9},{2,10},{3,11},{4,12},{5,13},{6,14},{7,15},{8,0},{9,1},... | collective-permute-start | bytes 221192 | tf_op jit(solution)/shard_map/ppermute | solution.py:199
  19.0 4.6 %copy-start.3 = (f32[64,128]{1,0:T(8,128)S(1)}, f32[64,128]{1,0:T(8,128)}, u32[]{:S(2)}) copy-start(f32[64,128]{1,0:T(8,128)} %a_ref.1) | copy-start | bytes 98308
  19.0 4.6 %collective-permute-start.4 = (f32[128,128]{1,0:T(8,128)S(1)}, f32[128,128]{1,0:T(8,128)S(1)}, u32[]{:S(2)}, u32[]{:S(2)}) collective-permute-start(f32[128,128]{1,0:T(8,128)S(1)} %add.3.gram_b_ref), channel_id=1, source_target_pairs={{0,8},{1,9},{2,10},{3,11},{4,12},{5,13},{6,14},{7,15},{8,0},{9,1},... | collective-permute-start | bytes 196616 | tf_op jit(solution)/shard_map/ppermute | solution.py:199
  19.3 4.7 %collective-permute-start.13 = (f32[64,128]{1,0:T(8,128)S(1)}, f32[64,128]{1,0:T(8,128)S(1)}, u32[]{:S(2)}, u32[]{:S(2)}) collective-permute-start(f32[64,128]{1,0:T(8,128)S(1)} %get-tuple-element.42), channel_id=1, source_target_pairs={{0,10},{1,11},{2,8},{3,9},{4,14},{5,15},{6,12},{7,13},{8,2},{9,3},... | collective-permute-start | bytes 98312 | tf_op jit(solution)/shard_map/ppermute | solution.py:199
  21.0 5.1 %collective-permute-start.14 = (f32[64,128]{1,0:T(8,128)S(1)}, f32[64,128]{1,0:T(8,128)S(1)}, u32[]{:S(2)}, u32[]{:S(2)}) collective-permute-start(f32[64,128]{1,0:T(8,128)S(1)} %get-tuple-element.43), channel_id=1, source_target_pairs={{0,12},{1,13},{2,14},{3,15},{4,8},{5,9},{6,10},{7,11},{8,4},{9,5},... | collective-permute-start | bytes 98312 | tf_op jit(solution)/shard_map/ppermute | solution.py:199
  23.3 5.1 %collective-permute-start.15 = (f32[64,128]{1,0:T(8,128)S(1)}, f32[64,128]{1,0:T(8,128)S(1)}, u32[]{:S(2)}, u32[]{:S(2)}) collective-permute-start(f32[64,128]{1,0:T(8,128)S(1)} %get-tuple-element.44), channel_id=1, source_target_pairs={{0,14},{1,15},{2,12},{3,13},{4,10},{5,11},{6,8},{7,9},{8,6},{9,7},... | collective-permute-start | bytes 98312 | tf_op jit(solution)/shard_map/ppermute | solution.py:199

commit v3 on v2

--- a/solution.py
+++ b/solution.py
@@ -137,7 +137,7 @@
             out[sub * BS : (sub + 1) * BS] = total
 
 
-def prepare_kernel(gram_b_ref, gram_c_ref, a_ref, low_ref, pre_ref, scale_ref):
+def prepare_kernel(gram_b_ref, gram_c_ref, a_ref, within_ref, after_ref, pre_ref, scale_ref, low_ref):
     gram_b, gram_c = gram_b_ref[...], gram_c_ref[...]
     shape = gram_b.shape
     at_row = lax.broadcasted_iota(jnp.int32, shape, 0)
@@ -157,9 +157,22 @@
         later, a_ref[...], (((1,), (1,)), ((), ())), precision=EXACT, preferred_element_type=jnp.float32
     )
     scale_ref[...] = jnp.broadcast_to(1.0 / (norm_b_col * norm_c_col * pivot), scale_ref.shape)
-
-
-def sweep_kernel(low_ref, pre_ref, scale_ref, *refs):
+    count, tile = shape[0] // TILE, within_ref.shape[1:]
+    at = 0
+    for column in range(shape[0]):
+        own = column // TILE
+        for t in range(own, count):
+            weights = jnp.broadcast_to(
+                low_ref[t * TILE : (t + 1) * TILE, column : column + 1], tile
+            )
+            if t == own:
+                within_ref[column] = weights
+            else:
+                after_ref[at] = weights
+                at += 1
+
+
+def sweep_kernel(within_ref, after_ref, pre_ref, scale_ref, *refs):
     sums, out_ref = refs[:-1], refs[-1]
     rank, rows = pre_ref.shape
     total = sums[0][...]
@@ -167,15 +180,23 @@
         total += ref[...]
     start = total.T * scale_ref[...] - pre_ref[...]
     count = rank // TILE
+    tile = (TILE, rows)
+    place = lax.broadcasted_iota(jnp.int32, tile, 0)
     rest = [start[t * TILE : (t + 1) * TILE] for t in range(count)]
+    at = 0
     for k in range(count):
+        wide = [jnp.broadcast_to(rest[k][s : s + 1], tile) for s in range(TILE)]
         for s in range(TILE):
+            done = wide[s] = jnp.maximum(wide[s], 0.0)
             column = k * TILE + s
-            done = jnp.broadcast_to(jnp.maximum(rest[k], 0.0)[s : s + 1], (TILE, rows))
-            for t in range(k if s < TILE - 1 else k + 1, count):
-                weight = low_ref[t * TILE : (t + 1) * TILE, column : column + 1]
-                rest[t] = rest[t] - weight * done
-        rest[k] = jnp.maximum(rest[k], 0.0)
+            for t in range(s + 1, TILE):
+                wide[t] = wide[t] - jnp.broadcast_to(within_ref[column, t : t + 1], tile) * done
+            for t in range(k + 1, count):
+                rest[t] = rest[t] - after_ref[at] * done
+                at += 1
+        rest[k] = wide[0]
+        for s in range(1, TILE):
+            rest[k] = jnp.where(place == s, wide[s], rest[k])
     out_ref[...] = jnp.concatenate(rest, 0).T
 
 
@@ -187,6 +208,7 @@
     line = n_rep // near
     nblk = blocks.shape[0]
     rank = factor_a.shape[1]
+    tiles = rank // TILE
     jb = factor_b.shape[0] // BS
     ab = factor_a.shape[0] // BS
     params = pltpu.CompilerParams(vmem_limit_bytes=16 * 2**20)
@@ -209,7 +231,10 @@
         scratch_shapes=[pltpu.SemaphoreType.DMA((2,))],
         compiler_params=params,
         name="load_shards",
-    )(factor_b, factor_c)
+    )(
+        pltpu.with_memory_space_constraint(factor_b, pltpu.HBM),
+        pltpu.with_memory_space_constraint(factor_c, pltpu.HBM),
+    )
     factors = (own_b, mate_b, own_c, mate_c)
 
     chip_gram = pl.pallas_call(
@@ -267,12 +292,14 @@
     prepared = pl.pallas_call(
         prepare_kernel,
         out_shape=[
-            jax.ShapeDtypeStruct((rank, rank), jnp.float32),
+            jax.ShapeDtypeStruct((rank, TILE, ab * BS), jnp.float32),
+            jax.ShapeDtypeStruct((tiles * (tiles - 1) // 2 * TILE, TILE, ab * BS), jnp.float32),
             jax.ShapeDtypeStruct((rank, ab * BS), jnp.float32),
             jax.ShapeDtypeStruct((rank, ab * BS), jnp.float32),
         ],
         in_specs=[VMEM] * 3,
-        out_specs=[VMEM] * 3,
+        out_specs=[VMEM] * 4,
+        scratch_shapes=[pltpu.VMEM((rank, rank), jnp.float32)],
         compiler_params=params,
         name="prepare_sweep",
     )(gram, move(gram, 0, 1), factor_a)
@@ -291,7 +318,7 @@
     return pl.pallas_call(
         sweep_kernel,
         out_shape=jax.ShapeDtypeStruct(factor_a.shape, jnp.float32),
-        in_specs=[VMEM] * (3 + line),
+        in_specs=[VMEM] * (4 + line),
         out_specs=VMEM,
         compiler_params=params,
         name="sweep",

time: 30.7 us -> 29.9 us (0.974)
  waiting for transfers between devices: 9.18 us -> 7.42 us
  Pallas kernels: 4.9 us -> 6.29 us
  local copies, waits for them, and re-layouts: 1.92 us -> 0.69 us
  starting transfers between devices: 14.4 us -> 15.2 us
    ppermute x16, waiting for transfers between devices: 9.18 us -> 7.42 us  [move(): return lax.ppermute(value, ('grp', 'rep'), moves(n_grp, n_rep, to))]
    pallas_call x1, Pallas kernels: 0.42 us -> 1.71 us  [body(): pl.pallas_call(prepare_kernel, out_shape=[jax.ShapeDtypeStruct((rank, TIL...]
    unnamed x10 -> x6, local copies, waits for them, and re-layouts: 1.92 us -> 0.69 us
    pallas_call x1, Pallas kernels: 0.06 us -> 1.04 us  [body(): pl.pallas_call(load_kernel, out_shape=[jax.ShapeDtypeStruct(factor_b.shap...]
    pallas_call x1, Pallas kernels: 2.13 us -> 1.25 us  [body(): pl.pallas_call(sweep_kernel, out_shape=jax.ShapeDtypeStruct(factor_a.shap...]
    ppermute x16, starting transfers between devices: 14.4 us -> 15.2 us  [move(): return lax.ppermute(value, ('grp', 'rep'), moves(n_grp, n_rep, to))]
  transfers between devices with their start and end apart: 16 -> 16, of which waited for: 6 -> 7; matrix products, arithmetic and copies ran while one was open for 0% -> 0% of each run, Pallas kernels for 5% -> 13%
where the time goes in v3:
time: 29.9 us; the launch traced here: 29.7 us
  starting transfers between devices  15.2 us (51%)
  waiting for transfers between devices  7.42 us (25%)
  Pallas kernels  6.29 us (21%)
  local copies, waits for them, and re-layouts  0.69 us (2%)
    ppermute x16, starting transfers between devices, move(): return lax.ppermute(value, ('grp', 'rep'), moves(n_grp, n_rep, to))  15.2 us
    ppermute x16, waiting for transfers between devices, move(): return lax.ppermute(value, ('grp', 'rep'), moves(n_grp, n_rep, to))  7.42 us
    pallas_call x1, Pallas kernels, body(): pl.pallas_call(prepare_kernel, out_shape=[jax.ShapeDtypeStruct((rank, TIL...  1.71 us
    pallas_call x1, Pallas kernels, body(): pl.pallas_call(sweep_kernel, out_shape=jax.ShapeDtypeStruct(factor_a.shap...  1.25 us
    pallas_call x1, Pallas kernels, body(): pl.pallas_call(load_kernel, out_shape=[jax.ShapeDtypeStruct(factor_b.shap...  1.04 us
    unnamed x6, local copies, waits for them, and re-layouts  0.69 us
    pallas_call x1, Pallas kernels, body(): pl.pallas_call(functools.partial(local_kernel, n_x, nblk, jb), out_shape=...  0.61 us
  transfers between devices with their start and end apart: 16, of which 7 were waited for; matrix products, arithmetic and copies ran while one was open for 0% of the time, Pallas kernels for 13%

profile of v3, /device:TPU:0, one launch (start us, length us, event | category | flops | bytes accessed | tf_op | source)
XLA Modules:
  0.0 29.7 jit_solution(4933514778208770656)
XLA Ops:
  0.0 0.0 copy-start
  0.0 0.0 copy-start.1
  0.0 0.5 %collective-permute-start.1 = (bf16[1024,128]{1,0:T(8,128)(2,1)}, bf16[1024,128]{1,0:T(8,128)(2,1)S(1)}, u32[]{:S(2)}, u32[]{:S(2)}) collective-permute-start(bf16[1024,128]{1,0:T(8,128)(2,1)} %b_ref.1), channel_id=1, source_target_pairs={{0,8},{1,9},{2,10},{3,11},{4,12},{5,13},{6,14},{7,15},{8,0},{9,1},... | collective-permute-start | bytes 786440 | tf_op jit(solution)/shard_map/ppermute | solution.py:221
  0.5 0.1 collective-permute-start.2
  0.5 2.6 %collective-permute-start = (s32[2,3]{1,0:T(2,128)}, s32[2,3]{1,0:T(2,128)S(1)}, u32[]{:S(2)}, u32[]{:S(2)}) collective-permute-start(s32[2,3]{1,0:T(2,128)} %ask_ref.1), channel_id=1, source_target_pairs={{0,24},{1,25},{2,26},{3,27},{4,28},{5,29},{6,30},{7,31},{8,16},{9,... | collective-permute-start | bytes 80 | tf_op jit(solution)/shard_map/ppermute | solution.py:221
  3.1 1.0 %load_shards.1 = (bf16[1024,128]{1,0:T(8,128)(2,1)S(1)}, bf16[1024,128]{1,0:T(8,128)(2,1)S(1)}) custom-call(bf16[1024,128]{1,0:T(8,128)(2,1)} %b_ref.1, bf16[1024,128]{1,0:T(8,128)(2,1)} %c_ref.1), custom_call_target="tpu_custom_call" | custom-call | tf_op jit(solution)/shard_map/load_shards/pallas_call | solution.py:226
  4.2 0.0 collective-permute-done.1.mate_b.refs_2_.refs_1_
  4.2 0.0 collective-permute-done.2.mate_c.refs_4_.refs_3_
  4.2 0.4 %chip_gram.1 = f32[128,128]{1,0:T(8,128)S(1)} custom-call(bf16[1024,128]{1,0:T(8,128)(2,1)S(1)} %get-tuple-element.26.own_b.refs_1_.refs_0_, bf16[1024,128]{1,0:T(8,128)(2,1)S(1)} %collective-permute-done.1.mate_b.refs_2_.refs_1_, bf16[1024,128]{1,0:T(8,128)(2,1)S(1)} %get-tuple-element.27.own_c.refs_3_.refs_2_, ...), custom_call_target="tpu_custom_call" | custom-call | tf_op jit(solution)/shard_map/chip_gram/pallas_call | solution.py:240
  4.6 0.1 collective-permute-done.refs_0_
  4.6 0.6 %gather_rows.1 = bf16[4,64,128]{2,1,0:T(8,128)(2,1)S(1)} custom-call(s32[2,3]{1,0:T(2,128)S(1)} %collective-permute-done.refs_0_, bf16[1024,128]{1,0:T(8,128)(2,1)S(1)} %get-tuple-element.26.own_b.refs_1_.refs_0_, bf16[1024,128]{1,0:T(8,128)(2,1)S(1)} %collective-permute-done.1.mate_b.refs_2_.refs_1_, ...), custom_call_target="tpu_custom_call" | custom-call | tf_op jit(solution)/shard_map/gather_rows/pallas_call | solution.py:250
  5.2 1.8 %collective-permute-start.5 = (bf16[4,64,128]{2,1,0:T(8,128)(2,1)S(1)}, bf16[4,64,128]{2,1,0:T(8,128)(2,1)S(1)}, u32[]{:S(2)}, u32[]{:S(2)}) collective-permute-start(bf16[4,64,128]{2,1,0:T(8,128)(2,1)S(1)} %gather_rows.1), channel_id=1, source_target_pairs={{0,24},{1,25},{2,26},{3,27},{4,28},{5,29},{6,30},{7,31},{8,16},{9,... | collective-permute-start | bytes 196616 | tf_op jit(solution)/shard_map/ppermute | solution.py:221
  7.0 0.0 copy-start.2
  7.1 0.7 %copy-done.2 = s32[2,3]{1,0:T(2,128)S(1)} copy-done((s32[2,3]{1,0:T(2,128)S(1)}, s32[2,3]{1,0:T(2,128)}, u32[]{:S(2)}) %copy-start.2) | copy-done | bytes 48
  7.7 0.6 %local_rows.1 = (bf16[4,64,128]{2,1,0:T(8,128)(2,1)S(1)}, s32[4,8,128]{2,1,0:T(8,128)S(1)}, f32[2,8,128]{2,1,0:T(8,128)S(1)}) custom-call(s32[2,3]{1,0:T(2,128)S(1)} %copy-done.2, bf16[1024,128]{1,0:T(8,128)(2,1)S(1)} %get-tuple-element.26.own_b.refs_1_.refs_0_, bf16[1024,128]{1,0:T(8,128)(2,1)S(1)} %collective-permute-done.1.mate_b.refs_2_.refs_1_, ...), custom_call_target="tpu_custom_call" | custom-call | tf_op jit(solution)/shard_map/local_rows/pallas_call | solution.py:264
  8.3 0.9 %collective-permute-done.5.refs_0_ = bf16[4,64,128]{2,1,0:T(8,128)(2,1)S(1)} collective-permute-done((bf16[4,64,128]{2,1,0:T(8,128)(2,1)S(1)}, bf16[4,64,128]{2,1,0:T(8,128)(2,1)S(1)}, u32[]{:S(2)}, u32[]{:S(2)}) %collective-permute-start.5) | collective-permute-done | bytes 65568 | tf_op jit(solution)/shard_map/ppermute | solution.py:221
  9.2 0.0 copy-done
  9.3 0.5 %block_products.1.refs_0_ = f32[2,72,128]{2,1,0:T(8,128)S(1)} custom-call(bf16[4,64,128]{2,1,0:T(8,128)(2,1)S(1)} %get-tuple-element.39.rows_ref, s32[4,8,128]{2,1,0:T(8,128)S(1)} %get-tuple-element.40.far_ref, f32[2,8,128]{2,1,0:T(8,128)S(1)} %get-tuple-element.41.first_ref, bf16[4,64,128]{2,1,0:T(8,128)(2,1)S(1)} %collective-permute-done.5.refs_0_, ...), custom_call_target="tpu_custom_call" | custom-call | tf_op jit(solution)/shard_map/block_products/pallas_call | solution.py:278
  9.8 2.9 %collective-permute-start.9 = (f32[2,72,128]{2,1,0:T(8,128)S(1)}, f32[2,72,128]{2,1,0:T(8,128)S(1)}, u32[]{:S(2)}, u32[]{:S(2)}) collective-permute-start(f32[2,72,128]{2,1,0:T(8,128)S(1)} %block_products.1.refs_0_), channel_id=1, source_target_pairs={{0,25},{1,24},{2,27},{3,26},{4,29},{5,28},{6,31},{7,30},{8,17},{9,... | collective-permute-start | bytes 221192 | tf_op jit(solution)/shard_map/ppermute | solution.py:221
  12.7 0.5 %collective-permute-start.8 = (f32[2,72,128]{2,1,0:T(8,128)S(1)}, f32[2,72,128]{2,1,0:T(8,128)S(1)}, u32[]{:S(2)}, u32[]{:S(2)}) collective-permute-start(f32[2,72,128]{2,1,0:T(8,128)S(1)} %block_products.1.refs_0_), channel_id=1, source_target_pairs={{0,24},{1,25},{2,26},{3,27},{4,28},{5,29},{6,30},{7,31},{8,16},{9,... | collective-permute-start | bytes 221192 | tf_op jit(solution)/shard_map/ppermute | solution.py:221
  13.2 0.1 collective-permute-start.7
  13.3 1.7 %collective-permute-start.3 = (f32[128,128]{1,0:T(8,128)S(1)}, f32[128,128]{1,0:T(8,128)S(1)}, u32[]{:S(2)}, u32[]{:S(2)}) collective-permute-start(f32[128,128]{1,0:T(8,128)S(1)} %chip_gram.1), channel_id=1, source_target_pairs={{0,16},{1,17},{2,18},{3,19},{4,20},{5,21},{6,22},{7,23},{8,24},{9,... | collective-permute-start | bytes 196616 | tf_op jit(solution)/shard_map/ppermute | solution.py:221
  15.0 0.1 collective-permute-start.6
  15.1 0.3 collective-permute-done.9.refs_4_
  15.4 0.2 collective-permute-start.12
  15.5 1.8 %collective-permute-done.8.refs_3_ = f32[2,72,128]{2,1,0:T(8,128)S(1)} collective-permute-done((f32[2,72,128]{2,1,0:T(8,128)S(1)}, f32[2,72,128]{2,1,0:T(8,128)S(1)}, u32[]{:S(2)}, u32[]{:S(2)}) %collective-permute-start.8) | collective-permute-done | bytes 73760 | tf_op jit(solution)/shard_map/ppermute | solution.py:221
  17.3 0.4 %collective-permute-start.11 = (f32[2,72,128]{2,1,0:T(8,128)S(1)}, f32[2,72,128]{2,1,0:T(8,128)S(1)}, u32[]{:S(2)}, u32[]{:S(2)}) collective-permute-start(f32[2,72,128]{2,1,0:T(8,128)S(1)} %collective-permute-done.8.refs_3_), channel_id=1, source_target_pairs={{0,8},{1,9},{2,10},{3,11},{4,12},{5,13},{6,14},{7,15},{8,0},{9,1},... | collective-permute-start | bytes 221192 | tf_op jit(solution)/shard_map/ppermute | solution.py:221
  17.8 0.0 collective-permute-done.7.refs_2_
  17.8 0.1 collective-permute-start.10
  17.8 1.2 %collective-permute-done.3 = f32[128,128]{1,0:T(8,128)S(1)} collective-permute-done((f32[128,128]{1,0:T(8,128)S(1)}, f32[128,128]{1,0:T(8,128)S(1)}, u32[]{:S(2)}, u32[]{:S(2)}) %collective-permute-start.3) | collective-permute-done | bytes 65568 | tf_op jit(solution)/shard_map/ppermute | solution.py:221
  19.1 0.1 collective-permute-start.4
  19.1 0.0 collective-permute-done.6.refs_1_
  19.1 0.0 collective-permute-done.12.refs_7_
  19.2 0.0 collective-permute-done.11.refs_6_
  19.2 0.0 collective-permute-done.10.refs_5_
  19.2 0.2 sum_by_owner.1
  19.4 1.7 %collective-permute-start.13 = (f32[64,128]{1,0:T(8,128)S(1)}, f32[64,128]{1,0:T(8,128)S(1)}, u32[]{:S(2)}, u32[]{:S(2)}) collective-permute-start(f32[64,128]{1,0:T(8,128)S(1)} %get-tuple-element.44), channel_id=1, source_target_pairs={{0,10},{1,11},{2,8},{3,9},{4,14},{5,15},{6,12},{7,13},{8,2},{9,3},... | collective-permute-start | bytes 98312 | tf_op jit(solution)/shard_map/ppermute | solution.py:221
  21.1 2.2 %collective-permute-start.14 = (f32[64,128]{1,0:T(8,128)S(1)}, f32[64,128]{1,0:T(8,128)S(1)}, u32[]{:S(2)}, u32[]{:S(2)}) collective-permute-start(f32[64,128]{1,0:T(8,128)S(1)} %get-tuple-element.45), channel_id=1, source_target_pairs={{0,12},{1,13},{2,14},{3,15},{4,8},{5,9},{6,10},{7,11},{8,4},{9,5},... | collective-permute-start | bytes 98312 | tf_op jit(solution)/shard_map/ppermute | solution.py:221
  23.3 0.3 %collective-permute-start.15 = (f32[64,128]{1,0:T(8,128)S(1)}, f32[64,128]{1,0:T(8,128)S(1)}, u32[]{:S(2)}, u32[]{:S(2)}) collective-permute-start(f32[64,128]{1,0:T(8,128)S(1)} %get-tuple-element.46), channel_id=1, source_target_pairs={{0,14},{1,15},{2,12},{3,13},{4,10},{5,11},{6,8},{7,9},{8,6},{9,7},... | collective-permute-start | bytes 98312 | tf_op jit(solution)/shard_map/ppermute | solution.py:221
  23.6 0.0 collective-permute-done.4.gram_c_ref
  23.6 0.0 copy-done.1
  23.6 1.7 %prepare_sweep.1 = (f32[128,8,64]{2,1,0:T(8,128)S(1)}, f32[960,8,64]{2,1,0:T(8,128)S(1)}, f32[128,64]{1,0:T(8,128)S(1)}, f32[128,64]{1,0:T(8,128)S(1)}) custom-call(f32[128,128]{1,0:T(8,128)S(1)} %add.3.gram_b_ref, f32[128,128]{1,0:T(8,128)S(1)} %collective-permute-done.4.gram_c_ref, f32[64,128]{1,0:T(8,128)S(1)} %copy-done.1), custom_call_target="tpu_custom_call" | custom-call | tf_op jit(solution)/shard_map/prepare_sweep/pallas_call | solution.py:292
  25.3 0.0 collective-permute-done.13.refs_1_
  25.4 0.9 %collective-permute-done.14.refs_2_ = f32[64,128]{1,0:T(8,128)S(1)} collective-permute-done((f32[64,128]{1,0:T(8,128)S(1)}, f32[64,128]{1,0:T(8,128)S(1)}, u32[]{:S(2)}, u32[]{:S(2)}) %collective-permute-start.14) | collective-permute-done | bytes 32800 | tf_op jit(solution)/shard_map/ppermute | solution.py:221
  26.2 2.3 %collective-permute-done.15.refs_3_ = f32[64,128]{1,0:T(8,128)S(1)} collective-permute-done((f32[64,128]{1,0:T(8,128)S(1)}, f32[64,128]{1,0:T(8,128)S(1)}, u32[]{:S(2)}, u32[]{:S(2)}) %collective-permute-start.15) | collective-permute-done | bytes 32800 | tf_op jit(solution)/shard_map/ppermute | solution.py:221
  28.5 1.2 %sweep.1 = f32[64,128]{1,0:T(8,128)} custom-call(f32[128,8,64]{2,1,0:T(8,128)S(1)} %get-tuple-element.31.within_ref, f32[960,8,64]{2,1,0:T(8,128)S(1)} %get-tuple-element.32.after_ref, f32[128,64]{1,0:T(8,128)S(1)} %get-tuple-element.33.pre_ref, f32[128,64]{1,0:T(8,128)S(1)} %get-tuple-element.34.scale_ref, f32[64,128]{1,0:T(8,128)S(1)} %get-tuple-element.43.refs_0_, ...), custom_call_target="tpu_custom_call" | custom-call | tf_op jit(solution)/shard_map/sweep/pallas_call | solution.py:318
  (1 shorter events, 0.0 us)
Async XLA Ops:
  0.0 9.3 %copy-start = (bf16[2,64,4096]{2,1,0:T(8,128)(2,1)S(1)}, bf16[2,64,4096]{2,1,0:T(8,128)(2,1)}, u32[]{:S(2)}) copy-start(bf16[2,64,4096]{2,1,0:T(8,128)(2,1)} %refs_1_.1) | copy-start | bytes 3145732
  0.0 23.6 %copy-start.1 = (f32[64,128]{1,0:T(8,128)S(1)}, f32[64,128]{1,0:T(8,128)}, u32[]{:S(2)}) copy-start(f32[64,128]{1,0:T(8,128)} %a_ref.1) | copy-start | bytes 98308
  0.0 4.2 %collective-permute-start.1 = (bf16[1024,128]{1,0:T(8,128)(2,1)}, bf16[1024,128]{1,0:T(8,128)(2,1)S(1)}, u32[]{:S(2)}, u32[]{:S(2)}) collective-permute-start(bf16[1024,128]{1,0:T(8,128)(2,1)} %b_ref.1), channel_id=1, source_target_pairs={{0,8},{1,9},{2,10},{3,11},{4,12},{5,13},{6,14},{7,15},{8,0},{9,1},... | collective-permute-start | bytes 786440 | tf_op jit(solution)/shard_map/ppermute | solution.py:221
  0.5 3.7 %collective-permute-start.2 = (bf16[1024,128]{1,0:T(8,128)(2,1)}, bf16[1024,128]{1,0:T(8,128)(2,1)S(1)}, u32[]{:S(2)}, u32[]{:S(2)}) collective-permute-start(bf16[1024,128]{1,0:T(8,128)(2,1)} %c_ref.1), channel_id=1, source_target_pairs={{0,8},{1,9},{2,10},{3,11},{4,12},{5,13},{6,14},{7,15},{8,0},{9,1},... | collective-permute-start | bytes 786440 | tf_op jit(solution)/shard_map/ppermute | solution.py:221
  0.5 4.1 %collective-permute-start = (s32[2,3]{1,0:T(2,128)}, s32[2,3]{1,0:T(2,128)S(1)}, u32[]{:S(2)}, u32[]{:S(2)}) collective-permute-start(s32[2,3]{1,0:T(2,128)} %ask_ref.1), channel_id=1, source_target_pairs={{0,24},{1,25},{2,26},{3,27},{4,28},{5,29},{6,30},{7,31},{8,16},{9,... | collective-permute-start | bytes 80 | tf_op jit(solution)/shard_map/ppermute | solution.py:221
  5.2 4.0 %collective-permute-start.5 = (bf16[4,64,128]{2,1,0:T(8,128)(2,1)S(1)}, bf16[4,64,128]{2,1,0:T(8,128)(2,1)S(1)}, u32[]{:S(2)}, u32[]{:S(2)}) collective-permute-start(bf16[4,64,128]{2,1,0:T(8,128)(2,1)S(1)} %gather_rows.1), channel_id=1, source_target_pairs={{0,24},{1,25},{2,26},{3,27},{4,28},{5,29},{6,30},{7,31},{8,16},{9,... | collective-permute-start | bytes 196616 | tf_op jit(solution)/shard_map/ppermute | solution.py:221
  7.0 0.7 %copy-start.2 = (s32[2,3]{1,0:T(2,128)S(1)}, s32[2,3]{1,0:T(2,128)}, u32[]{:S(2)}) copy-start(s32[2,3]{1,0:T(2,128)} %ask_ref.1) | copy-start | bytes 76
  9.8 5.6 %collective-permute-start.9 = (f32[2,72,128]{2,1,0:T(8,128)S(1)}, f32[2,72,128]{2,1,0:T(8,128)S(1)}, u32[]{:S(2)}, u32[]{:S(2)}) collective-permute-start(f32[2,72,128]{2,1,0:T(8,128)S(1)} %block_products.1.refs_0_), channel_id=1, source_target_pairs={{0,25},{1,24},{2,27},{3,26},{4,29},{5,28},{6,31},{7,30},{8,17},{9,... | collective-permute-start | bytes 221192 | tf_op jit(solution)/shard_map/ppermute | solution.py:221
  12.7 4.6 %collective-permute-start.8 = (f32[2,72,128]{2,1,0:T(8,128)S(1)}, f32[2,72,128]{2,1,0:T(8,128)S(1)}, u32[]{:S(2)}, u32[]{:S(2)}) collective-permute-start(f32[2,72,128]{2,1,0:T(8,128)S(1)} %block_products.1.refs_0_), channel_id=1, source_target_pairs={{0,24},{1,25},{2,26},{3,27},{4,28},{5,29},{6,30},{7,31},{8,16},{9,... | collective-permute-start | bytes 221192 | tf_op jit(solution)/shard_map/ppermute | solution.py:221
  13.2 4.5 %collective-permute-start.7 = (f32[2,72,128]{2,1,0:T(8,128)S(1)}, f32[2,72,128]{2,1,0:T(8,128)S(1)}, u32[]{:S(2)}, u32[]{:S(2)}) collective-permute-start(f32[2,72,128]{2,1,0:T(8,128)S(1)} %block_products.1.refs_0_), channel_id=1, source_target_pairs={{0,9},{1,8},{2,11},{3,10},{4,13},{5,12},{6,15},{7,14},{8,1},{9,0},... | collective-permute-start | bytes 221192 | tf_op jit(solution)/shard_map/ppermute | solution.py:221
  13.3 5.7 %collective-permute-start.3 = (f32[128,128]{1,0:T(8,128)S(1)}, f32[128,128]{1,0:T(8,128)S(1)}, u32[]{:S(2)}, u32[]{:S(2)}) collective-permute-start(f32[128,128]{1,0:T(8,128)S(1)} %chip_gram.1), channel_id=1, source_target_pairs={{0,16},{1,17},{2,18},{3,19},{4,20},{5,21},{6,22},{7,23},{8,24},{9,... | collective-permute-start | bytes 196616 | tf_op jit(solution)/shard_map/ppermute | solution.py:221
  15.0 4.1 %collective-permute-start.6 = (f32[2,72,128]{2,1,0:T(8,128)S(1)}, f32[2,72,128]{2,1,0:T(8,128)S(1)}, u32[]{:S(2)}, u32[]{:S(2)}) collective-permute-start(f32[2,72,128]{2,1,0:T(8,128)S(1)} %block_products.1.refs_0_), channel_id=1, source_target_pairs={{0,8},{1,9},{2,10},{3,11},{4,12},{5,13},{6,14},{7,15},{8,0},{9,1},... | collective-permute-start | bytes 221192 | tf_op jit(solution)/shard_map/ppermute | solution.py:221
  15.4 3.8 %collective-permute-start.12 = (f32[2,72,128]{2,1,0:T(8,128)S(1)}, f32[2,72,128]{2,1,0:T(8,128)S(1)}, u32[]{:S(2)}, u32[]{:S(2)}) collective-permute-start(f32[2,72,128]{2,1,0:T(8,128)S(1)} %collective-permute-done.9.refs_4_), channel_id=1, source_target_pairs={{0,8},{1,9},{2,10},{3,11},{4,12},{5,13},{6,14},{7,15},{8,0},{9,1},... | collective-permute-start | bytes 221192 | tf_op jit(solution)/shard_map/ppermute | solution.py:221
  17.3 1.8 %collective-permute-start.11 = (f32[2,72,128]{2,1,0:T(8,128)S(1)}, f32[2,72,128]{2,1,0:T(8,128)S(1)}, u32[]{:S(2)}, u32[]{:S(2)}) collective-permute-start(f32[2,72,128]{2,1,0:T(8,128)S(1)} %collective-permute-done.8.refs_3_), channel_id=1, source_target_pairs={{0,8},{1,9},{2,10},{3,11},{4,12},{5,13},{6,14},{7,15},{8,0},{9,1},... | collective-permute-start | bytes 221192 | tf_op jit(solution)/shard_map/ppermute | solution.py:221
  17.8 1.4 %collective-permute-start.10 = (f32[2,72,128]{2,1,0:T(8,128)S(1)}, f32[2,72,128]{2,1,0:T(8,128)S(1)}, u32[]{:S(2)}, u32[]{:S(2)}) collective-permute-start(f32[2,72,128]{2,1,0:T(8,128)S(1)} %collective-permute-done.7.refs_2_), channel_id=1, source_target_pairs={{0,8},{1,9},{2,10},{3,11},{4,12},{5,13},{6,14},{7,15},{8,0},{9,1},... | collective-permute-start | bytes 221192 | tf_op jit(solution)/shard_map/ppermute | solution.py:221
  19.1 4.6 %collective-permute-start.4 = (f32[128,128]{1,0:T(8,128)S(1)}, f32[128,128]{1,0:T(8,128)S(1)}, u32[]{:S(2)}, u32[]{:S(2)}) collective-permute-start(f32[128,128]{1,0:T(8,128)S(1)} %add.3.gram_b_ref), channel_id=1, source_target_pairs={{0,8},{1,9},{2,10},{3,11},{4,12},{5,13},{6,14},{7,15},{8,0},{9,1},... | collective-permute-start | bytes 196616 | tf_op jit(solution)/shard_map/ppermute | solution.py:221
  19.4 6.0 %collective-permute-start.13 = (f32[64,128]{1,0:T(8,128)S(1)}, f32[64,128]{1,0:T(8,128)S(1)}, u32[]{:S(2)}, u32[]{:S(2)}) collective-permute-start(f32[64,128]{1,0:T(8,128)S(1)} %get-tuple-element.44), channel_id=1, source_target_pairs={{0,10},{1,11},{2,8},{3,9},{4,14},{5,15},{6,12},{7,13},{8,2},{9,3},... | collective-permute-start | bytes 98312 | tf_op jit(solution)/shard_map/ppermute | solution.py:221
  21.1 5.1 %collective-permute-start.14 = (f32[64,128]{1,0:T(8,128)S(1)}, f32[64,128]{1,0:T(8,128)S(1)}, u32[]{:S(2)}, u32[]{:S(2)}) collective-permute-start(f32[64,128]{1,0:T(8,128)S(1)} %get-tuple-element.45), channel_id=1, source_target_pairs={{0,12},{1,13},{2,14},{3,15},{4,8},{5,9},{6,10},{7,11},{8,4},{9,5},... | collective-permute-start | bytes 98312 | tf_op jit(solution)/shard_map/ppermute | solution.py:221
  23.3 5.1 %collective-permute-start.15 = (f32[64,128]{1,0:T(8,128)S(1)}, f32[64,128]{1,0:T(8,128)S(1)}, u32[]{:S(2)}, u32[]{:S(2)}) collective-permute-start(f32[64,128]{1,0:T(8,128)S(1)} %get-tuple-element.46), channel_id=1, source_target_pairs={{0,14},{1,15},{2,12},{3,13},{4,10},{5,11},{6,8},{7,9},{8,6},{9,7},... | collective-permute-start | bytes 98312 | tf_op jit(solution)/shard_map/ppermute | solution.py:221

commit v4 on v3

--- a/solution.py
+++ b/solution.py
@@ -13,7 +13,6 @@
 EXACT = lax.Precision.HIGHEST
 VMEM = pl.BlockSpec(memory_space=pltpu.VMEM)
 HBM = pl.BlockSpec(memory_space=pltpu.HBM)
-SMEM = pl.BlockSpec(memory_space=pltpu.SMEM)
 
 
 def moves(n_grp, n_rep, to):
@@ -46,17 +45,12 @@
 
 
 def gram_kernel(own_b, mate_b, own_c, mate_c, out_ref):
-    _, core, _ = here()
     dims = (((0,), (0,)), ((), ()))
-
-    def fill(*shards):
+    for mode, shards in enumerate(((own_b, mate_b), (own_c, mate_c))):
         total = 0.0
         for ref in shards:
             total += lax.dot_general(ref[...], ref[...], dims, preferred_element_type=jnp.float32)
-        out_ref[...] = total
-
-    pl.when(core == 0)(lambda: fill(own_b, mate_b))
-    pl.when(core != 0)(lambda: fill(own_c, mate_c))
+        out_ref[mode] = total
 
 
 def row_block(own, mate, local, core, jb):
@@ -70,23 +64,27 @@
     for ask, out in zip(asks, outs):
         for mode in range(2):
             for n in range(nblk):
-                local = lax.rem(ask[n, 1 + mode], CORES * jb)
+                local = lax.rem(ask[...][n, 1 + mode], CORES * jb)
                 out[mode * nblk + n] = row_block(*factors[2 * mode : 2 * mode + 2], local, core, jb)
 
 
 def local_kernel(n_x, nblk, jb, ask_ref, *refs):
     factors, (rows_ref, far_ref, first_ref) = refs[:4], refs[4:]
+    ask = ask_ref[...]
     my_x, core, _ = here()
     for mode in range(2):
         for n in range(nblk):
             slot = mode * nblk + n
-            wanted = ask_ref[n, 1 + mode]
+            wanted = ask[n, 1 + mode]
             local = lax.rem(wanted, CORES * jb)
             rows_ref[slot] = row_block(*factors[2 * mode : 2 * mode + 2], local, core, jb)
             far = lax.rem(lax.div(wanted, CORES * jb) - my_x + n_x, n_x)
             far_ref[slot] = jnp.full(far_ref.shape[1:], far, jnp.int32)
+    place = lax.broadcasted_iota(jnp.int32, first_ref.shape, 0)
+    first = jnp.zeros(first_ref.shape, jnp.int32)
     for n in range(nblk):
-        first_ref[n] = jnp.full(first_ref.shape[1:], ask_ref[n, 0].astype(jnp.float32))
+        first = jnp.where(place == n, ask[n, 0], first)
+    first_ref[...] = first.astype(jnp.float32)
 
 
 def partial_kernel(n_x, nblk, rows_ref, far_ref, first_ref, *refs):
@@ -111,11 +109,11 @@
                 khatri.reshape(step * BS, rank),
                 preferred_element_type=jnp.float32,
             )
-        out_ref[n, :BS] = total
-        out_ref[n, BS:] = first_ref[n]
-
-
-def owner_kernel(n_rep, near, ab, count, *refs):
+        out_ref[n * BS : (n + 1) * BS] = total
+    out_ref[nblk * BS :] = first_ref[...]
+
+
+def owner_kernel(nblk, n_rep, near, ab, count, *refs):
     arrived, outs = refs[:count], refs[count:]
     my_x, core, rep = here()
     line = n_rep // near
@@ -131,14 +129,22 @@
             target = (first + sub).astype(jnp.float32)
             total = None
             for ref in arrived:
-                for n in range(ref.shape[0]):
-                    term = jnp.where(ref[n, BS : BS + 1] == target, ref[n, :BS], 0.0)
+                for n in range(nblk):
+                    at_id = nblk * BS + n
+                    term = jnp.where(
+                        ref[at_id : at_id + 1] == target, ref[n * BS : (n + 1) * BS], 0.0
+                    )
                     total = term if total is None else total + term
             out[sub * BS : (sub + 1) * BS] = total
 
 
-def prepare_kernel(gram_b_ref, gram_c_ref, a_ref, within_ref, after_ref, pre_ref, scale_ref, low_ref):
-    gram_b, gram_c = gram_b_ref[...], gram_c_ref[...]
+def prepare_kernel(n_x, *refs):
+    grams = refs[:n_x]
+    a_ref, within_ref, after_ref, pre_ref, scale_ref, low_ref = refs[n_x:]
+    gram_b, gram_c = grams[0][0], grams[0][1]
+    for ref in grams[1:]:
+        gram_b += ref[0]
+        gram_c += ref[1]
     shape = gram_b.shape
     at_row = lax.broadcasted_iota(jnp.int32, shape, 0)
     at_col = lax.broadcasted_iota(jnp.int32, shape, 1)
@@ -209,6 +215,7 @@
     nblk = blocks.shape[0]
     rank = factor_a.shape[1]
     tiles = rank // TILE
+    id_rows = -(-nblk // TILE) * TILE
     jb = factor_b.shape[0] // BS
     ab = factor_a.shape[0] // BS
     params = pltpu.CompilerParams(vmem_limit_bytes=16 * 2**20)
@@ -239,36 +246,33 @@
 
     chip_gram = pl.pallas_call(
         gram_kernel,
-        out_shape=jax.ShapeDtypeStruct((rank, rank), jnp.float32),
+        out_shape=jax.ShapeDtypeStruct((2, rank, rank), jnp.float32),
         in_specs=[VMEM] * 4,
         out_specs=VMEM,
         compiler_params=params,
         name="chip_gram",
     )(*factors)
-    asks, chip_gram = lax.optimization_barrier((asks, chip_gram))
 
     answers = pl.pallas_call(
         functools.partial(gather_kernel, n_x - 1, nblk, jb),
         out_shape=[jax.ShapeDtypeStruct((2 * nblk, BS, rank), factor_b.dtype)] * (n_x - 1),
-        in_specs=[SMEM] * (n_x - 1) + [VMEM] * 4,
+        in_specs=[VMEM] * (n_x - 1) + [VMEM] * 4,
         out_specs=[VMEM] * (n_x - 1),
         compiler_params=params,
         name="gather_rows",
     )(*asks, *factors)
     answers, chip_gram = lax.optimization_barrier((answers, chip_gram))
     found = [move(answers[d - 1], -d, 1) for d in range(1, n_x)]
-    gram = chip_gram
-    for d in range(1, n_x):
-        gram = gram + move(chip_gram, d, 0)
+    grams = [chip_gram] + [move(chip_gram, d, 1) for d in range(1, n_x)]
 
     local = pl.pallas_call(
         functools.partial(local_kernel, n_x, nblk, jb),
         out_shape=[
             jax.ShapeDtypeStruct((2 * nblk, BS, rank), factor_b.dtype),
             jax.ShapeDtypeStruct((2 * nblk, TILE, rank), jnp.int32),
-            jax.ShapeDtypeStruct((nblk, TILE, rank), jnp.float32),
+            jax.ShapeDtypeStruct((id_rows, rank), jnp.float32),
         ],
-        in_specs=[SMEM] + [VMEM] * 4,
+        in_specs=[VMEM] * 5,
         out_specs=[VMEM] * 3,
         compiler_params=params,
         name="local_rows",
@@ -277,7 +281,7 @@
 
     partial = pl.pallas_call(
         functools.partial(partial_kernel, n_x, nblk),
-        out_shape=jax.ShapeDtypeStruct((nblk, BS + TILE, rank), jnp.float32),
+        out_shape=jax.ShapeDtypeStruct((nblk * BS + id_rows, rank), jnp.float32),
         in_specs=[VMEM] * (3 + n_x),
         out_specs=VMEM,
         compiler_params=params,
@@ -290,30 +294,30 @@
         if d or beside
     ]
     prepared = pl.pallas_call(
-        prepare_kernel,
+        functools.partial(prepare_kernel, n_x),
         out_shape=[
             jax.ShapeDtypeStruct((rank, TILE, ab * BS), jnp.float32),
             jax.ShapeDtypeStruct((tiles * (tiles - 1) // 2 * TILE, TILE, ab * BS), jnp.float32),
             jax.ShapeDtypeStruct((rank, ab * BS), jnp.float32),
             jax.ShapeDtypeStruct((rank, ab * BS), jnp.float32),
         ],
-        in_specs=[VMEM] * 3,
+        in_specs=[VMEM] * (n_x + 1),
         out_specs=[VMEM] * 4,
         scratch_shapes=[pltpu.VMEM((rank, rank), jnp.float32)],
         compiler_params=params,
         name="prepare_sweep",
-    )(gram, move(gram, 0, 1), factor_a)
+    )(*grams, factor_a)
     arrived = [partial, move(partial, 0, 1), *others, *(move(value, 0, 1) for value in others)]
 
     sums = pl.pallas_call(
-        functools.partial(owner_kernel, n_rep, near, ab, len(arrived)),
+        functools.partial(owner_kernel, nblk, n_rep, near, ab, len(arrived)),
         out_shape=[jax.ShapeDtypeStruct(factor_a.shape, jnp.float32)] * line,
         in_specs=[VMEM] * len(arrived),
         out_specs=[VMEM] * line,
         compiler_params=params,
         name="sum_by_owner",
     )(*arrived)
-    sums = [sums[0]] + [move(sums[d], 0, 1, 0, d) for d in range(1, line)]
+    sums = [sums[0]] + [move(sums[d], 0, 1, 0, d) for d in range(line - 1, 0, -1)]
 
     return pl.pallas_call(
         sweep_kernel,

time: 29.9 us -> 28 us (0.936)
  waiting for transfers between devices: 7.42 us -> 6.41 us
  Pallas kernels: 6.29 us -> 5.49 us
    ppermute x16 -> x15, waiting for transfers between devices: 7.42 us -> 6.41 us  [move(): return lax.ppermute(value, ('grp', 'rep'), moves(n_grp, n_rep, to))]
    pallas_call x1, Pallas kernels: 0.61 us -> 0.15 us  [body(): pl.pallas_call(functools.partial(local_kernel, n_x, nblk, jb), out_shape=...]
    pallas_call x1, Pallas kernels: 0.6 us -> 0.14 us  [body(): pl.pallas_call(functools.partial(gather_kernel, n_x - 1, nblk, jb), out_s...]
    ppermute x16 -> x15, starting transfers between devices: 15.2 us -> 15.1 us  [move(): return lax.ppermute(value, ('grp', 'rep'), moves(n_grp, n_rep, to))]
  transfers between devices with their start and end apart: 16 -> 15, of which waited for: 7 -> 6; matrix products, arithmetic and copies ran while one was open for 0% -> 0% of each run, Pallas kernels for 13% -> 13%
where the time goes in v4:
time: 28 us; the launch traced here: 27.8 us
  starting transfers between devices  15.1 us (54%)
  waiting for transfers between devices  6.41 us (23%)
  Pallas kernels  5.49 us (20%)
  local copies, waits for them, and re-layouts  0.69 us (2%)
    ppermute x15, starting transfers between devices, move(): return lax.ppermute(value, ('grp', 'rep'), moves(n_grp, n_rep, to))  15.1 us
    ppermute x15, waiting for transfers between devices, move(): return lax.ppermute(value, ('grp', 'rep'), moves(n_grp, n_rep, to))  6.41 us
    pallas_call x1, Pallas kernels, body(): pl.pallas_call(functools.partial(prepare_kernel, n_x), out_shape=[jax.Sha...  1.71 us
    pallas_call x1, Pallas kernels, body(): pl.pallas_call(sweep_kernel, out_shape=jax.ShapeDtypeStruct(factor_a.shap...  1.25 us
    pallas_call x1, Pallas kernels, body(): pl.pallas_call(load_kernel, out_shape=[jax.ShapeDtypeStruct(factor_b.shap...  1.04 us
    unnamed x6, local copies, waits for them, and re-layouts  0.69 us
  transfers between devices with their start and end apart: 15, of which 6 were waited for; matrix products, arithmetic and copies ran while one was open for 0% of the time, Pallas kernels for 13%

profile of v4, /device:TPU:0, one launch (start us, length us, event | category | flops | bytes accessed | tf_op | source)
XLA Modules:
  0.0 27.8 jit_solution(12503790622589423415)
XLA Ops:
  0.0 0.0 copy-start
  0.0 0.0 copy-start.1
  0.0 0.5 %collective-permute-start.1 = (bf16[1024,128]{1,0:T(8,128)(2,1)}, bf16[1024,128]{1,0:T(8,128)(2,1)S(1)}, u32[]{:S(2)}, u32[]{:S(2)}) collective-permute-start(bf16[1024,128]{1,0:T(8,128)(2,1)} %b_ref.1), channel_id=1, source_target_pairs={{0,8},{1,9},{2,10},{3,11},{4,12},{5,13},{6,14},{7,15},{8,0},{9,1},... | collective-permute-start | bytes 786440 | tf_op jit(solution)/shard_map/ppermute | solution.py:228
  0.5 0.1 collective-permute-start.2
  0.5 2.6 %collective-permute-start = (s32[2,3]{1,0:T(2,128)}, s32[2,3]{1,0:T(2,128)S(1)}, u32[]{:S(2)}, u32[]{:S(2)}) collective-permute-start(s32[2,3]{1,0:T(2,128)} %ask_ref.1), channel_id=1, source_target_pairs={{0,24},{1,25},{2,26},{3,27},{4,28},{5,29},{6,30},{7,31},{8,16},{9,... | collective-permute-start | bytes 80 | tf_op jit(solution)/shard_map/ppermute | solution.py:228
  3.1 1.0 %load_shards.1 = (bf16[1024,128]{1,0:T(8,128)(2,1)S(1)}, bf16[1024,128]{1,0:T(8,128)(2,1)S(1)}) custom-call(bf16[1024,128]{1,0:T(8,128)(2,1)} %b_ref.1, bf16[1024,128]{1,0:T(8,128)(2,1)} %c_ref.1), custom_call_target="tpu_custom_call" | custom-call | tf_op jit(solution)/shard_map/load_shards/pallas_call | solution.py:233
  4.2 0.0 collective-permute-done.1.refs_2_.mate_b.refs_1_
  4.2 0.0 collective-permute-done.2.refs_4_.mate_c.refs_3_
  4.2 0.5 %chip_gram.1.refs_0_ = f32[2,128,128]{2,1,0:T(8,128)S(1)} custom-call(bf16[1024,128]{1,0:T(8,128)(2,1)S(1)} %get-tuple-element.24.refs_1_.own_b.refs_0_, bf16[1024,128]{1,0:T(8,128)(2,1)S(1)} %collective-permute-done.1.refs_2_.mate_b.refs_1_, bf16[1024,128]{1,0:T(8,128)(2,1)S(1)} %get-tuple-element.25.refs_3_.own_c.refs_2_, ...), custom_call_target="tpu_custom_call" | custom-call | tf_op jit(solution)/shard_map/chip_gram/pallas_call | solution.py:247
  4.7 0.0 collective-permute-done.refs_0_
  4.7 0.1 gather_rows.1
  4.9 1.7 %collective-permute-start.4 = (bf16[4,64,128]{2,1,0:T(8,128)(2,1)S(1)}, bf16[4,64,128]{2,1,0:T(8,128)(2,1)S(1)}, u32[]{:S(2)}, u32[]{:S(2)}) collective-permute-start(bf16[4,64,128]{2,1,0:T(8,128)(2,1)S(1)} %gather_rows.1), channel_id=1, source_target_pairs={{0,24},{1,25},{2,26},{3,27},{4,28},{5,29},{6,30},{7,31},{8,16},{9,... | collective-permute-start | bytes 196616 | tf_op jit(solution)/shard_map/ppermute | solution.py:228
  6.6 0.0 copy-start.2
  6.6 0.7 %copy-done.2 = s32[2,3]{1,0:T(2,128)S(1)} copy-done((s32[2,3]{1,0:T(2,128)S(1)}, s32[2,3]{1,0:T(2,128)}, u32[]{:S(2)}) %copy-start.2) | copy-done | bytes 48
  7.3 0.1 local_rows.1
  7.4 1.4 %collective-permute-done.4.refs_0_ = bf16[4,64,128]{2,1,0:T(8,128)(2,1)S(1)} collective-permute-done((bf16[4,64,128]{2,1,0:T(8,128)(2,1)S(1)}, bf16[4,64,128]{2,1,0:T(8,128)(2,1)S(1)}, u32[]{:S(2)}, u32[]{:S(2)}) %collective-permute-start.4) | collective-permute-done | bytes 65568 | tf_op jit(solution)/shard_map/ppermute | solution.py:228
  8.8 0.0 copy-done
  8.8 0.5 %block_products.1.refs_0_ = f32[136,128]{1,0:T(8,128)S(1)} custom-call(bf16[4,64,128]{2,1,0:T(8,128)(2,1)S(1)} %get-tuple-element.35.rows_ref, s32[4,8,128]{2,1,0:T(8,128)S(1)} %get-tuple-element.36.far_ref, f32[8,128]{1,0:T(8,128)S(1)} %get-tuple-element.37.first_ref, bf16[4,64,128]{2,1,0:T(8,128)(2,1)S(1)} %collective-permute-done.4.refs_0_, ...), custom_call_target="tpu_custom_call" | custom-call | tf_op jit(solution)/shard_map/block_products/pallas_call | solution.py:282
  9.3 2.9 %collective-permute-start.8 = (f32[136,128]{1,0:T(8,128)S(1)}, f32[136,128]{1,0:T(8,128)S(1)}, u32[]{:S(2)}, u32[]{:S(2)}) collective-permute-start(f32[136,128]{1,0:T(8,128)S(1)} %block_products.1.refs_0_), channel_id=1, source_target_pairs={{0,25},{1,24},{2,27},{3,26},{4,29},{5,28},{6,31},{7,30},{8,17},{9,... | collective-permute-start | bytes 208904 | tf_op jit(solution)/shard_map/ppermute | solution.py:228
  12.2 0.6 %collective-permute-start.7 = (f32[136,128]{1,0:T(8,128)S(1)}, f32[136,128]{1,0:T(8,128)S(1)}, u32[]{:S(2)}, u32[]{:S(2)}) collective-permute-start(f32[136,128]{1,0:T(8,128)S(1)} %block_products.1.refs_0_), channel_id=1, source_target_pairs={{0,24},{1,25},{2,26},{3,27},{4,28},{5,29},{6,30},{7,31},{8,16},{9,... | collective-permute-start | bytes 208904 | tf_op jit(solution)/shard_map/ppermute | solution.py:228
  12.8 0.1 collective-permute-start.6
  12.9 1.6 %collective-permute-start.3 = (f32[2,128,128]{2,1,0:T(8,128)S(1)}, f32[2,128,128]{2,1,0:T(8,128)S(1)}, u32[]{:S(2)}, u32[]{:S(2)}) collective-permute-start(f32[2,128,128]{2,1,0:T(8,128)S(1)} %chip_gram.1.refs_0_), channel_id=1, source_target_pairs={{0,24},{1,25},{2,26},{3,27},{4,28},{5,29},{6,30},{7,31},{8,16},{9,... | collective-permute-start | bytes 393224 | tf_op jit(solution)/shard_map/ppermute | solution.py:228
  14.5 0.2 collective-permute-start.5
  14.6 0.2 collective-permute-done.8.refs_4_
  14.8 0.2 collective-permute-start.11
  15.0 1.7 %collective-permute-done.7.refs_3_ = f32[136,128]{1,0:T(8,128)S(1)} collective-permute-done((f32[136,128]{1,0:T(8,128)S(1)}, f32[136,128]{1,0:T(8,128)S(1)}, u32[]{:S(2)}, u32[]{:S(2)}) %collective-permute-start.7) | collective-permute-done | bytes 69664 | tf_op jit(solution)/shard_map/ppermute | solution.py:228
  16.7 0.7 %collective-permute-start.10 = (f32[136,128]{1,0:T(8,128)S(1)}, f32[136,128]{1,0:T(8,128)S(1)}, u32[]{:S(2)}, u32[]{:S(2)}) collective-permute-start(f32[136,128]{1,0:T(8,128)S(1)} %collective-permute-done.7.refs_3_), channel_id=1, source_target_pairs={{0,8},{1,9},{2,10},{3,11},{4,12},{5,13},{6,14},{7,15},{8,0},{9,1},... | collective-permute-start | bytes 208904 | tf_op jit(solution)/shard_map/ppermute | solution.py:228
  17.4 0.0 collective-permute-done.6.refs_2_
  17.4 0.0 collective-permute-start.9
  17.4 0.0 collective-permute-done.5.refs_1_
  17.4 0.0 collective-permute-done.11.refs_7_
  17.4 0.9 %collective-permute-done.10.refs_6_ = f32[136,128]{1,0:T(8,128)S(1)} collective-permute-done((f32[136,128]{1,0:T(8,128)S(1)}, f32[136,128]{1,0:T(8,128)S(1)}, u32[]{:S(2)}, u32[]{:S(2)}) %collective-permute-start.10) | collective-permute-done | bytes 69664 | tf_op jit(solution)/shard_map/ppermute | solution.py:228
  18.3 0.4 %collective-permute-done.9.refs_5_ = f32[136,128]{1,0:T(8,128)S(1)} collective-permute-done((f32[136,128]{1,0:T(8,128)S(1)}, f32[136,128]{1,0:T(8,128)S(1)}, u32[]{:S(2)}, u32[]{:S(2)}) %collective-permute-start.9) | collective-permute-done | bytes 69664 | tf_op jit(solution)/shard_map/ppermute | solution.py:228
  18.7 0.2 sum_by_owner.1
  18.9 3.5 %collective-permute-start.12 = (f32[64,128]{1,0:T(8,128)S(1)}, f32[64,128]{1,0:T(8,128)S(1)}, u32[]{:S(2)}, u32[]{:S(2)}) collective-permute-start(f32[64,128]{1,0:T(8,128)S(1)} %get-tuple-element.40), channel_id=1, source_target_pairs={{0,14},{1,15},{2,12},{3,13},{4,10},{5,11},{6,8},{7,9},{8,6},{9,7},... | collective-permute-start | bytes 98312 | tf_op jit(solution)/shard_map/ppermute | solution.py:228
  22.3 0.0 collective-permute-start.13
  22.3 0.6 %collective-permute-start.14 = (f32[64,128]{1,0:T(8,128)S(1)}, f32[64,128]{1,0:T(8,128)S(1)}, u32[]{:S(2)}, u32[]{:S(2)}) collective-permute-start(f32[64,128]{1,0:T(8,128)S(1)} %get-tuple-element.42), channel_id=1, source_target_pairs={{0,10},{1,11},{2,8},{3,9},{4,14},{5,15},{6,12},{7,13},{8,2},{9,3},... | collective-permute-start | bytes 98312 | tf_op jit(solution)/shard_map/ppermute | solution.py:228
  22.9 0.0 collective-permute-done.3.refs_1_
  22.9 0.0 copy-done.1
  22.9 1.7 %prepare_sweep.1 = (f32[128,8,64]{2,1,0:T(8,128)S(1)}, f32[960,8,64]{2,1,0:T(8,128)S(1)}, f32[128,64]{1,0:T(8,128)S(1)}, f32[128,64]{1,0:T(8,128)S(1)}) custom-call(f32[2,128,128]{2,1,0:T(8,128)S(1)} %chip_gram.1.refs_0_, f32[2,128,128]{2,1,0:T(8,128)S(1)} %collective-permute-done.3.refs_1_, f32[64,128]{1,0:T(8,128)S(1)} %copy-done.1), custom_call_target="tpu_custom_call" | custom-call | tf_op jit(solution)/shard_map/prepare_sweep/pallas_call | solution.py:296
  24.7 0.0 collective-permute-done.12.refs_1_
  24.7 1.9 %collective-permute-done.13.refs_2_ = f32[64,128]{1,0:T(8,128)S(1)} collective-permute-done((f32[64,128]{1,0:T(8,128)S(1)}, f32[64,128]{1,0:T(8,128)S(1)}, u32[]{:S(2)}, u32[]{:S(2)}) %collective-permute-start.13) | collective-permute-done | bytes 32800 | tf_op jit(solution)/shard_map/ppermute | solution.py:228
  26.6 0.0 collective-permute-done.14.refs_3_
  26.6 1.2 %sweep.1 = f32[64,128]{1,0:T(8,128)} custom-call(f32[128,8,64]{2,1,0:T(8,128)S(1)} %get-tuple-element.27.within_ref, f32[960,8,64]{2,1,0:T(8,128)S(1)} %get-tuple-element.28.after_ref, f32[128,64]{1,0:T(8,128)S(1)} %get-tuple-element.29.pre_ref, f32[128,64]{1,0:T(8,128)S(1)} %get-tuple-element.30.scale_ref, f32[64,128]{1,0:T(8,128)S(1)} %get-tuple-element.39.refs_0_, ...), custom_call_target="tpu_custom_call" | custom-call | tf_op jit(solution)/shard_map/sweep/pallas_call | solution.py:322
Async XLA Ops:
  0.0 8.8 %copy-start = (bf16[2,64,4096]{2,1,0:T(8,128)(2,1)S(1)}, bf16[2,64,4096]{2,1,0:T(8,128)(2,1)}, u32[]{:S(2)}) copy-start(bf16[2,64,4096]{2,1,0:T(8,128)(2,1)} %refs_1_.1) | copy-start | bytes 3145732
  0.0 22.9 %copy-start.1 = (f32[64,128]{1,0:T(8,128)S(1)}, f32[64,128]{1,0:T(8,128)}, u32[]{:S(2)}) copy-start(f32[64,128]{1,0:T(8,128)} %refs_2_.1) | copy-start | bytes 98308
  0.0 4.2 %collective-permute-start.1 = (bf16[1024,128]{1,0:T(8,128)(2,1)}, bf16[1024,128]{1,0:T(8,128)(2,1)S(1)}, u32[]{:S(2)}, u32[]{:S(2)}) collective-permute-start(bf16[1024,128]{1,0:T(8,128)(2,1)} %b_ref.1), channel_id=1, source_target_pairs={{0,8},{1,9},{2,10},{3,11},{4,12},{5,13},{6,14},{7,15},{8,0},{9,1},... | collective-permute-start | bytes 786440 | tf_op jit(solution)/shard_map/ppermute | solution.py:228
  0.5 3.7 %collective-permute-start.2 = (bf16[1024,128]{1,0:T(8,128)(2,1)}, bf16[1024,128]{1,0:T(8,128)(2,1)S(1)}, u32[]{:S(2)}, u32[]{:S(2)}) collective-permute-start(bf16[1024,128]{1,0:T(8,128)(2,1)} %c_ref.1), channel_id=1, source_target_pairs={{0,8},{1,9},{2,10},{3,11},{4,12},{5,13},{6,14},{7,15},{8,0},{9,1},... | collective-permute-start | bytes 786440 | tf_op jit(solution)/shard_map/ppermute | solution.py:228
  0.5 4.2 %collective-permute-start = (s32[2,3]{1,0:T(2,128)}, s32[2,3]{1,0:T(2,128)S(1)}, u32[]{:S(2)}, u32[]{:S(2)}) collective-permute-start(s32[2,3]{1,0:T(2,128)} %ask_ref.1), channel_id=1, source_target_pairs={{0,24},{1,25},{2,26},{3,27},{4,28},{5,29},{6,30},{7,31},{8,16},{9,... | collective-permute-start | bytes 80 | tf_op jit(solution)/shard_map/ppermute | solution.py:228
  4.9 3.9 %collective-permute-start.4 = (bf16[4,64,128]{2,1,0:T(8,128)(2,1)S(1)}, bf16[4,64,128]{2,1,0:T(8,128)(2,1)S(1)}, u32[]{:S(2)}, u32[]{:S(2)}) collective-permute-start(bf16[4,64,128]{2,1,0:T(8,128)(2,1)S(1)} %gather_rows.1), channel_id=1, source_target_pairs={{0,24},{1,25},{2,26},{3,27},{4,28},{5,29},{6,30},{7,31},{8,16},{9,... | collective-permute-start | bytes 196616 | tf_op jit(solution)/shard_map/ppermute | solution.py:228
  6.6 0.7 %copy-start.2 = (s32[2,3]{1,0:T(2,128)S(1)}, s32[2,3]{1,0:T(2,128)}, u32[]{:S(2)}) copy-start(s32[2,3]{1,0:T(2,128)} %ask_ref.1) | copy-start | bytes 76
  9.3 5.5 %collective-permute-start.8 = (f32[136,128]{1,0:T(8,128)S(1)}, f32[136,128]{1,0:T(8,128)S(1)}, u32[]{:S(2)}, u32[]{:S(2)}) collective-permute-start(f32[136,128]{1,0:T(8,128)S(1)} %block_products.1.refs_0_), channel_id=1, source_target_pairs={{0,25},{1,24},{2,27},{3,26},{4,29},{5,28},{6,31},{7,30},{8,17},{9,... | collective-permute-start | bytes 208904 | tf_op jit(solution)/shard_map/ppermute | solution.py:228
  12.2 4.5 %collective-permute-start.7 = (f32[136,128]{1,0:T(8,128)S(1)}, f32[136,128]{1,0:T(8,128)S(1)}, u32[]{:S(2)}, u32[]{:S(2)}) collective-permute-start(f32[136,128]{1,0:T(8,128)S(1)} %block_products.1.refs_0_), channel_id=1, source_target_pairs={{0,24},{1,25},{2,26},{3,27},{4,28},{5,29},{6,30},{7,31},{8,16},{9,... | collective-permute-start | bytes 208904 | tf_op jit(solution)/shard_map/ppermute | solution.py:228
  12.8 4.6 %collective-permute-start.6 = (f32[136,128]{1,0:T(8,128)S(1)}, f32[136,128]{1,0:T(8,128)S(1)}, u32[]{:S(2)}, u32[]{:S(2)}) collective-permute-start(f32[136,128]{1,0:T(8,128)S(1)} %block_products.1.refs_0_), channel_id=1, source_target_pairs={{0,9},{1,8},{2,11},{3,10},{4,13},{5,12},{6,15},{7,14},{8,1},{9,0},... | collective-permute-start | bytes 208904 | tf_op jit(solution)/shard_map/ppermute | solution.py:228
  12.9 10.1 %collective-permute-start.3 = (f32[2,128,128]{2,1,0:T(8,128)S(1)}, f32[2,128,128]{2,1,0:T(8,128)S(1)}, u32[]{:S(2)}, u32[]{:S(2)}) collective-permute-start(f32[2,128,128]{2,1,0:T(8,128)S(1)} %chip_gram.1.refs_0_), channel_id=1, source_target_pairs={{0,24},{1,25},{2,26},{3,27},{4,28},{5,29},{6,30},{7,31},{8,16},{9,... | collective-permute-start | bytes 393224 | tf_op jit(solution)/shard_map/ppermute | solution.py:228
  14.5 2.9 %collective-permute-start.5 = (f32[136,128]{1,0:T(8,128)S(1)}, f32[136,128]{1,0:T(8,128)S(1)}, u32[]{:S(2)}, u32[]{:S(2)}) collective-permute-start(f32[136,128]{1,0:T(8,128)S(1)} %block_products.1.refs_0_), channel_id=1, source_target_pairs={{0,8},{1,9},{2,10},{3,11},{4,12},{5,13},{6,14},{7,15},{8,0},{9,1},... | collective-permute-start | bytes 208904 | tf_op jit(solution)/shard_map/ppermute | solution.py:228
  14.8 2.6 %collective-permute-start.11 = (f32[136,128]{1,0:T(8,128)S(1)}, f32[136,128]{1,0:T(8,128)S(1)}, u32[]{:S(2)}, u32[]{:S(2)}) collective-permute-start(f32[136,128]{1,0:T(8,128)S(1)} %collective-permute-done.8.refs_4_), channel_id=1, source_target_pairs={{0,8},{1,9},{2,10},{3,11},{4,12},{5,13},{6,14},{7,15},{8,0},{9,1},... | collective-permute-start | bytes 208904 | tf_op jit(solution)/shard_map/ppermute | solution.py:228
  16.7 1.6 %collective-permute-start.10 = (f32[136,128]{1,0:T(8,128)S(1)}, f32[136,128]{1,0:T(8,128)S(1)}, u32[]{:S(2)}, u32[]{:S(2)}) collective-permute-start(f32[136,128]{1,0:T(8,128)S(1)} %collective-permute-done.7.refs_3_), channel_id=1, source_target_pairs={{0,8},{1,9},{2,10},{3,11},{4,12},{5,13},{6,14},{7,15},{8,0},{9,1},... | collective-permute-start | bytes 208904 | tf_op jit(solution)/shard_map/ppermute | solution.py:228
  17.4 1.3 %collective-permute-start.9 = (f32[136,128]{1,0:T(8,128)S(1)}, f32[136,128]{1,0:T(8,128)S(1)}, u32[]{:S(2)}, u32[]{:S(2)}) collective-permute-start(f32[136,128]{1,0:T(8,128)S(1)} %collective-permute-done.6.refs_2_), channel_id=1, source_target_pairs={{0,8},{1,9},{2,10},{3,11},{4,12},{5,13},{6,14},{7,15},{8,0},{9,1},... | collective-permute-start | bytes 208904 | tf_op jit(solution)/shard_map/ppermute | solution.py:228
  18.9 5.8 %collective-permute-start.12 = (f32[64,128]{1,0:T(8,128)S(1)}, f32[64,128]{1,0:T(8,128)S(1)}, u32[]{:S(2)}, u32[]{:S(2)}) collective-permute-start(f32[64,128]{1,0:T(8,128)S(1)} %get-tuple-element.40), channel_id=1, source_target_pairs={{0,14},{1,15},{2,12},{3,13},{4,10},{5,11},{6,8},{7,9},{8,6},{9,7},... | collective-permute-start | bytes 98312 | tf_op jit(solution)/shard_map/ppermute | solution.py:228
  22.3 4.2 %collective-permute-start.13 = (f32[64,128]{1,0:T(8,128)S(1)}, f32[64,128]{1,0:T(8,128)S(1)}, u32[]{:S(2)}, u32[]{:S(2)}) collective-permute-start(f32[64,128]{1,0:T(8,128)S(1)} %get-tuple-element.41), channel_id=1, source_target_pairs={{0,12},{1,13},{2,14},{3,15},{4,8},{5,9},{6,10},{7,11},{8,4},{9,5},... | collective-permute-start | bytes 98312 | tf_op jit(solution)/shard_map/ppermute | solution.py:228
  22.3 4.2 %collective-permute-start.14 = (f32[64,128]{1,0:T(8,128)S(1)}, f32[64,128]{1,0:T(8,128)S(1)}, u32[]{:S(2)}, u32[]{:S(2)}) collective-permute-start(f32[64,128]{1,0:T(8,128)S(1)} %get-tuple-element.42), channel_id=1, source_target_pairs={{0,10},{1,11},{2,8},{3,9},{4,14},{5,15},{6,12},{7,13},{8,2},{9,3},... | collective-permute-start | bytes 98312 | tf_op jit(solution)/shard_map/ppermute | solution.py:228

commit v5 on v4

--- a/solution.py
+++ b/solution.py
@@ -287,12 +287,17 @@
         compiler_params=params,
         name="block_products",
     )(*local, *found, blocks)
-    others = [
-        move(partial, d, 1, beside)
-        for d in range(n_x)
-        for beside in range(near)
-        if d or beside
-    ]
+    offsets = [(d, b) for d in range(n_x) for b in range(near) if d or b]
+
+    def spread(value, pair):
+        def to(x, c, rep):
+            chips, beside = pair[(x + c + rep % near) % 2]
+            to_rep = rep // near * near + (rep + beside) % near
+            return (x + chips) % n_x, (c + chips + beside) % CORES, to_rep
+
+        return lax.ppermute(value, ("grp", "rep"), moves(n_grp, n_rep, to))
+
+    others = [spread(partial, pair) for pair in zip(offsets, reversed(offsets))]
     prepared = pl.pallas_call(
         functools.partial(prepare_kernel, n_x),
         out_shape=[

time: 28 us -> 27.5 us (0.982)
  waiting for transfers between devices: 6.41 us -> 6 us
    ppermute x15 -> x12, starting transfers between devices: 15.1 us -> 11.5 us  [move(): return lax.ppermute(value, ('grp', 'rep'), moves(n_grp, n_rep, to))]
    ppermute x0 -> x3, starting transfers between devices: none -> 3.57 us  [spread(): return lax.ppermute(value, ('grp', 'rep'), moves(n_grp, n_rep, to))]
    ppermute x15 -> x12, waiting for transfers between devices: 6.41 us -> 4.31 us  [move(): return lax.ppermute(value, ('grp', 'rep'), moves(n_grp, n_rep, to))]
    ppermute x0 -> x3, waiting for transfers between devices: none -> 1.69 us  [spread(): return lax.ppermute(value, ('grp', 'rep'), moves(n_grp, n_rep, to))]
where the time goes in v5:
time: 27.5 us; the launch traced here: 27.3 us
  starting transfers between devices  15.1 us (55%)
  waiting for transfers between devices  6 us (22%)
  Pallas kernels  5.49 us (20%)
  local copies, waits for them, and re-layouts  0.69 us (3%)
    ppermute x12, starting transfers between devices, move(): return lax.ppermute(value, ('grp', 'rep'), moves(n_grp, n_rep, to))  11.5 us
    ppermute x12, waiting for transfers between devices, move(): return lax.ppermute(value, ('grp', 'rep'), moves(n_grp, n_rep, to))  4.31 us
    ppermute x3, starting transfers between devices, spread(): return lax.ppermute(value, ('grp', 'rep'), moves(n_grp, n_rep, to))  3.57 us
    pallas_call x1, Pallas kernels, body(): pl.pallas_call(functools.partial(prepare_kernel, n_x), out_shape=[jax.Sha...  1.71 us
    ppermute x3, waiting for transfers between devices, spread(): return lax.ppermute(value, ('grp', 'rep'), moves(n_grp, n_rep, to))  1.69 us
    pallas_call x1, Pallas kernels, body(): pl.pallas_call(sweep_kernel, out_shape=jax.ShapeDtypeStruct(factor_a.shap...  1.25 us
    pallas_call x1, Pallas kernels, body(): pl.pallas_call(load_kernel, out_shape=[jax.ShapeDtypeStruct(factor_b.shap...  1.04 us
    unnamed x6, local copies, waits for them, and re-layouts  0.69 us
  transfers between devices with their start and end apart: 15, of which 6 were waited for; matrix products, arithmetic and copies ran while one was open for 0% of the time, Pallas kernels for 13%

profile of v5, /device:TPU:0, one launch (start us, length us, event | category | flops | bytes accessed | tf_op | source)
XLA Modules:
  0.0 27.3 jit_solution(3792179128897305008)
XLA Ops:
  0.0 0.0 copy-start
  0.0 0.0 copy-start.1
  0.0 0.5 %collective-permute-start.1 = (bf16[1024,128]{1,0:T(8,128)(2,1)}, bf16[1024,128]{1,0:T(8,128)(2,1)S(1)}, u32[]{:S(2)}, u32[]{:S(2)}) collective-permute-start(bf16[1024,128]{1,0:T(8,128)(2,1)} %b_ref.1), channel_id=1, source_target_pairs={{0,8},{1,9},{2,10},{3,11},{4,12},{5,13},{6,14},{7,15},{8,0},{9,1},... | collective-permute-start | bytes 786440 | tf_op jit(solution)/shard_map/ppermute | solution.py:228
  0.5 0.1 collective-permute-start.2
  0.5 2.6 %collective-permute-start = (s32[2,3]{1,0:T(2,128)}, s32[2,3]{1,0:T(2,128)S(1)}, u32[]{:S(2)}, u32[]{:S(2)}) collective-permute-start(s32[2,3]{1,0:T(2,128)} %ask_ref.1), channel_id=1, source_target_pairs={{0,24},{1,25},{2,26},{3,27},{4,28},{5,29},{6,30},{7,31},{8,16},{9,... | collective-permute-start | bytes 80 | tf_op jit(solution)/shard_map/ppermute | solution.py:228
  3.1 1.0 %load_shards.1 = (bf16[1024,128]{1,0:T(8,128)(2,1)S(1)}, bf16[1024,128]{1,0:T(8,128)(2,1)S(1)}) custom-call(bf16[1024,128]{1,0:T(8,128)(2,1)} %b_ref.1, bf16[1024,128]{1,0:T(8,128)(2,1)} %c_ref.1), custom_call_target="tpu_custom_call" | custom-call | tf_op jit(solution)/shard_map/load_shards/pallas_call | solution.py:233
  4.2 0.0 collective-permute-done.1.refs_2_.mate_b.refs_1_
  4.2 0.0 collective-permute-done.2.refs_4_.mate_c.refs_3_
  4.2 0.5 %chip_gram.1.refs_0_ = f32[2,128,128]{2,1,0:T(8,128)S(1)} custom-call(bf16[1024,128]{1,0:T(8,128)(2,1)S(1)} %get-tuple-element.24.refs_1_.own_b.refs_0_, bf16[1024,128]{1,0:T(8,128)(2,1)S(1)} %collective-permute-done.1.refs_2_.mate_b.refs_1_, bf16[1024,128]{1,0:T(8,128)(2,1)S(1)} %get-tuple-element.25.refs_3_.own_c.refs_2_, ...), custom_call_target="tpu_custom_call" | custom-call | tf_op jit(solution)/shard_map/chip_gram/pallas_call | solution.py:247
  4.7 0.0 collective-permute-done.refs_0_
  4.7 0.1 gather_rows.1
  4.9 1.7 %collective-permute-start.4 = (bf16[4,64,128]{2,1,0:T(8,128)(2,1)S(1)}, bf16[4,64,128]{2,1,0:T(8,128)(2,1)S(1)}, u32[]{:S(2)}, u32[]{:S(2)}) collective-permute-start(bf16[4,64,128]{2,1,0:T(8,128)(2,1)S(1)} %gather_rows.1), channel_id=1, source_target_pairs={{0,24},{1,25},{2,26},{3,27},{4,28},{5,29},{6,30},{7,31},{8,16},{9,... | collective-permute-start | bytes 196616 | tf_op jit(solution)/shard_map/ppermute | solution.py:228
  6.6 0.0 copy-start.2
  6.6 0.7 %copy-done.2 = s32[2,3]{1,0:T(2,128)S(1)} copy-done((s32[2,3]{1,0:T(2,128)S(1)}, s32[2,3]{1,0:T(2,128)}, u32[]{:S(2)}) %copy-start.2) | copy-done | bytes 48
  7.3 0.1 local_rows.1
  7.4 1.4 %collective-permute-done.4.refs_0_ = bf16[4,64,128]{2,1,0:T(8,128)(2,1)S(1)} collective-permute-done((bf16[4,64,128]{2,1,0:T(8,128)(2,1)S(1)}, bf16[4,64,128]{2,1,0:T(8,128)(2,1)S(1)}, u32[]{:S(2)}, u32[]{:S(2)}) %collective-permute-start.4) | collective-permute-done | bytes 65568 | tf_op jit(solution)/shard_map/ppermute | solution.py:228
  8.8 0.0 copy-done
  8.8 0.5 %block_products.1.refs_0_ = f32[136,128]{1,0:T(8,128)S(1)} custom-call(bf16[4,64,128]{2,1,0:T(8,128)(2,1)S(1)} %get-tuple-element.35.rows_ref, s32[4,8,128]{2,1,0:T(8,128)S(1)} %get-tuple-element.36.far_ref, f32[8,128]{1,0:T(8,128)S(1)} %get-tuple-element.37.first_ref, bf16[4,64,128]{2,1,0:T(8,128)(2,1)S(1)} %collective-permute-done.4.refs_0_, ...), custom_call_target="tpu_custom_call" | custom-call | tf_op jit(solution)/shard_map/block_products/pallas_call | solution.py:282
  9.3 3.2 %collective-permute-start.8 = (f32[136,128]{1,0:T(8,128)S(1)}, f32[136,128]{1,0:T(8,128)S(1)}, u32[]{:S(2)}, u32[]{:S(2)}) collective-permute-start(f32[136,128]{1,0:T(8,128)S(1)} %block_products.1.refs_0_), channel_id=1, source_target_pairs={{0,17},{1,8},{2,19},{3,10},{4,21},{5,12},{6,23},{7,14},{8,1},{9,24... | collective-permute-start | bytes 208904 | tf_op jit(solution)/shard_map/ppermute | solution.py:298
  12.5 0.0 collective-permute-start.7
  12.5 0.4 %collective-permute-start.6 = (f32[136,128]{1,0:T(8,128)S(1)}, f32[136,128]{1,0:T(8,128)S(1)}, u32[]{:S(2)}, u32[]{:S(2)}) collective-permute-start(f32[136,128]{1,0:T(8,128)S(1)} %block_products.1.refs_0_), channel_id=1, source_target_pairs={{0,9},{1,16},{2,11},{3,18},{4,13},{5,20},{6,15},{7,22},{8,25},{9,0... | collective-permute-start | bytes 208904 | tf_op jit(solution)/shard_map/ppermute | solution.py:298
  12.9 1.4 %collective-permute-start.3 = (f32[2,128,128]{2,1,0:T(8,128)S(1)}, f32[2,128,128]{2,1,0:T(8,128)S(1)}, u32[]{:S(2)}, u32[]{:S(2)}) collective-permute-start(f32[2,128,128]{2,1,0:T(8,128)S(1)} %chip_gram.1.refs_0_), channel_id=1, source_target_pairs={{0,24},{1,25},{2,26},{3,27},{4,28},{5,29},{6,30},{7,31},{8,16},{9,... | collective-permute-start | bytes 393224 | tf_op jit(solution)/shard_map/ppermute | solution.py:228
  14.3 0.6 %collective-permute-start.5 = (f32[136,128]{1,0:T(8,128)S(1)}, f32[136,128]{1,0:T(8,128)S(1)}, u32[]{:S(2)}, u32[]{:S(2)}) collective-permute-start(f32[136,128]{1,0:T(8,128)S(1)} %block_products.1.refs_0_), channel_id=1, source_target_pairs={{0,8},{1,9},{2,10},{3,11},{4,12},{5,13},{6,14},{7,15},{8,0},{9,1},... | collective-permute-start | bytes 208904 | tf_op jit(solution)/shard_map/ppermute | solution.py:228
  14.9 0.6 %collective-permute-done.8.refs_4_ = f32[136,128]{1,0:T(8,128)S(1)} collective-permute-done((f32[136,128]{1,0:T(8,128)S(1)}, f32[136,128]{1,0:T(8,128)S(1)}, u32[]{:S(2)}, u32[]{:S(2)}) %collective-permute-start.8) | collective-permute-done | bytes 69664 | tf_op jit(solution)/shard_map/ppermute | solution.py:298
  15.5 0.0 collective-permute-start.11
  15.5 1.1 %collective-permute-done.7.refs_3_ = f32[136,128]{1,0:T(8,128)S(1)} collective-permute-done((f32[136,128]{1,0:T(8,128)S(1)}, f32[136,128]{1,0:T(8,128)S(1)}, u32[]{:S(2)}, u32[]{:S(2)}) %collective-permute-start.7) | collective-permute-done | bytes 69664 | tf_op jit(solution)/shard_map/ppermute | solution.py:298
  16.6 0.0 collective-permute-start.10
  16.6 0.0 collective-permute-done.6.refs_2_
  16.6 0.5 %collective-permute-start.9 = (f32[136,128]{1,0:T(8,128)S(1)}, f32[136,128]{1,0:T(8,128)S(1)}, u32[]{:S(2)}, u32[]{:S(2)}) collective-permute-start(f32[136,128]{1,0:T(8,128)S(1)} %collective-permute-done.6.refs_2_), channel_id=1, source_target_pairs={{0,8},{1,9},{2,10},{3,11},{4,12},{5,13},{6,14},{7,15},{8,0},{9,1},... | collective-permute-start | bytes 208904 | tf_op jit(solution)/shard_map/ppermute | solution.py:228
  17.1 0.0 collective-permute-done.5.refs_1_
  17.1 0.0 collective-permute-done.11.refs_7_
  17.1 0.7 %collective-permute-done.10.refs_6_ = f32[136,128]{1,0:T(8,128)S(1)} collective-permute-done((f32[136,128]{1,0:T(8,128)S(1)}, f32[136,128]{1,0:T(8,128)S(1)}, u32[]{:S(2)}, u32[]{:S(2)}) %collective-permute-start.10) | collective-permute-done | bytes 69664 | tf_op jit(solution)/shard_map/ppermute | solution.py:228
  17.8 0.2 collective-permute-done.9.refs_5_
  18.0 0.2 sum_by_owner.1
  18.2 3.6 %collective-permute-start.12 = (f32[64,128]{1,0:T(8,128)S(1)}, f32[64,128]{1,0:T(8,128)S(1)}, u32[]{:S(2)}, u32[]{:S(2)}) collective-permute-start(f32[64,128]{1,0:T(8,128)S(1)} %get-tuple-element.40), channel_id=1, source_target_pairs={{0,14},{1,15},{2,12},{3,13},{4,10},{5,11},{6,8},{7,9},{8,6},{9,7},... | collective-permute-start | bytes 98312 | tf_op jit(solution)/shard_map/ppermute | solution.py:228
  21.8 0.0 collective-permute-start.13
  21.8 0.5 %collective-permute-start.14 = (f32[64,128]{1,0:T(8,128)S(1)}, f32[64,128]{1,0:T(8,128)S(1)}, u32[]{:S(2)}, u32[]{:S(2)}) collective-permute-start(f32[64,128]{1,0:T(8,128)S(1)} %get-tuple-element.42), channel_id=1, source_target_pairs={{0,10},{1,11},{2,8},{3,9},{4,14},{5,15},{6,12},{7,13},{8,2},{9,3},... | collective-permute-start | bytes 98312 | tf_op jit(solution)/shard_map/ppermute | solution.py:228
  22.3 0.0 collective-permute-done.3.refs_1_
  22.3 0.0 copy-done.1
  22.3 1.7 %prepare_sweep.1 = (f32[128,8,64]{2,1,0:T(8,128)S(1)}, f32[960,8,64]{2,1,0:T(8,128)S(1)}, f32[128,64]{1,0:T(8,128)S(1)}, f32[128,64]{1,0:T(8,128)S(1)}) custom-call(f32[2,128,128]{2,1,0:T(8,128)S(1)} %chip_gram.1.refs_0_, f32[2,128,128]{2,1,0:T(8,128)S(1)} %collective-permute-done.3.refs_1_, f32[64,128]{1,0:T(8,128)S(1)} %copy-done.1), custom_call_target="tpu_custom_call" | custom-call | tf_op jit(solution)/shard_map/prepare_sweep/pallas_call | solution.py:301
  24.0 0.0 collective-permute-done.12.refs_1_
  24.1 2.0 %collective-permute-done.13.refs_2_ = f32[64,128]{1,0:T(8,128)S(1)} collective-permute-done((f32[64,128]{1,0:T(8,128)S(1)}, f32[64,128]{1,0:T(8,128)S(1)}, u32[]{:S(2)}, u32[]{:S(2)}) %collective-permute-start.13) | collective-permute-done | bytes 32800 | tf_op jit(solution)/shard_map/ppermute | solution.py:228
  26.1 0.0 collective-permute-done.14.refs_3_
  26.1 1.2 %sweep.1 = f32[64,128]{1,0:T(8,128)} custom-call(f32[128,8,64]{2,1,0:T(8,128)S(1)} %get-tuple-element.27.within_ref, f32[960,8,64]{2,1,0:T(8,128)S(1)} %get-tuple-element.28.after_ref, f32[128,64]{1,0:T(8,128)S(1)} %get-tuple-element.29.pre_ref, f32[128,64]{1,0:T(8,128)S(1)} %get-tuple-element.30.scale_ref, f32[64,128]{1,0:T(8,128)S(1)} %get-tuple-element.39.refs_0_, ...), custom_call_target="tpu_custom_call" | custom-call | tf_op jit(solution)/shard_map/sweep/pallas_call | solution.py:327
Async XLA Ops:
  0.0 8.8 %copy-start = (bf16[2,64,4096]{2,1,0:T(8,128)(2,1)S(1)}, bf16[2,64,4096]{2,1,0:T(8,128)(2,1)}, u32[]{:S(2)}) copy-start(bf16[2,64,4096]{2,1,0:T(8,128)(2,1)} %refs_1_.1) | copy-start | bytes 3145732
  0.0 22.3 %copy-start.1 = (f32[64,128]{1,0:T(8,128)S(1)}, f32[64,128]{1,0:T(8,128)}, u32[]{:S(2)}) copy-start(f32[64,128]{1,0:T(8,128)} %refs_2_.1) | copy-start | bytes 98308
  0.0 4.2 %collective-permute-start.1 = (bf16[1024,128]{1,0:T(8,128)(2,1)}, bf16[1024,128]{1,0:T(8,128)(2,1)S(1)}, u32[]{:S(2)}, u32[]{:S(2)}) collective-permute-start(bf16[1024,128]{1,0:T(8,128)(2,1)} %b_ref.1), channel_id=1, source_target_pairs={{0,8},{1,9},{2,10},{3,11},{4,12},{5,13},{6,14},{7,15},{8,0},{9,1},... | collective-permute-start | bytes 786440 | tf_op jit(solution)/shard_map/ppermute | solution.py:228
  0.5 3.7 %collective-permute-start.2 = (bf16[1024,128]{1,0:T(8,128)(2,1)}, bf16[1024,128]{1,0:T(8,128)(2,1)S(1)}, u32[]{:S(2)}, u32[]{:S(2)}) collective-permute-start(bf16[1024,128]{1,0:T(8,128)(2,1)} %c_ref.1), channel_id=1, source_target_pairs={{0,8},{1,9},{2,10},{3,11},{4,12},{5,13},{6,14},{7,15},{8,0},{9,1},... | collective-permute-start | bytes 786440 | tf_op jit(solution)/shard_map/ppermute | solution.py:228
  0.5 4.2 %collective-permute-start = (s32[2,3]{1,0:T(2,128)}, s32[2,3]{1,0:T(2,128)S(1)}, u32[]{:S(2)}, u32[]{:S(2)}) collective-permute-start(s32[2,3]{1,0:T(2,128)} %ask_ref.1), channel_id=1, source_target_pairs={{0,24},{1,25},{2,26},{3,27},{4,28},{5,29},{6,30},{7,31},{8,16},{9,... | collective-permute-start | bytes 80 | tf_op jit(solution)/shard_map/ppermute | solution.py:228
  4.9 3.9 %collective-permute-start.4 = (bf16[4,64,128]{2,1,0:T(8,128)(2,1)S(1)}, bf16[4,64,128]{2,1,0:T(8,128)(2,1)S(1)}, u32[]{:S(2)}, u32[]{:S(2)}) collective-permute-start(bf16[4,64,128]{2,1,0:T(8,128)(2,1)S(1)} %gather_rows.1), channel_id=1, source_target_pairs={{0,24},{1,25},{2,26},{3,27},{4,28},{5,29},{6,30},{7,31},{8,16},{9,... | collective-permute-start | bytes 196616 | tf_op jit(solution)/shard_map/ppermute | solution.py:228
  6.6 0.7 %copy-start.2 = (s32[2,3]{1,0:T(2,128)S(1)}, s32[2,3]{1,0:T(2,128)}, u32[]{:S(2)}) copy-start(s32[2,3]{1,0:T(2,128)} %ask_ref.1) | copy-start | bytes 76
  9.3 6.2 %collective-permute-start.8 = (f32[136,128]{1,0:T(8,128)S(1)}, f32[136,128]{1,0:T(8,128)S(1)}, u32[]{:S(2)}, u32[]{:S(2)}) collective-permute-start(f32[136,128]{1,0:T(8,128)S(1)} %block_products.1.refs_0_), channel_id=1, source_target_pairs={{0,17},{1,8},{2,19},{3,10},{4,21},{5,12},{6,23},{7,14},{8,1},{9,24... | collective-permute-start | bytes 208904 | tf_op jit(solution)/shard_map/ppermute | solution.py:298
  12.5 4.1 %collective-permute-start.7 = (f32[136,128]{1,0:T(8,128)S(1)}, f32[136,128]{1,0:T(8,128)S(1)}, u32[]{:S(2)}, u32[]{:S(2)}) collective-permute-start(f32[136,128]{1,0:T(8,128)S(1)} %block_products.1.refs_0_), channel_id=1, source_target_pairs={{0,24},{1,25},{2,26},{3,27},{4,28},{5,29},{6,30},{7,31},{8,16},{9,... | collective-permute-start | bytes 208904 | tf_op jit(solution)/shard_map/ppermute | solution.py:298
  12.5 4.1 %collective-permute-start.6 = (f32[136,128]{1,0:T(8,128)S(1)}, f32[136,128]{1,0:T(8,128)S(1)}, u32[]{:S(2)}, u32[]{:S(2)}) collective-permute-start(f32[136,128]{1,0:T(8,128)S(1)} %block_products.1.refs_0_), channel_id=1, source_target_pairs={{0,9},{1,16},{2,11},{3,18},{4,13},{5,20},{6,15},{7,22},{8,25},{9,0... | collective-permute-start | bytes 208904 | tf_op jit(solution)/shard_map/ppermute | solution.py:298
  12.9 9.5 %collective-permute-start.3 = (f32[2,128,128]{2,1,0:T(8,128)S(1)}, f32[2,128,128]{2,1,0:T(8,128)S(1)}, u32[]{:S(2)}, u32[]{:S(2)}) collective-permute-start(f32[2,128,128]{2,1,0:T(8,128)S(1)} %chip_gram.1.refs_0_), channel_id=1, source_target_pairs={{0,24},{1,25},{2,26},{3,27},{4,28},{5,29},{6,30},{7,31},{8,16},{9,... | collective-permute-start | bytes 393224 | tf_op jit(solution)/shard_map/ppermute | solution.py:228
  14.3 2.8 %collective-permute-start.5 = (f32[136,128]{1,0:T(8,128)S(1)}, f32[136,128]{1,0:T(8,128)S(1)}, u32[]{:S(2)}, u32[]{:S(2)}) collective-permute-start(f32[136,128]{1,0:T(8,128)S(1)} %block_products.1.refs_0_), channel_id=1, source_target_pairs={{0,8},{1,9},{2,10},{3,11},{4,12},{5,13},{6,14},{7,15},{8,0},{9,1},... | collective-permute-start | bytes 208904 | tf_op jit(solution)/shard_map/ppermute | solution.py:228
  15.5 1.6 %collective-permute-start.11 = (f32[136,128]{1,0:T(8,128)S(1)}, f32[136,128]{1,0:T(8,128)S(1)}, u32[]{:S(2)}, u32[]{:S(2)}) collective-permute-start(f32[136,128]{1,0:T(8,128)S(1)} %collective-permute-done.8.refs_4_), channel_id=1, source_target_pairs={{0,8},{1,9},{2,10},{3,11},{4,12},{5,13},{6,14},{7,15},{8,0},{9,1},... | collective-permute-start | bytes 208904 | tf_op jit(solution)/shard_map/ppermute | solution.py:228
  16.6 1.3 %collective-permute-start.10 = (f32[136,128]{1,0:T(8,128)S(1)}, f32[136,128]{1,0:T(8,128)S(1)}, u32[]{:S(2)}, u32[]{:S(2)}) collective-permute-start(f32[136,128]{1,0:T(8,128)S(1)} %collective-permute-done.7.refs_3_), channel_id=1, source_target_pairs={{0,8},{1,9},{2,10},{3,11},{4,12},{5,13},{6,14},{7,15},{8,0},{9,1},... | collective-permute-start | bytes 208904 | tf_op jit(solution)/shard_map/ppermute | solution.py:228
  16.6 1.4 %collective-permute-start.9 = (f32[136,128]{1,0:T(8,128)S(1)}, f32[136,128]{1,0:T(8,128)S(1)}, u32[]{:S(2)}, u32[]{:S(2)}) collective-permute-start(f32[136,128]{1,0:T(8,128)S(1)} %collective-permute-done.6.refs_2_), channel_id=1, source_target_pairs={{0,8},{1,9},{2,10},{3,11},{4,12},{5,13},{6,14},{7,15},{8,0},{9,1},... | collective-permute-start | bytes 208904 | tf_op jit(solution)/shard_map/ppermute | solution.py:228
  18.2 5.8 %collective-permute-start.12 = (f32[64,128]{1,0:T(8,128)S(1)}, f32[64,128]{1,0:T(8,128)S(1)}, u32[]{:S(2)}, u32[]{:S(2)}) collective-permute-start(f32[64,128]{1,0:T(8,128)S(1)} %get-tuple-element.40), channel_id=1, source_target_pairs={{0,14},{1,15},{2,12},{3,13},{4,10},{5,11},{6,8},{7,9},{8,6},{9,7},... | collective-permute-start | bytes 98312 | tf_op jit(solution)/shard_map/ppermute | solution.py:228
  21.8 4.2 %collective-permute-start.13 = (f32[64,128]{1,0:T(8,128)S(1)}, f32[64,128]{1,0:T(8,128)S(1)}, u32[]{:S(2)}, u32[]{:S(2)}) collective-permute-start(f32[64,128]{1,0:T(8,128)S(1)} %get-tuple-element.41), channel_id=1, source_target_pairs={{0,12},{1,13},{2,14},{3,15},{4,8},{5,9},{6,10},{7,11},{8,4},{9,5},... | collective-permute-start | bytes 98312 | tf_op jit(solution)/shard_map/ppermute | solution.py:228
  21.8 4.2 %collective-permute-start.14 = (f32[64,128]{1,0:T(8,128)S(1)}, f32[64,128]{1,0:T(8,128)S(1)}, u32[]{:S(2)}, u32[]{:S(2)}) collective-permute-start(f32[64,128]{1,0:T(8,128)S(1)} %get-tuple-element.42), channel_id=1, source_target_pairs={{0,10},{1,11},{2,8},{3,9},{4,14},{5,15},{6,12},{7,13},{8,2},{9,3},... | collective-permute-start | bytes 98312 | tf_op jit(solution)/shard_map/ppermute | solution.py:228

commit v6 on v5

--- a/solution.py
+++ b/solution.py
@@ -92,9 +92,9 @@
 
     def rows_of(n, mode):
         slot = mode * nblk + n
-        rows = rows_ref[slot].astype(jnp.float32)
+        rows = rows_ref[slot]
         for d in range(1, n_x):
-            rows = jnp.where(far_ref[slot, :1] == d, found[d - 1][slot].astype(jnp.float32), rows)
+            rows = jnp.where(far_ref[slot, :1] == d, found[d - 1][slot], rows)
         return rows
 
     step = 8
@@ -103,7 +103,7 @@
         rank = left.shape[1]
         total = jnp.zeros((BS, rank), jnp.float32)
         for j in range(0, BS, step):
-            khatri = (left[j : j + step, None, :] * right[None, :, :]).astype(jnp.bfloat16)
+            khatri = left[j : j + step, None, :] * right[None, :, :]
             total += jnp.dot(
                 blocks_ref[n, :, j * BS : (j + step) * BS],
                 khatri.reshape(step * BS, rank),

time: 27.5 us -> 27.4 us (level)
  no operation moved by 1% of the time
where the time goes in v6:
time: 27.4 us; the launch traced here: 27.3 us
  starting transfers between devices  15.1 us (55%)
  waiting for transfers between devices  6 us (22%)
  Pallas kernels  5.43 us (20%)
  local copies, waits for them, and re-layouts  0.69 us (3%)
    ppermute x12, starting transfers between devices, move(): return lax.ppermute(value, ('grp', 'rep'), moves(n_grp, n_rep, to))  11.5 us
    ppermute x12, waiting for transfers between devices, move(): return lax.ppermute(value, ('grp', 'rep'), moves(n_grp, n_rep, to))  4.3 us
    ppermute x3, starting transfers between devices, spread(): return lax.ppermute(value, ('grp', 'rep'), moves(n_grp, n_rep, to))  3.56 us
    pallas_call x1, Pallas kernels, body(): pl.pallas_call(functools.partial(prepare_kernel, n_x), out_shape=[jax.Sha...  1.71 us
    ppermute x3, waiting for transfers between devices, spread(): return lax.ppermute(value, ('grp', 'rep'), moves(n_grp, n_rep, to))  1.7 us
    pallas_call x1, Pallas kernels, body(): pl.pallas_call(sweep_kernel, out_shape=jax.ShapeDtypeStruct(factor_a.shap...  1.25 us
    pallas_call x1, Pallas kernels, body(): pl.pallas_call(load_kernel, out_shape=[jax.ShapeDtypeStruct(factor_b.shap...  1.04 us
    unnamed x6, local copies, waits for them, and re-layouts  0.69 us
  transfers between devices with their start and end apart: 15, of which 6 were waited for; matrix products, arithmetic and copies ran while one was open for 0% of the time, Pallas kernels for 13%

profile of v6, /device:TPU:0, one launch (start us, length us, event | category | flops | bytes accessed | tf_op | source)
XLA Modules:
  0.0 27.3 jit_solution(4659071166430016739)
XLA Ops:
  0.0 0.0 copy-start
  0.0 0.0 copy-start.1
  0.0 0.5 %collective-permute-start.1 = (bf16[1024,128]{1,0:T(8,128)(2,1)}, bf16[1024,128]{1,0:T(8,128)(2,1)S(1)}, u32[]{:S(2)}, u32[]{:S(2)}) collective-permute-start(bf16[1024,128]{1,0:T(8,128)(2,1)} %b_ref.1), channel_id=1, source_target_pairs={{0,8},{1,9},{2,10},{3,11},{4,12},{5,13},{6,14},{7,15},{8,0},{9,1},... | collective-permute-start | bytes 786440 | tf_op jit(solution)/shard_map/ppermute | solution.py:228
  0.5 0.1 collective-permute-start.2
  0.5 2.6 %collective-permute-start = (s32[2,3]{1,0:T(2,128)}, s32[2,3]{1,0:T(2,128)S(1)}, u32[]{:S(2)}, u32[]{:S(2)}) collective-permute-start(s32[2,3]{1,0:T(2,128)} %ask_ref.1), channel_id=1, source_target_pairs={{0,24},{1,25},{2,26},{3,27},{4,28},{5,29},{6,30},{7,31},{8,16},{9,... | collective-permute-start | bytes 80 | tf_op jit(solution)/shard_map/ppermute | solution.py:228
  3.1 1.0 %load_shards.1 = (bf16[1024,128]{1,0:T(8,128)(2,1)S(1)}, bf16[1024,128]{1,0:T(8,128)(2,1)S(1)}) custom-call(bf16[1024,128]{1,0:T(8,128)(2,1)} %b_ref.1, bf16[1024,128]{1,0:T(8,128)(2,1)} %c_ref.1), custom_call_target="tpu_custom_call" | custom-call | tf_op jit(solution)/shard_map/load_shards/pallas_call | solution.py:233
  4.2 0.0 collective-permute-done.1.refs_2_.mate_b.refs_1_
  4.2 0.0 collective-permute-done.2.refs_4_.mate_c.refs_3_
  4.2 0.5 %chip_gram.1.refs_0_ = f32[2,128,128]{2,1,0:T(8,128)S(1)} custom-call(bf16[1024,128]{1,0:T(8,128)(2,1)S(1)} %get-tuple-element.24.refs_1_.own_b.refs_0_, bf16[1024,128]{1,0:T(8,128)(2,1)S(1)} %collective-permute-done.1.refs_2_.mate_b.refs_1_, bf16[1024,128]{1,0:T(8,128)(2,1)S(1)} %get-tuple-element.25.refs_3_.own_c.refs_2_, ...), custom_call_target="tpu_custom_call" | custom-call | tf_op jit(solution)/shard_map/chip_gram/pallas_call | solution.py:247
  4.7 0.0 collective-permute-done.refs_0_
  4.7 0.1 gather_rows.1
  4.9 1.7 %collective-permute-start.4 = (bf16[4,64,128]{2,1,0:T(8,128)(2,1)S(1)}, bf16[4,64,128]{2,1,0:T(8,128)(2,1)S(1)}, u32[]{:S(2)}, u32[]{:S(2)}) collective-permute-start(bf16[4,64,128]{2,1,0:T(8,128)(2,1)S(1)} %gather_rows.1), channel_id=1, source_target_pairs={{0,24},{1,25},{2,26},{3,27},{4,28},{5,29},{6,30},{7,31},{8,16},{9,... | collective-permute-start | bytes 196616 | tf_op jit(solution)/shard_map/ppermute | solution.py:228
  6.6 0.0 copy-start.2
  6.6 0.7 %copy-done.2 = s32[2,3]{1,0:T(2,128)S(1)} copy-done((s32[2,3]{1,0:T(2,128)S(1)}, s32[2,3]{1,0:T(2,128)}, u32[]{:S(2)}) %copy-start.2) | copy-done | bytes 48
  7.3 0.1 local_rows.1
  7.4 1.4 %collective-permute-done.4.refs_0_ = bf16[4,64,128]{2,1,0:T(8,128)(2,1)S(1)} collective-permute-done((bf16[4,64,128]{2,1,0:T(8,128)(2,1)S(1)}, bf16[4,64,128]{2,1,0:T(8,128)(2,1)S(1)}, u32[]{:S(2)}, u32[]{:S(2)}) %collective-permute-start.4) | collective-permute-done | bytes 65568 | tf_op jit(solution)/shard_map/ppermute | solution.py:228
  8.8 0.0 copy-done
  8.8 0.4 %block_products.1.refs_0_ = f32[136,128]{1,0:T(8,128)S(1)} custom-call(bf16[4,64,128]{2,1,0:T(8,128)(2,1)S(1)} %get-tuple-element.35.rows_ref, s32[4,8,128]{2,1,0:T(8,128)S(1)} %get-tuple-element.36.far_ref, f32[8,128]{1,0:T(8,128)S(1)} %get-tuple-element.37.first_ref, bf16[4,64,128]{2,1,0:T(8,128)(2,1)S(1)} %collective-permute-done.4.refs_0_, ...), custom_call_target="tpu_custom_call" | custom-call | tf_op jit(solution)/shard_map/block_products/pallas_call | solution.py:282
  9.2 3.2 %collective-permute-start.8 = (f32[136,128]{1,0:T(8,128)S(1)}, f32[136,128]{1,0:T(8,128)S(1)}, u32[]{:S(2)}, u32[]{:S(2)}) collective-permute-start(f32[136,128]{1,0:T(8,128)S(1)} %block_products.1.refs_0_), channel_id=1, source_target_pairs={{0,17},{1,8},{2,19},{3,10},{4,21},{5,12},{6,23},{7,14},{8,1},{9,24... | collective-permute-start | bytes 208904 | tf_op jit(solution)/shard_map/ppermute | solution.py:298
  12.4 0.0 collective-permute-start.7
  12.4 0.4 %collective-permute-start.6 = (f32[136,128]{1,0:T(8,128)S(1)}, f32[136,128]{1,0:T(8,128)S(1)}, u32[]{:S(2)}, u32[]{:S(2)}) collective-permute-start(f32[136,128]{1,0:T(8,128)S(1)} %block_products.1.refs_0_), channel_id=1, source_target_pairs={{0,9},{1,16},{2,11},{3,18},{4,13},{5,20},{6,15},{7,22},{8,25},{9,0... | collective-permute-start | bytes 208904 | tf_op jit(solution)/shard_map/ppermute | solution.py:298
  12.8 1.4 %collective-permute-start.3 = (f32[2,128,128]{2,1,0:T(8,128)S(1)}, f32[2,128,128]{2,1,0:T(8,128)S(1)}, u32[]{:S(2)}, u32[]{:S(2)}) collective-permute-start(f32[2,128,128]{2,1,0:T(8,128)S(1)} %chip_gram.1.refs_0_), channel_id=1, source_target_pairs={{0,24},{1,25},{2,26},{3,27},{4,28},{5,29},{6,30},{7,31},{8,16},{9,... | collective-permute-start | bytes 393224 | tf_op jit(solution)/shard_map/ppermute | solution.py:228
  14.2 0.6 %collective-permute-start.5 = (f32[136,128]{1,0:T(8,128)S(1)}, f32[136,128]{1,0:T(8,128)S(1)}, u32[]{:S(2)}, u32[]{:S(2)}) collective-permute-start(f32[136,128]{1,0:T(8,128)S(1)} %block_products.1.refs_0_), channel_id=1, source_target_pairs={{0,8},{1,9},{2,10},{3,11},{4,12},{5,13},{6,14},{7,15},{8,0},{9,1},... | collective-permute-start | bytes 208904 | tf_op jit(solution)/shard_map/ppermute | solution.py:228
  14.8 0.6 %collective-permute-done.8.refs_4_ = f32[136,128]{1,0:T(8,128)S(1)} collective-permute-done((f32[136,128]{1,0:T(8,128)S(1)}, f32[136,128]{1,0:T(8,128)S(1)}, u32[]{:S(2)}, u32[]{:S(2)}) %collective-permute-start.8) | collective-permute-done | bytes 69664 | tf_op jit(solution)/shard_map/ppermute | solution.py:298
  15.4 0.0 collective-permute-start.11
  15.5 1.1 %collective-permute-done.7.refs_3_ = f32[136,128]{1,0:T(8,128)S(1)} collective-permute-done((f32[136,128]{1,0:T(8,128)S(1)}, f32[136,128]{1,0:T(8,128)S(1)}, u32[]{:S(2)}, u32[]{:S(2)}) %collective-permute-start.7) | collective-permute-done | bytes 69664 | tf_op jit(solution)/shard_map/ppermute | solution.py:298
  16.5 0.0 collective-permute-start.10
  16.5 0.0 collective-permute-done.6.refs_2_
  16.5 0.5 %collective-permute-start.9 = (f32[136,128]{1,0:T(8,128)S(1)}, f32[136,128]{1,0:T(8,128)S(1)}, u32[]{:S(2)}, u32[]{:S(2)}) collective-permute-start(f32[136,128]{1,0:T(8,128)S(1)} %collective-permute-done.6.refs_2_), channel_id=1, source_target_pairs={{0,8},{1,9},{2,10},{3,11},{4,12},{5,13},{6,14},{7,15},{8,0},{9,1},... | collective-permute-start | bytes 208904 | tf_op jit(solution)/shard_map/ppermute | solution.py:228
  17.0 0.0 collective-permute-done.5.refs_1_
  17.0 0.0 collective-permute-done.11.refs_7_
  17.0 0.7 %collective-permute-done.10.refs_6_ = f32[136,128]{1,0:T(8,128)S(1)} collective-permute-done((f32[136,128]{1,0:T(8,128)S(1)}, f32[136,128]{1,0:T(8,128)S(1)}, u32[]{:S(2)}, u32[]{:S(2)}) %collective-permute-start.10) | collective-permute-done | bytes 69664 | tf_op jit(solution)/shard_map/ppermute | solution.py:228
  17.8 0.2 collective-permute-done.9.refs_5_
  17.9 0.2 sum_by_owner.1
  18.1 3.6 %collective-permute-start.12 = (f32[64,128]{1,0:T(8,128)S(1)}, f32[64,128]{1,0:T(8,128)S(1)}, u32[]{:S(2)}, u32[]{:S(2)}) collective-permute-start(f32[64,128]{1,0:T(8,128)S(1)} %get-tuple-element.40), channel_id=1, source_target_pairs={{0,14},{1,15},{2,12},{3,13},{4,10},{5,11},{6,8},{7,9},{8,6},{9,7},... | collective-permute-start | bytes 98312 | tf_op jit(solution)/shard_map/ppermute | solution.py:228
  21.8 0.0 collective-permute-start.13
  21.8 0.5 %collective-permute-start.14 = (f32[64,128]{1,0:T(8,128)S(1)}, f32[64,128]{1,0:T(8,128)S(1)}, u32[]{:S(2)}, u32[]{:S(2)}) collective-permute-start(f32[64,128]{1,0:T(8,128)S(1)} %get-tuple-element.42), channel_id=1, source_target_pairs={{0,10},{1,11},{2,8},{3,9},{4,14},{5,15},{6,12},{7,13},{8,2},{9,3},... | collective-permute-start | bytes 98312 | tf_op jit(solution)/shard_map/ppermute | solution.py:228
  22.3 0.0 collective-permute-done.3.refs_1_
  22.3 0.0 copy-done.1
  22.3 1.7 %prepare_sweep.1 = (f32[128,8,64]{2,1,0:T(8,128)S(1)}, f32[960,8,64]{2,1,0:T(8,128)S(1)}, f32[128,64]{1,0:T(8,128)S(1)}, f32[128,64]{1,0:T(8,128)S(1)}) custom-call(f32[2,128,128]{2,1,0:T(8,128)S(1)} %chip_gram.1.refs_0_, f32[2,128,128]{2,1,0:T(8,128)S(1)} %collective-permute-done.3.refs_1_, f32[64,128]{1,0:T(8,128)S(1)} %copy-done.1), custom_call_target="tpu_custom_call" | custom-call | tf_op jit(solution)/shard_map/prepare_sweep/pallas_call | solution.py:301
  24.0 0.0 collective-permute-done.12.refs_1_
  24.0 2.0 %collective-permute-done.13.refs_2_ = f32[64,128]{1,0:T(8,128)S(1)} collective-permute-done((f32[64,128]{1,0:T(8,128)S(1)}, f32[64,128]{1,0:T(8,128)S(1)}, u32[]{:S(2)}, u32[]{:S(2)}) %collective-permute-start.13) | collective-permute-done | bytes 32800 | tf_op jit(solution)/shard_map/ppermute | solution.py:228
  26.0 0.0 collective-permute-done.14.refs_3_
  26.0 1.2 %sweep.1 = f32[64,128]{1,0:T(8,128)} custom-call(f32[128,8,64]{2,1,0:T(8,128)S(1)} %get-tuple-element.27.within_ref, f32[960,8,64]{2,1,0:T(8,128)S(1)} %get-tuple-element.28.after_ref, f32[128,64]{1,0:T(8,128)S(1)} %get-tuple-element.29.pre_ref, f32[128,64]{1,0:T(8,128)S(1)} %get-tuple-element.30.scale_ref, f32[64,128]{1,0:T(8,128)S(1)} %get-tuple-element.39.refs_0_, ...), custom_call_target="tpu_custom_call" | custom-call | tf_op jit(solution)/shard_map/sweep/pallas_call | solution.py:327
Async XLA Ops:
  0.0 8.8 %copy-start = (bf16[2,64,4096]{2,1,0:T(8,128)(2,1)S(1)}, bf16[2,64,4096]{2,1,0:T(8,128)(2,1)}, u32[]{:S(2)}) copy-start(bf16[2,64,4096]{2,1,0:T(8,128)(2,1)} %refs_1_.1) | copy-start | bytes 3145732
  0.0 22.3 %copy-start.1 = (f32[64,128]{1,0:T(8,128)S(1)}, f32[64,128]{1,0:T(8,128)}, u32[]{:S(2)}) copy-start(f32[64,128]{1,0:T(8,128)} %refs_2_.1) | copy-start | bytes 98308
  0.0 4.2 %collective-permute-start.1 = (bf16[1024,128]{1,0:T(8,128)(2,1)}, bf16[1024,128]{1,0:T(8,128)(2,1)S(1)}, u32[]{:S(2)}, u32[]{:S(2)}) collective-permute-start(bf16[1024,128]{1,0:T(8,128)(2,1)} %b_ref.1), channel_id=1, source_target_pairs={{0,8},{1,9},{2,10},{3,11},{4,12},{5,13},{6,14},{7,15},{8,0},{9,1},... | collective-permute-start | bytes 786440 | tf_op jit(solution)/shard_map/ppermute | solution.py:228
  0.5 3.7 %collective-permute-start.2 = (bf16[1024,128]{1,0:T(8,128)(2,1)}, bf16[1024,128]{1,0:T(8,128)(2,1)S(1)}, u32[]{:S(2)}, u32[]{:S(2)}) collective-permute-start(bf16[1024,128]{1,0:T(8,128)(2,1)} %c_ref.1), channel_id=1, source_target_pairs={{0,8},{1,9},{2,10},{3,11},{4,12},{5,13},{6,14},{7,15},{8,0},{9,1},... | collective-permute-start | bytes 786440 | tf_op jit(solution)/shard_map/ppermute | solution.py:228
  0.5 4.2 %collective-permute-start = (s32[2,3]{1,0:T(2,128)}, s32[2,3]{1,0:T(2,128)S(1)}, u32[]{:S(2)}, u32[]{:S(2)}) collective-permute-start(s32[2,3]{1,0:T(2,128)} %ask_ref.1), channel_id=1, source_target_pairs={{0,24},{1,25},{2,26},{3,27},{4,28},{5,29},{6,30},{7,31},{8,16},{9,... | collective-permute-start | bytes 80 | tf_op jit(solution)/shard_map/ppermute | solution.py:228
  4.9 3.9 %collective-permute-start.4 = (bf16[4,64,128]{2,1,0:T(8,128)(2,1)S(1)}, bf16[4,64,128]{2,1,0:T(8,128)(2,1)S(1)}, u32[]{:S(2)}, u32[]{:S(2)}) collective-permute-start(bf16[4,64,128]{2,1,0:T(8,128)(2,1)S(1)} %gather_rows.1), channel_id=1, source_target_pairs={{0,24},{1,25},{2,26},{3,27},{4,28},{5,29},{6,30},{7,31},{8,16},{9,... | collective-permute-start | bytes 196616 | tf_op jit(solution)/shard_map/ppermute | solution.py:228
  6.6 0.7 %copy-start.2 = (s32[2,3]{1,0:T(2,128)S(1)}, s32[2,3]{1,0:T(2,128)}, u32[]{:S(2)}) copy-start(s32[2,3]{1,0:T(2,128)} %ask_ref.1) | copy-start | bytes 76
  9.2 6.2 %collective-permute-start.8 = (f32[136,128]{1,0:T(8,128)S(1)}, f32[136,128]{1,0:T(8,128)S(1)}, u32[]{:S(2)}, u32[]{:S(2)}) collective-permute-start(f32[136,128]{1,0:T(8,128)S(1)} %block_products.1.refs_0_), channel_id=1, source_target_pairs={{0,17},{1,8},{2,19},{3,10},{4,21},{5,12},{6,23},{7,14},{8,1},{9,24... | collective-permute-start | bytes 208904 | tf_op jit(solution)/shard_map/ppermute | solution.py:298
  12.4 4.1 %collective-permute-start.7 = (f32[136,128]{1,0:T(8,128)S(1)}, f32[136,128]{1,0:T(8,128)S(1)}, u32[]{:S(2)}, u32[]{:S(2)}) collective-permute-start(f32[136,128]{1,0:T(8,128)S(1)} %block_products.1.refs_0_), channel_id=1, source_target_pairs={{0,24},{1,25},{2,26},{3,27},{4,28},{5,29},{6,30},{7,31},{8,16},{9,... | collective-permute-start | bytes 208904 | tf_op jit(solution)/shard_map/ppermute | solution.py:298
  12.4 4.1 %collective-permute-start.6 = (f32[136,128]{1,0:T(8,128)S(1)}, f32[136,128]{1,0:T(8,128)S(1)}, u32[]{:S(2)}, u32[]{:S(2)}) collective-permute-start(f32[136,128]{1,0:T(8,128)S(1)} %block_products.1.refs_0_), channel_id=1, source_target_pairs={{0,9},{1,16},{2,11},{3,18},{4,13},{5,20},{6,15},{7,22},{8,25},{9,0... | collective-permute-start | bytes 208904 | tf_op jit(solution)/shard_map/ppermute | solution.py:298
  12.8 9.5 %collective-permute-start.3 = (f32[2,128,128]{2,1,0:T(8,128)S(1)}, f32[2,128,128]{2,1,0:T(8,128)S(1)}, u32[]{:S(2)}, u32[]{:S(2)}) collective-permute-start(f32[2,128,128]{2,1,0:T(8,128)S(1)} %chip_gram.1.refs_0_), channel_id=1, source_target_pairs={{0,24},{1,25},{2,26},{3,27},{4,28},{5,29},{6,30},{7,31},{8,16},{9,... | collective-permute-start | bytes 393224 | tf_op jit(solution)/shard_map/ppermute | solution.py:228
  14.2 2.8 %collective-permute-start.5 = (f32[136,128]{1,0:T(8,128)S(1)}, f32[136,128]{1,0:T(8,128)S(1)}, u32[]{:S(2)}, u32[]{:S(2)}) collective-permute-start(f32[136,128]{1,0:T(8,128)S(1)} %block_products.1.refs_0_), channel_id=1, source_target_pairs={{0,8},{1,9},{2,10},{3,11},{4,12},{5,13},{6,14},{7,15},{8,0},{9,1},... | collective-permute-start | bytes 208904 | tf_op jit(solution)/shard_map/ppermute | solution.py:228
  15.4 1.6 %collective-permute-start.11 = (f32[136,128]{1,0:T(8,128)S(1)}, f32[136,128]{1,0:T(8,128)S(1)}, u32[]{:S(2)}, u32[]{:S(2)}) collective-permute-start(f32[136,128]{1,0:T(8,128)S(1)} %collective-permute-done.8.refs_4_), channel_id=1, source_target_pairs={{0,8},{1,9},{2,10},{3,11},{4,12},{5,13},{6,14},{7,15},{8,0},{9,1},... | collective-permute-start | bytes 208904 | tf_op jit(solution)/shard_map/ppermute | solution.py:228
  16.5 1.3 %collective-permute-start.10 = (f32[136,128]{1,0:T(8,128)S(1)}, f32[136,128]{1,0:T(8,128)S(1)}, u32[]{:S(2)}, u32[]{:S(2)}) collective-permute-start(f32[136,128]{1,0:T(8,128)S(1)} %collective-permute-done.7.refs_3_), channel_id=1, source_target_pairs={{0,8},{1,9},{2,10},{3,11},{4,12},{5,13},{6,14},{7,15},{8,0},{9,1},... | collective-permute-start | bytes 208904 | tf_op jit(solution)/shard_map/ppermute | solution.py:228
  16.5 1.4 %collective-permute-start.9 = (f32[136,128]{1,0:T(8,128)S(1)}, f32[136,128]{1,0:T(8,128)S(1)}, u32[]{:S(2)}, u32[]{:S(2)}) collective-permute-start(f32[136,128]{1,0:T(8,128)S(1)} %collective-permute-done.6.refs_2_), channel_id=1, source_target_pairs={{0,8},{1,9},{2,10},{3,11},{4,12},{5,13},{6,14},{7,15},{8,0},{9,1},... | collective-permute-start | bytes 208904 | tf_op jit(solution)/shard_map/ppermute | solution.py:228
  18.1 5.8 %collective-permute-start.12 = (f32[64,128]{1,0:T(8,128)S(1)}, f32[64,128]{1,0:T(8,128)S(1)}, u32[]{:S(2)}, u32[]{:S(2)}) collective-permute-start(f32[64,128]{1,0:T(8,128)S(1)} %get-tuple-element.40), channel_id=1, source_target_pairs={{0,14},{1,15},{2,12},{3,13},{4,10},{5,11},{6,8},{7,9},{8,6},{9,7},... | collective-permute-start | bytes 98312 | tf_op jit(solution)/shard_map/ppermute | solution.py:228
  21.8 4.2 %collective-permute-start.13 = (f32[64,128]{1,0:T(8,128)S(1)}, f32[64,128]{1,0:T(8,128)S(1)}, u32[]{:S(2)}, u32[]{:S(2)}) collective-permute-start(f32[64,128]{1,0:T(8,128)S(1)} %get-tuple-element.41), channel_id=1, source_target_pairs={{0,12},{1,13},{2,14},{3,15},{4,8},{5,9},{6,10},{7,11},{8,4},{9,5},... | collective-permute-start | bytes 98312 | tf_op jit(solution)/shard_map/ppermute | solution.py:228
  21.8 4.2 %collective-permute-start.14 = (f32[64,128]{1,0:T(8,128)S(1)}, f32[64,128]{1,0:T(8,128)S(1)}, u32[]{:S(2)}, u32[]{:S(2)}) collective-permute-start(f32[64,128]{1,0:T(8,128)S(1)} %get-tuple-element.42), channel_id=1, source_target_pairs={{0,10},{1,11},{2,8},{3,9},{4,14},{5,15},{6,12},{7,13},{8,2},{9,3},... | collective-permute-start | bytes 98312 | tf_op jit(solution)/shard_map/ppermute | solution.py:228

commit v7 on v6

--- a/solution.py
+++ b/solution.py
@@ -113,12 +113,12 @@
     out_ref[nblk * BS :] = first_ref[...]
 
 
-def owner_kernel(nblk, n_rep, near, ab, count, *refs):
+def owner_kernel(places, nblk, n_rep, near, ab, count, *refs):
     arrived, outs = refs[:count], refs[count:]
     my_x, core, rep = here()
     line = n_rep // near
     at, side = lax.div(rep, near), lax.rem(rep, near)
-    for offset, out in enumerate(outs):
+    for offset, out in zip(places, outs):
         if line & (line - 1) == 0:
             to_at = lax.bitwise_xor(at, offset)
         else:
@@ -314,15 +314,21 @@
     )(*grams, factor_a)
     arrived = [partial, move(partial, 0, 1), *others, *(move(value, 0, 1) for value in others)]
 
-    sums = pl.pallas_call(
-        functools.partial(owner_kernel, nblk, n_rep, near, ab, len(arrived)),
-        out_shape=[jax.ShapeDtypeStruct(factor_a.shape, jnp.float32)] * line,
-        in_specs=[VMEM] * len(arrived),
-        out_specs=[VMEM] * line,
-        compiler_params=params,
-        name="sum_by_owner",
-    )(*arrived)
-    sums = [sums[0]] + [move(sums[d], 0, 1, 0, d) for d in range(line - 1, 0, -1)]
+    def sums_for(places, inputs, name):
+        return pl.pallas_call(
+            functools.partial(owner_kernel, places, nblk, n_rep, near, ab, len(inputs)),
+            out_shape=[jax.ShapeDtypeStruct(factor_a.shape, jnp.float32)] * len(places),
+            in_specs=[VMEM] * len(inputs),
+            out_specs=[VMEM] * len(places),
+            compiler_params=params,
+            name=name,
+        )(*inputs)
+
+    order = range(line - 1, 0, -1)
+    leaving = sums_for(order, arrived, "sums_to_send")
+    arrived, leaving = lax.optimization_barrier((arrived, leaving))
+    staying = sums_for((0,), arrived, "own_sum")
+    sums = [*staying] + [move(value, 0, 1, 0, d) for d, value in zip(order, leaving)]
 
     return pl.pallas_call(
         sweep_kernel,

time: 27.4 us -> 27.4 us (level)
  no operation moved by 1% of the time
where the time goes in v7:
time: 27.4 us; the launch traced here: 27.3 us
  starting transfers between devices  15.1 us (55%)
  waiting for transfers between devices  5.92 us (22%)
  Pallas kernels  5.52 us (20%)
  local copies, waits for them, and re-layouts  0.69 us (3%)
    ppermute x12, starting transfers between devices, move(): return lax.ppermute(value, ('grp', 'rep'), moves(n_grp, n_rep, to))  11.5 us
    ppermute x12, waiting for transfers between devices, move(): return lax.ppermute(value, ('grp', 'rep'), moves(n_grp, n_rep, to))  4.22 us
    ppermute x3, starting transfers between devices, spread(): return lax.ppermute(value, ('grp', 'rep'), moves(n_grp, n_rep, to))  3.56 us
    pallas_call x1, Pallas kernels, body(): pl.pallas_call(functools.partial(prepare_kernel, n_x), out_shape=[jax.Sha...  1.71 us
    ppermute x3, waiting for transfers between devices, spread(): return lax.ppermute(value, ('grp', 'rep'), moves(n_grp, n_rep, to))  1.7 us
    pallas_call x1, Pallas kernels, body(): pl.pallas_call(sweep_kernel, out_shape=jax.ShapeDtypeStruct(factor_a.shap...  1.31 us
    pallas_call x1, Pallas kernels, body(): pl.pallas_call(load_kernel, out_shape=[jax.ShapeDtypeStruct(factor_b.shap...  1.04 us
    unnamed x6, local copies, waits for them, and re-layouts  0.69 us
  transfers between devices with their start and end apart: 15, of which 6 were waited for; matrix products, arithmetic and copies ran while one was open for 0% of the time, Pallas kernels for 13%

profile of v7, /device:TPU:0, one launch (start us, length us, event | category | flops | bytes accessed | tf_op | source)
XLA Modules:
  0.0 27.3 jit_solution(15322059438930813570)
XLA Ops:
  0.0 0.0 copy-start
  0.0 0.0 copy-start.1
  0.0 0.5 %collective-permute-start.1 = (bf16[1024,128]{1,0:T(8,128)(2,1)}, bf16[1024,128]{1,0:T(8,128)(2,1)S(1)}, u32[]{:S(2)}, u32[]{:S(2)}) collective-permute-start(bf16[1024,128]{1,0:T(8,128)(2,1)} %b_ref.1), channel_id=1, source_target_pairs={{0,8},{1,9},{2,10},{3,11},{4,12},{5,13},{6,14},{7,15},{8,0},{9,1},... | collective-permute-start | bytes 786440 | tf_op jit(solution)/shard_map/ppermute | solution.py:228
  0.5 0.1 collective-permute-start.2
  0.5 2.6 %collective-permute-start = (s32[2,3]{1,0:T(2,128)}, s32[2,3]{1,0:T(2,128)S(1)}, u32[]{:S(2)}, u32[]{:S(2)}) collective-permute-start(s32[2,3]{1,0:T(2,128)} %ask_ref.1), channel_id=1, source_target_pairs={{0,24},{1,25},{2,26},{3,27},{4,28},{5,29},{6,30},{7,31},{8,16},{9,... | collective-permute-start | bytes 80 | tf_op jit(solution)/shard_map/ppermute | solution.py:228
  3.1 1.0 %load_shards.1 = (bf16[1024,128]{1,0:T(8,128)(2,1)S(1)}, bf16[1024,128]{1,0:T(8,128)(2,1)S(1)}) custom-call(bf16[1024,128]{1,0:T(8,128)(2,1)} %b_ref.1, bf16[1024,128]{1,0:T(8,128)(2,1)} %c_ref.1), custom_call_target="tpu_custom_call" | custom-call | tf_op jit(solution)/shard_map/load_shards/pallas_call | solution.py:233
  4.2 0.0 collective-permute-done.1.refs_2_.mate_b.refs_1_
  4.2 0.0 collective-permute-done.2.refs_4_.mate_c.refs_3_
  4.2 0.5 %chip_gram.1.refs_0_ = f32[2,128,128]{2,1,0:T(8,128)S(1)} custom-call(bf16[1024,128]{1,0:T(8,128)(2,1)S(1)} %get-tuple-element.34.refs_1_.own_b.refs_0_, bf16[1024,128]{1,0:T(8,128)(2,1)S(1)} %collective-permute-done.1.refs_2_.mate_b.refs_1_, bf16[1024,128]{1,0:T(8,128)(2,1)S(1)} %get-tuple-element.35.refs_3_.own_c.refs_2_, ...), custom_call_target="tpu_custom_call" | custom-call | tf_op jit(solution)/shard_map/chip_gram/pallas_call | solution.py:247
  4.7 0.0 collective-permute-done.refs_0_
  4.7 0.1 gather_rows.1
  4.9 1.7 %collective-permute-start.4 = (bf16[4,64,128]{2,1,0:T(8,128)(2,1)S(1)}, bf16[4,64,128]{2,1,0:T(8,128)(2,1)S(1)}, u32[]{:S(2)}, u32[]{:S(2)}) collective-permute-start(bf16[4,64,128]{2,1,0:T(8,128)(2,1)S(1)} %gather_rows.1), channel_id=1, source_target_pairs={{0,24},{1,25},{2,26},{3,27},{4,28},{5,29},{6,30},{7,31},{8,16},{9,... | collective-permute-start | bytes 196616 | tf_op jit(solution)/shard_map/ppermute | solution.py:228
  6.6 0.0 copy-start.2
  6.6 0.7 %copy-done.2 = s32[2,3]{1,0:T(2,128)S(1)} copy-done((s32[2,3]{1,0:T(2,128)S(1)}, s32[2,3]{1,0:T(2,128)}, u32[]{:S(2)}) %copy-start.2) | copy-done | bytes 48
  7.3 0.1 local_rows.1
  7.4 1.4 %collective-permute-done.4.refs_0_ = bf16[4,64,128]{2,1,0:T(8,128)(2,1)S(1)} collective-permute-done((bf16[4,64,128]{2,1,0:T(8,128)(2,1)S(1)}, bf16[4,64,128]{2,1,0:T(8,128)(2,1)S(1)}, u32[]{:S(2)}, u32[]{:S(2)}) %collective-permute-start.4) | collective-permute-done | bytes 65568 | tf_op jit(solution)/shard_map/ppermute | solution.py:228
  8.8 0.0 copy-done
  8.8 0.4 %block_products.1.refs_0_ = f32[136,128]{1,0:T(8,128)S(1)} custom-call(bf16[4,64,128]{2,1,0:T(8,128)(2,1)S(1)} %get-tuple-element.45.rows_ref, s32[4,8,128]{2,1,0:T(8,128)S(1)} %get-tuple-element.46.far_ref, f32[8,128]{1,0:T(8,128)S(1)} %get-tuple-element.47.first_ref, bf16[4,64,128]{2,1,0:T(8,128)(2,1)S(1)} %collective-permute-done.4.refs_0_, ...), custom_call_target="tpu_custom_call" | custom-call | tf_op jit(solution)/shard_map/block_products/pallas_call | solution.py:282
  9.2 3.2 %collective-permute-start.8 = (f32[136,128]{1,0:T(8,128)S(1)}, f32[136,128]{1,0:T(8,128)S(1)}, u32[]{:S(2)}, u32[]{:S(2)}) collective-permute-start(f32[136,128]{1,0:T(8,128)S(1)} %block_products.1.refs_0_), channel_id=1, source_target_pairs={{0,17},{1,8},{2,19},{3,10},{4,21},{5,12},{6,23},{7,14},{8,1},{9,24... | collective-permute-start | bytes 208904 | tf_op jit(solution)/shard_map/ppermute | solution.py:298
  12.4 0.0 collective-permute-start.7
  12.4 0.4 %collective-permute-start.6 = (f32[136,128]{1,0:T(8,128)S(1)}, f32[136,128]{1,0:T(8,128)S(1)}, u32[]{:S(2)}, u32[]{:S(2)}) collective-permute-start(f32[136,128]{1,0:T(8,128)S(1)} %block_products.1.refs_0_), channel_id=1, source_target_pairs={{0,9},{1,16},{2,11},{3,18},{4,13},{5,20},{6,15},{7,22},{8,25},{9,0... | collective-permute-start | bytes 208904 | tf_op jit(solution)/shard_map/ppermute | solution.py:298
  12.8 1.4 %collective-permute-start.3 = (f32[2,128,128]{2,1,0:T(8,128)S(1)}, f32[2,128,128]{2,1,0:T(8,128)S(1)}, u32[]{:S(2)}, u32[]{:S(2)}) collective-permute-start(f32[2,128,128]{2,1,0:T(8,128)S(1)} %chip_gram.1.refs_0_), channel_id=1, source_target_pairs={{0,24},{1,25},{2,26},{3,27},{4,28},{5,29},{6,30},{7,31},{8,16},{9,... | collective-permute-start | bytes 393224 | tf_op jit(solution)/shard_map/ppermute | solution.py:228
  14.2 0.6 %collective-permute-start.5 = (f32[136,128]{1,0:T(8,128)S(1)}, f32[136,128]{1,0:T(8,128)S(1)}, u32[]{:S(2)}, u32[]{:S(2)}) collective-permute-start(f32[136,128]{1,0:T(8,128)S(1)} %block_products.1.refs_0_), channel_id=1, source_target_pairs={{0,8},{1,9},{2,10},{3,11},{4,12},{5,13},{6,14},{7,15},{8,0},{9,1},... | collective-permute-start | bytes 208904 | tf_op jit(solution)/shard_map/ppermute | solution.py:228
  14.8 0.6 %collective-permute-done.8.refs_4_ = f32[136,128]{1,0:T(8,128)S(1)} collective-permute-done((f32[136,128]{1,0:T(8,128)S(1)}, f32[136,128]{1,0:T(8,128)S(1)}, u32[]{:S(2)}, u32[]{:S(2)}) %collective-permute-start.8) | collective-permute-done | bytes 69664 | tf_op jit(solution)/shard_map/ppermute | solution.py:298
  15.4 0.0 collective-permute-start.11
  15.5 1.1 %collective-permute-done.7.refs_3_ = f32[136,128]{1,0:T(8,128)S(1)} collective-permute-done((f32[136,128]{1,0:T(8,128)S(1)}, f32[136,128]{1,0:T(8,128)S(1)}, u32[]{:S(2)}, u32[]{:S(2)}) %collective-permute-start.7) | collective-permute-done | bytes 69664 | tf_op jit(solution)/shard_map/ppermute | solution.py:298
  16.5 0.0 collective-permute-start.10
  16.5 0.0 collective-permute-done.6.refs_2_
  16.5 0.5 %collective-permute-start.9 = (f32[136,128]{1,0:T(8,128)S(1)}, f32[136,128]{1,0:T(8,128)S(1)}, u32[]{:S(2)}, u32[]{:S(2)}) collective-permute-start(f32[136,128]{1,0:T(8,128)S(1)} %collective-permute-done.6.refs_2_), channel_id=1, source_target_pairs={{0,8},{1,9},{2,10},{3,11},{4,12},{5,13},{6,14},{7,15},{8,0},{9,1},... | collective-permute-start | bytes 208904 | tf_op jit(solution)/shard_map/ppermute | solution.py:228
  17.0 0.0 collective-permute-done.5.refs_1_
  17.0 0.0 collective-permute-done.11.refs_7_
  17.0 0.7 %collective-permute-done.10.refs_6_ = f32[136,128]{1,0:T(8,128)S(1)} collective-permute-done((f32[136,128]{1,0:T(8,128)S(1)}, f32[136,128]{1,0:T(8,128)S(1)}, u32[]{:S(2)}, u32[]{:S(2)}) %collective-permute-start.10) | collective-permute-done | bytes 69664 | tf_op jit(solution)/shard_map/ppermute | solution.py:228
  17.8 0.2 collective-permute-done.9.refs_5_
  17.9 0.2 sums_to_send.1
  18.1 3.6 %collective-permute-start.12 = (f32[64,128]{1,0:T(8,128)S(1)}, f32[64,128]{1,0:T(8,128)S(1)}, u32[]{:S(2)}, u32[]{:S(2)}) collective-permute-start(f32[64,128]{1,0:T(8,128)S(1)} %get-tuple-element.60), channel_id=1, source_target_pairs={{0,14},{1,15},{2,12},{3,13},{4,10},{5,11},{6,8},{7,9},{8,6},{9,7},... | collective-permute-start | bytes 98312 | tf_op jit(solution)/shard_map/ppermute | solution.py:228
  21.7 0.0 collective-permute-start.13
  21.7 0.5 %collective-permute-start.14 = (f32[64,128]{1,0:T(8,128)S(1)}, f32[64,128]{1,0:T(8,128)S(1)}, u32[]{:S(2)}, u32[]{:S(2)}) collective-permute-start(f32[64,128]{1,0:T(8,128)S(1)} %get-tuple-element.62), channel_id=1, source_target_pairs={{0,10},{1,11},{2,8},{3,9},{4,14},{5,15},{6,12},{7,13},{8,2},{9,3},... | collective-permute-start | bytes 98312 | tf_op jit(solution)/shard_map/ppermute | solution.py:228
  22.2 0.0 collective-permute-done.3.refs_1_
  22.2 0.0 copy-done.1
  22.2 1.7 %prepare_sweep.1 = (f32[128,8,64]{2,1,0:T(8,128)S(1)}, f32[960,8,64]{2,1,0:T(8,128)S(1)}, f32[128,64]{1,0:T(8,128)S(1)}, f32[128,64]{1,0:T(8,128)S(1)}) custom-call(f32[2,128,128]{2,1,0:T(8,128)S(1)} %chip_gram.1.refs_0_, f32[2,128,128]{2,1,0:T(8,128)S(1)} %collective-permute-done.3.refs_1_, f32[64,128]{1,0:T(8,128)S(1)} %copy-done.1), custom_call_target="tpu_custom_call" | custom-call | tf_op jit(solution)/shard_map/prepare_sweep/pallas_call | solution.py:301
  23.9 0.1 own_sum.1.refs_0_
  24.0 0.0 collective-permute-done.12.refs_1_
  24.0 1.9 %collective-permute-done.13.refs_2_ = f32[64,128]{1,0:T(8,128)S(1)} collective-permute-done((f32[64,128]{1,0:T(8,128)S(1)}, f32[64,128]{1,0:T(8,128)S(1)}, u32[]{:S(2)}, u32[]{:S(2)}) %collective-permute-start.13) | collective-permute-done | bytes 32800 | tf_op jit(solution)/shard_map/ppermute | solution.py:228
  26.0 0.0 collective-permute-done.14.refs_3_
  26.0 1.3 %sweep.1 = f32[64,128]{1,0:T(8,128)} custom-call(f32[128,8,64]{2,1,0:T(8,128)S(1)} %get-tuple-element.37.within_ref, f32[960,8,64]{2,1,0:T(8,128)S(1)} %get-tuple-element.38.after_ref, f32[128,64]{1,0:T(8,128)S(1)} %get-tuple-element.39.pre_ref, f32[128,64]{1,0:T(8,128)S(1)} %get-tuple-element.40.scale_ref, f32[64,128]{1,0:T(8,128)S(1)} %own_sum.1.refs_0_, ...), custom_call_target="tpu_custom_call" | custom-call | tf_op jit(solution)/shard_map/sweep/pallas_call | solution.py:333
Async XLA Ops:
  0.0 8.8 %copy-start = (bf16[2,64,4096]{2,1,0:T(8,128)(2,1)S(1)}, bf16[2,64,4096]{2,1,0:T(8,128)(2,1)}, u32[]{:S(2)}) copy-start(bf16[2,64,4096]{2,1,0:T(8,128)(2,1)} %refs_1_.1) | copy-start | bytes 3145732
  0.0 22.2 %copy-start.1 = (f32[64,128]{1,0:T(8,128)S(1)}, f32[64,128]{1,0:T(8,128)}, u32[]{:S(2)}) copy-start(f32[64,128]{1,0:T(8,128)} %refs_2_.1) | copy-start | bytes 98308
  0.0 4.2 %collective-permute-start.1 = (bf16[1024,128]{1,0:T(8,128)(2,1)}, bf16[1024,128]{1,0:T(8,128)(2,1)S(1)}, u32[]{:S(2)}, u32[]{:S(2)}) collective-permute-start(bf16[1024,128]{1,0:T(8,128)(2,1)} %b_ref.1), channel_id=1, source_target_pairs={{0,8},{1,9},{2,10},{3,11},{4,12},{5,13},{6,14},{7,15},{8,0},{9,1},... | collective-permute-start | bytes 786440 | tf_op jit(solution)/shard_map/ppermute | solution.py:228
  0.5 3.7 %collective-permute-start.2 = (bf16[1024,128]{1,0:T(8,128)(2,1)}, bf16[1024,128]{1,0:T(8,128)(2,1)S(1)}, u32[]{:S(2)}, u32[]{:S(2)}) collective-permute-start(bf16[1024,128]{1,0:T(8,128)(2,1)} %c_ref.1), channel_id=1, source_target_pairs={{0,8},{1,9},{2,10},{3,11},{4,12},{5,13},{6,14},{7,15},{8,0},{9,1},... | collective-permute-start | bytes 786440 | tf_op jit(solution)/shard_map/ppermute | solution.py:228
  0.5 4.2 %collective-permute-start = (s32[2,3]{1,0:T(2,128)}, s32[2,3]{1,0:T(2,128)S(1)}, u32[]{:S(2)}, u32[]{:S(2)}) collective-permute-start(s32[2,3]{1,0:T(2,128)} %ask_ref.1), channel_id=1, source_target_pairs={{0,24},{1,25},{2,26},{3,27},{4,28},{5,29},{6,30},{7,31},{8,16},{9,... | collective-permute-start | bytes 80 | tf_op jit(solution)/shard_map/ppermute | solution.py:228
  4.9 3.9 %collective-permute-start.4 = (bf16[4,64,128]{2,1,0:T(8,128)(2,1)S(1)}, bf16[4,64,128]{2,1,0:T(8,128)(2,1)S(1)}, u32[]{:S(2)}, u32[]{:S(2)}) collective-permute-start(bf16[4,64,128]{2,1,0:T(8,128)(2,1)S(1)} %gather_rows.1), channel_id=1, source_target_pairs={{0,24},{1,25},{2,26},{3,27},{4,28},{5,29},{6,30},{7,31},{8,16},{9,... | collective-permute-start | bytes 196616 | tf_op jit(solution)/shard_map/ppermute | solution.py:228
  6.6 0.7 %copy-start.2 = (s32[2,3]{1,0:T(2,128)S(1)}, s32[2,3]{1,0:T(2,128)}, u32[]{:S(2)}) copy-start(s32[2,3]{1,0:T(2,128)} %ask_ref.1) | copy-start | bytes 76
  9.2 6.2 %collective-permute-start.8 = (f32[136,128]{1,0:T(8,128)S(1)}, f32[136,128]{1,0:T(8,128)S(1)}, u32[]{:S(2)}, u32[]{:S(2)}) collective-permute-start(f32[136,128]{1,0:T(8,128)S(1)} %block_products.1.refs_0_), channel_id=1, source_target_pairs={{0,17},{1,8},{2,19},{3,10},{4,21},{5,12},{6,23},{7,14},{8,1},{9,24... | collective-permute-start | bytes 208904 | tf_op jit(solution)/shard_map/ppermute | solution.py:298
  12.4 4.1 %collective-permute-start.7 = (f32[136,128]{1,0:T(8,128)S(1)}, f32[136,128]{1,0:T(8,128)S(1)}, u32[]{:S(2)}, u32[]{:S(2)}) collective-permute-start(f32[136,128]{1,0:T(8,128)S(1)} %block_products.1.refs_0_), channel_id=1, source_target_pairs={{0,24},{1,25},{2,26},{3,27},{4,28},{5,29},{6,30},{7,31},{8,16},{9,... | collective-permute-start | bytes 208904 | tf_op jit(solution)/shard_map/ppermute | solution.py:298
  12.4 4.1 %collective-permute-start.6 = (f32[136,128]{1,0:T(8,128)S(1)}, f32[136,128]{1,0:T(8,128)S(1)}, u32[]{:S(2)}, u32[]{:S(2)}) collective-permute-start(f32[136,128]{1,0:T(8,128)S(1)} %block_products.1.refs_0_), channel_id=1, source_target_pairs={{0,9},{1,16},{2,11},{3,18},{4,13},{5,20},{6,15},{7,22},{8,25},{9,0... | collective-permute-start | bytes 208904 | tf_op jit(solution)/shard_map/ppermute | solution.py:298
  12.8 9.4 %collective-permute-start.3 = (f32[2,128,128]{2,1,0:T(8,128)S(1)}, f32[2,128,128]{2,1,0:T(8,128)S(1)}, u32[]{:S(2)}, u32[]{:S(2)}) collective-permute-start(f32[2,128,128]{2,1,0:T(8,128)S(1)} %chip_gram.1.refs_0_), channel_id=1, source_target_pairs={{0,24},{1,25},{2,26},{3,27},{4,28},{5,29},{6,30},{7,31},{8,16},{9,... | collective-permute-start | bytes 393224 | tf_op jit(solution)/shard_map/ppermute | solution.py:228
  14.2 2.8 %collective-permute-start.5 = (f32[136,128]{1,0:T(8,128)S(1)}, f32[136,128]{1,0:T(8,128)S(1)}, u32[]{:S(2)}, u32[]{:S(2)}) collective-permute-start(f32[136,128]{1,0:T(8,128)S(1)} %block_products.1.refs_0_), channel_id=1, source_target_pairs={{0,8},{1,9},{2,10},{3,11},{4,12},{5,13},{6,14},{7,15},{8,0},{9,1},... | collective-permute-start | bytes 208904 | tf_op jit(solution)/shard_map/ppermute | solution.py:228
  15.4 1.6 %collective-permute-start.11 = (f32[136,128]{1,0:T(8,128)S(1)}, f32[136,128]{1,0:T(8,128)S(1)}, u32[]{:S(2)}, u32[]{:S(2)}) collective-permute-start(f32[136,128]{1,0:T(8,128)S(1)} %collective-permute-done.8.refs_4_), channel_id=1, source_target_pairs={{0,8},{1,9},{2,10},{3,11},{4,12},{5,13},{6,14},{7,15},{8,0},{9,1},... | collective-permute-start | bytes 208904 | tf_op jit(solution)/shard_map/ppermute | solution.py:228
  16.5 1.3 %collective-permute-start.10 = (f32[136,128]{1,0:T(8,128)S(1)}, f32[136,128]{1,0:T(8,128)S(1)}, u32[]{:S(2)}, u32[]{:S(2)}) collective-permute-start(f32[136,128]{1,0:T(8,128)S(1)} %collective-permute-done.7.refs_3_), channel_id=1, source_target_pairs={{0,8},{1,9},{2,10},{3,11},{4,12},{5,13},{6,14},{7,15},{8,0},{9,1},... | collective-permute-start | bytes 208904 | tf_op jit(solution)/shard_map/ppermute | solution.py:228
  16.5 1.4 %collective-permute-start.9 = (f32[136,128]{1,0:T(8,128)S(1)}, f32[136,128]{1,0:T(8,128)S(1)}, u32[]{:S(2)}, u32[]{:S(2)}) collective-permute-start(f32[136,128]{1,0:T(8,128)S(1)} %collective-permute-done.6.refs_2_), channel_id=1, source_target_pairs={{0,8},{1,9},{2,10},{3,11},{4,12},{5,13},{6,14},{7,15},{8,0},{9,1},... | collective-permute-start | bytes 208904 | tf_op jit(solution)/shard_map/ppermute | solution.py:228
  18.1 5.9 %collective-permute-start.12 = (f32[64,128]{1,0:T(8,128)S(1)}, f32[64,128]{1,0:T(8,128)S(1)}, u32[]{:S(2)}, u32[]{:S(2)}) collective-permute-start(f32[64,128]{1,0:T(8,128)S(1)} %get-tuple-element.60), channel_id=1, source_target_pairs={{0,14},{1,15},{2,12},{3,13},{4,10},{5,11},{6,8},{7,9},{8,6},{9,7},... | collective-permute-start | bytes 98312 | tf_op jit(solution)/shard_map/ppermute | solution.py:228
  21.7 4.2 %collective-permute-start.13 = (f32[64,128]{1,0:T(8,128)S(1)}, f32[64,128]{1,0:T(8,128)S(1)}, u32[]{:S(2)}, u32[]{:S(2)}) collective-permute-start(f32[64,128]{1,0:T(8,128)S(1)} %get-tuple-element.61), channel_id=1, source_target_pairs={{0,12},{1,13},{2,14},{3,15},{4,8},{5,9},{6,10},{7,11},{8,4},{9,5},... | collective-permute-start | bytes 98312 | tf_op jit(solution)/shard_map/ppermute | solution.py:228
  21.7 4.2 %collective-permute-start.14 = (f32[64,128]{1,0:T(8,128)S(1)}, f32[64,128]{1,0:T(8,128)S(1)}, u32[]{:S(2)}, u32[]{:S(2)}) collective-permute-start(f32[64,128]{1,0:T(8,128)S(1)} %get-tuple-element.62), channel_id=1, source_target_pairs={{0,10},{1,11},{2,8},{3,9},{4,14},{5,15},{6,12},{7,13},{8,2},{9,3},... | collective-permute-start | bytes 98312 | tf_op jit(solution)/shard_map/ppermute | solution.py:228

commit v8 on v7

--- a/solution.py
+++ b/solution.py
@@ -97,7 +97,7 @@
             rows = jnp.where(far_ref[slot, :1] == d, found[d - 1][slot], rows)
         return rows
 
-    step = 8
+    step = 16
     for n in range(nblk):
         left, right = rows_of(n, 0), rows_of(n, 1)
         rank = left.shape[1]

time: 27.4 us -> 27.4 us (level)
  no operation moved by 1% of the time
where the time goes in v8:
time: 27.4 us; the launch traced here: 27.3 us
  starting transfers between devices  15.1 us (55%)
  waiting for transfers between devices  5.92 us (22%)
  Pallas kernels  5.53 us (20%)
  local copies, waits for them, and re-layouts  0.69 us (3%)
    ppermute x12, starting transfers between devices, move(): return lax.ppermute(value, ('grp', 'rep'), moves(n_grp, n_rep, to))  11.5 us
    ppermute x12, waiting for transfers between devices, move(): return lax.ppermute(value, ('grp', 'rep'), moves(n_grp, n_rep, to))  4.22 us
    ppermute x3, starting transfers between devices, spread(): return lax.ppermute(value, ('grp', 'rep'), moves(n_grp, n_rep, to))  3.57 us
    pallas_call x1, Pallas kernels, body(): pl.pallas_call(functools.partial(prepare_kernel, n_x), out_shape=[jax.Sha...  1.71 us
    ppermute x3, waiting for transfers between devices, spread(): return lax.ppermute(value, ('grp', 'rep'), moves(n_grp, n_rep, to))  1.7 us
    pallas_call x1, Pallas kernels, body(): pl.pallas_call(sweep_kernel, out_shape=jax.ShapeDtypeStruct(factor_a.shap...  1.31 us
    pallas_call x1, Pallas kernels, body(): pl.pallas_call(load_kernel, out_shape=[jax.ShapeDtypeStruct(factor_b.shap...  1.04 us
    unnamed x6, local copies, waits for them, and re-layouts  0.69 us
  transfers between devices with their start and end apart: 15, of which 6 were waited for; matrix products, arithmetic and copies ran while one was open for 0% of the time, Pallas kernels for 13%

profile of v8, /device:TPU:0, one launch (start us, length us, event | category | flops | bytes accessed | tf_op | source)
XLA Modules:
  0.0 27.3 jit_solution(17265996423721700302)
XLA Ops:
  0.0 0.0 copy-start
  0.0 0.0 copy-start.1
  0.0 0.5 %collective-permute-start.1 = (bf16[1024,128]{1,0:T(8,128)(2,1)}, bf16[1024,128]{1,0:T(8,128)(2,1)S(1)}, u32[]{:S(2)}, u32[]{:S(2)}) collective-permute-start(bf16[1024,128]{1,0:T(8,128)(2,1)} %b_ref.1), channel_id=1, source_target_pairs={{0,8},{1,9},{2,10},{3,11},{4,12},{5,13},{6,14},{7,15},{8,0},{9,1},... | collective-permute-start | bytes 786440 | tf_op jit(solution)/shard_map/ppermute | solution.py:228
  0.5 0.1 collective-permute-start.2
  0.5 2.6 %collective-permute-start = (s32[2,3]{1,0:T(2,128)}, s32[2,3]{1,0:T(2,128)S(1)}, u32[]{:S(2)}, u32[]{:S(2)}) collective-permute-start(s32[2,3]{1,0:T(2,128)} %ask_ref.1), channel_id=1, source_target_pairs={{0,24},{1,25},{2,26},{3,27},{4,28},{5,29},{6,30},{7,31},{8,16},{9,... | collective-permute-start | bytes 80 | tf_op jit(solution)/shard_map/ppermute | solution.py:228
  3.1 1.0 %load_shards.1 = (bf16[1024,128]{1,0:T(8,128)(2,1)S(1)}, bf16[1024,128]{1,0:T(8,128)(2,1)S(1)}) custom-call(bf16[1024,128]{1,0:T(8,128)(2,1)} %b_ref.1, bf16[1024,128]{1,0:T(8,128)(2,1)} %c_ref.1), custom_call_target="tpu_custom_call" | custom-call | tf_op jit(solution)/shard_map/load_shards/pallas_call | solution.py:233
  4.2 0.0 collective-permute-done.1.refs_2_.mate_b.refs_1_
  4.2 0.0 collective-permute-done.2.refs_4_.mate_c.refs_3_
  4.2 0.5 %chip_gram.1.refs_0_ = f32[2,128,128]{2,1,0:T(8,128)S(1)} custom-call(bf16[1024,128]{1,0:T(8,128)(2,1)S(1)} %get-tuple-element.34.refs_1_.own_b.refs_0_, bf16[1024,128]{1,0:T(8,128)(2,1)S(1)} %collective-permute-done.1.refs_2_.mate_b.refs_1_, bf16[1024,128]{1,0:T(8,128)(2,1)S(1)} %get-tuple-element.35.refs_3_.own_c.refs_2_, ...), custom_call_target="tpu_custom_call" | custom-call | tf_op jit(solution)/shard_map/chip_gram/pallas_call | solution.py:247
  4.7 0.0 collective-permute-done.refs_0_
  4.7 0.1 gather_rows.1
  4.9 1.7 %collective-permute-start.4 = (bf16[4,64,128]{2,1,0:T(8,128)(2,1)S(1)}, bf16[4,64,128]{2,1,0:T(8,128)(2,1)S(1)}, u32[]{:S(2)}, u32[]{:S(2)}) collective-permute-start(bf16[4,64,128]{2,1,0:T(8,128)(2,1)S(1)} %gather_rows.1), channel_id=1, source_target_pairs={{0,24},{1,25},{2,26},{3,27},{4,28},{5,29},{6,30},{7,31},{8,16},{9,... | collective-permute-start | bytes 196616 | tf_op jit(solution)/shard_map/ppermute | solution.py:228
  6.6 0.0 copy-start.2
  6.6 0.7 %copy-done.2 = s32[2,3]{1,0:T(2,128)S(1)} copy-done((s32[2,3]{1,0:T(2,128)S(1)}, s32[2,3]{1,0:T(2,128)}, u32[]{:S(2)}) %copy-start.2) | copy-done | bytes 48
  7.3 0.1 local_rows.1
  7.4 1.4 %collective-permute-done.4.refs_0_ = bf16[4,64,128]{2,1,0:T(8,128)(2,1)S(1)} collective-permute-done((bf16[4,64,128]{2,1,0:T(8,128)(2,1)S(1)}, bf16[4,64,128]{2,1,0:T(8,128)(2,1)S(1)}, u32[]{:S(2)}, u32[]{:S(2)}) %collective-permute-start.4) | collective-permute-done | bytes 65568 | tf_op jit(solution)/shard_map/ppermute | solution.py:228
  8.8 0.0 copy-done
  8.8 0.5 %block_products.1.refs_0_ = f32[136,128]{1,0:T(8,128)S(1)} custom-call(bf16[4,64,128]{2,1,0:T(8,128)(2,1)S(1)} %get-tuple-element.45.rows_ref, s32[4,8,128]{2,1,0:T(8,128)S(1)} %get-tuple-element.46.far_ref, f32[8,128]{1,0:T(8,128)S(1)} %get-tuple-element.47.first_ref, bf16[4,64,128]{2,1,0:T(8,128)(2,1)S(1)} %collective-permute-done.4.refs_0_, ...), custom_call_target="tpu_custom_call" | custom-call | tf_op jit(solution)/shard_map/block_products/pallas_call | solution.py:282
  9.2 3.2 %collective-permute-start.8 = (f32[136,128]{1,0:T(8,128)S(1)}, f32[136,128]{1,0:T(8,128)S(1)}, u32[]{:S(2)}, u32[]{:S(2)}) collective-permute-start(f32[136,128]{1,0:T(8,128)S(1)} %block_products.1.refs_0_), channel_id=1, source_target_pairs={{0,17},{1,8},{2,19},{3,10},{4,21},{5,12},{6,23},{7,14},{8,1},{9,24... | collective-permute-start | bytes 208904 | tf_op jit(solution)/shard_map/ppermute | solution.py:298
  12.5 0.0 collective-permute-start.7
  12.5 0.4 %collective-permute-start.6 = (f32[136,128]{1,0:T(8,128)S(1)}, f32[136,128]{1,0:T(8,128)S(1)}, u32[]{:S(2)}, u32[]{:S(2)}) collective-permute-start(f32[136,128]{1,0:T(8,128)S(1)} %block_products.1.refs_0_), channel_id=1, source_target_pairs={{0,9},{1,16},{2,11},{3,18},{4,13},{5,20},{6,15},{7,22},{8,25},{9,0... | collective-permute-start | bytes 208904 | tf_op jit(solution)/shard_map/ppermute | solution.py:298
  12.8 1.4 %collective-permute-start.3 = (f32[2,128,128]{2,1,0:T(8,128)S(1)}, f32[2,128,128]{2,1,0:T(8,128)S(1)}, u32[]{:S(2)}, u32[]{:S(2)}) collective-permute-start(f32[2,128,128]{2,1,0:T(8,128)S(1)} %chip_gram.1.refs_0_), channel_id=1, source_target_pairs={{0,24},{1,25},{2,26},{3,27},{4,28},{5,29},{6,30},{7,31},{8,16},{9,... | collective-permute-start | bytes 393224 | tf_op jit(solution)/shard_map/ppermute | solution.py:228
  14.2 0.6 %collective-permute-start.5 = (f32[136,128]{1,0:T(8,128)S(1)}, f32[136,128]{1,0:T(8,128)S(1)}, u32[]{:S(2)}, u32[]{:S(2)}) collective-permute-start(f32[136,128]{1,0:T(8,128)S(1)} %block_products.1.refs_0_), channel_id=1, source_target_pairs={{0,8},{1,9},{2,10},{3,11},{4,12},{5,13},{6,14},{7,15},{8,0},{9,1},... | collective-permute-start | bytes 208904 | tf_op jit(solution)/shard_map/ppermute | solution.py:228
  14.8 0.6 %collective-permute-done.8.refs_4_ = f32[136,128]{1,0:T(8,128)S(1)} collective-permute-done((f32[136,128]{1,0:T(8,128)S(1)}, f32[136,128]{1,0:T(8,128)S(1)}, u32[]{:S(2)}, u32[]{:S(2)}) %collective-permute-start.8) | collective-permute-done | bytes 69664 | tf_op jit(solution)/shard_map/ppermute | solution.py:298
  15.5 0.0 collective-permute-start.11
  15.5 1.1 %collective-permute-done.7.refs_3_ = f32[136,128]{1,0:T(8,128)S(1)} collective-permute-done((f32[136,128]{1,0:T(8,128)S(1)}, f32[136,128]{1,0:T(8,128)S(1)}, u32[]{:S(2)}, u32[]{:S(2)}) %collective-permute-start.7) | collective-permute-done | bytes 69664 | tf_op jit(solution)/shard_map/ppermute | solution.py:298
  16.5 0.0 collective-permute-start.10
  16.5 0.0 collective-permute-done.6.refs_2_
  16.5 0.5 %collective-permute-start.9 = (f32[136,128]{1,0:T(8,128)S(1)}, f32[136,128]{1,0:T(8,128)S(1)}, u32[]{:S(2)}, u32[]{:S(2)}) collective-permute-start(f32[136,128]{1,0:T(8,128)S(1)} %collective-permute-done.6.refs_2_), channel_id=1, source_target_pairs={{0,8},{1,9},{2,10},{3,11},{4,12},{5,13},{6,14},{7,15},{8,0},{9,1},... | collective-permute-start | bytes 208904 | tf_op jit(solution)/shard_map/ppermute | solution.py:228
  17.0 0.0 collective-permute-done.5.refs_1_
  17.0 0.0 collective-permute-done.11.refs_7_
  17.0 0.7 %collective-permute-done.10.refs_6_ = f32[136,128]{1,0:T(8,128)S(1)} collective-permute-done((f32[136,128]{1,0:T(8,128)S(1)}, f32[136,128]{1,0:T(8,128)S(1)}, u32[]{:S(2)}, u32[]{:S(2)}) %collective-permute-start.10) | collective-permute-done | bytes 69664 | tf_op jit(solution)/shard_map/ppermute | solution.py:228
  17.8 0.2 collective-permute-done.9.refs_5_
  17.9 0.2 sums_to_send.1
  18.1 3.6 %collective-permute-start.12 = (f32[64,128]{1,0:T(8,128)S(1)}, f32[64,128]{1,0:T(8,128)S(1)}, u32[]{:S(2)}, u32[]{:S(2)}) collective-permute-start(f32[64,128]{1,0:T(8,128)S(1)} %get-tuple-element.60), channel_id=1, source_target_pairs={{0,14},{1,15},{2,12},{3,13},{4,10},{5,11},{6,8},{7,9},{8,6},{9,7},... | collective-permute-start | bytes 98312 | tf_op jit(solution)/shard_map/ppermute | solution.py:228
  21.7 0.0 collective-permute-start.13
  21.7 0.5 %collective-permute-start.14 = (f32[64,128]{1,0:T(8,128)S(1)}, f32[64,128]{1,0:T(8,128)S(1)}, u32[]{:S(2)}, u32[]{:S(2)}) collective-permute-start(f32[64,128]{1,0:T(8,128)S(1)} %get-tuple-element.62), channel_id=1, source_target_pairs={{0,10},{1,11},{2,8},{3,9},{4,14},{5,15},{6,12},{7,13},{8,2},{9,3},... | collective-permute-start | bytes 98312 | tf_op jit(solution)/shard_map/ppermute | solution.py:228
  22.2 0.0 collective-permute-done.3.refs_1_
  22.2 0.0 copy-done.1
  22.2 1.7 %prepare_sweep.1 = (f32[128,8,64]{2,1,0:T(8,128)S(1)}, f32[960,8,64]{2,1,0:T(8,128)S(1)}, f32[128,64]{1,0:T(8,128)S(1)}, f32[128,64]{1,0:T(8,128)S(1)}) custom-call(f32[2,128,128]{2,1,0:T(8,128)S(1)} %chip_gram.1.refs_0_, f32[2,128,128]{2,1,0:T(8,128)S(1)} %collective-permute-done.3.refs_1_, f32[64,128]{1,0:T(8,128)S(1)} %copy-done.1), custom_call_target="tpu_custom_call" | custom-call | tf_op jit(solution)/shard_map/prepare_sweep/pallas_call | solution.py:301
  23.9 0.1 own_sum.1.refs_0_
  24.0 0.0 collective-permute-done.12.refs_1_
  24.0 1.9 %collective-permute-done.13.refs_2_ = f32[64,128]{1,0:T(8,128)S(1)} collective-permute-done((f32[64,128]{1,0:T(8,128)S(1)}, f32[64,128]{1,0:T(8,128)S(1)}, u32[]{:S(2)}, u32[]{:S(2)}) %collective-permute-start.13) | collective-permute-done | bytes 32800 | tf_op jit(solution)/shard_map/ppermute | solution.py:228
  26.0 0.0 collective-permute-done.14.refs_3_
  26.0 1.3 %sweep.1 = f32[64,128]{1,0:T(8,128)} custom-call(f32[128,8,64]{2,1,0:T(8,128)S(1)} %get-tuple-element.37.within_ref, f32[960,8,64]{2,1,0:T(8,128)S(1)} %get-tuple-element.38.after_ref, f32[128,64]{1,0:T(8,128)S(1)} %get-tuple-element.39.pre_ref, f32[128,64]{1,0:T(8,128)S(1)} %get-tuple-element.40.scale_ref, f32[64,128]{1,0:T(8,128)S(1)} %own_sum.1.refs_0_, ...), custom_call_target="tpu_custom_call" | custom-call | tf_op jit(solution)/shard_map/sweep/pallas_call | solution.py:333
Async XLA Ops:
  0.0 8.8 %copy-start = (bf16[2,64,4096]{2,1,0:T(8,128)(2,1)S(1)}, bf16[2,64,4096]{2,1,0:T(8,128)(2,1)}, u32[]{:S(2)}) copy-start(bf16[2,64,4096]{2,1,0:T(8,128)(2,1)} %refs_1_.1) | copy-start | bytes 3145732
  0.0 22.2 %copy-start.1 = (f32[64,128]{1,0:T(8,128)S(1)}, f32[64,128]{1,0:T(8,128)}, u32[]{:S(2)}) copy-start(f32[64,128]{1,0:T(8,128)} %refs_2_.1) | copy-start | bytes 98308
  0.0 4.2 %collective-permute-start.1 = (bf16[1024,128]{1,0:T(8,128)(2,1)}, bf16[1024,128]{1,0:T(8,128)(2,1)S(1)}, u32[]{:S(2)}, u32[]{:S(2)}) collective-permute-start(bf16[1024,128]{1,0:T(8,128)(2,1)} %b_ref.1), channel_id=1, source_target_pairs={{0,8},{1,9},{2,10},{3,11},{4,12},{5,13},{6,14},{7,15},{8,0},{9,1},... | collective-permute-start | bytes 786440 | tf_op jit(solution)/shard_map/ppermute | solution.py:228
  0.5 3.7 %collective-permute-start.2 = (bf16[1024,128]{1,0:T(8,128)(2,1)}, bf16[1024,128]{1,0:T(8,128)(2,1)S(1)}, u32[]{:S(2)}, u32[]{:S(2)}) collective-permute-start(bf16[1024,128]{1,0:T(8,128)(2,1)} %c_ref.1), channel_id=1, source_target_pairs={{0,8},{1,9},{2,10},{3,11},{4,12},{5,13},{6,14},{7,15},{8,0},{9,1},... | collective-permute-start | bytes 786440 | tf_op jit(solution)/shard_map/ppermute | solution.py:228
  0.5 4.2 %collective-permute-start = (s32[2,3]{1,0:T(2,128)}, s32[2,3]{1,0:T(2,128)S(1)}, u32[]{:S(2)}, u32[]{:S(2)}) collective-permute-start(s32[2,3]{1,0:T(2,128)} %ask_ref.1), channel_id=1, source_target_pairs={{0,24},{1,25},{2,26},{3,27},{4,28},{5,29},{6,30},{7,31},{8,16},{9,... | collective-permute-start | bytes 80 | tf_op jit(solution)/shard_map/ppermute | solution.py:228
  4.9 3.9 %collective-permute-start.4 = (bf16[4,64,128]{2,1,0:T(8,128)(2,1)S(1)}, bf16[4,64,128]{2,1,0:T(8,128)(2,1)S(1)}, u32[]{:S(2)}, u32[]{:S(2)}) collective-permute-start(bf16[4,64,128]{2,1,0:T(8,128)(2,1)S(1)} %gather_rows.1), channel_id=1, source_target_pairs={{0,24},{1,25},{2,26},{3,27},{4,28},{5,29},{6,30},{7,31},{8,16},{9,... | collective-permute-start | bytes 196616 | tf_op jit(solution)/shard_map/ppermute | solution.py:228
  6.6 0.7 %copy-start.2 = (s32[2,3]{1,0:T(2,128)S(1)}, s32[2,3]{1,0:T(2,128)}, u32[]{:S(2)}) copy-start(s32[2,3]{1,0:T(2,128)} %ask_ref.1) | copy-start | bytes 76
  9.2 6.2 %collective-permute-start.8 = (f32[136,128]{1,0:T(8,128)S(1)}, f32[136,128]{1,0:T(8,128)S(1)}, u32[]{:S(2)}, u32[]{:S(2)}) collective-permute-start(f32[136,128]{1,0:T(8,128)S(1)} %block_products.1.refs_0_), channel_id=1, source_target_pairs={{0,17},{1,8},{2,19},{3,10},{4,21},{5,12},{6,23},{7,14},{8,1},{9,24... | collective-permute-start | bytes 208904 | tf_op jit(solution)/shard_map/ppermute | solution.py:298
  12.5 4.1 %collective-permute-start.7 = (f32[136,128]{1,0:T(8,128)S(1)}, f32[136,128]{1,0:T(8,128)S(1)}, u32[]{:S(2)}, u32[]{:S(2)}) collective-permute-start(f32[136,128]{1,0:T(8,128)S(1)} %block_products.1.refs_0_), channel_id=1, source_target_pairs={{0,24},{1,25},{2,26},{3,27},{4,28},{5,29},{6,30},{7,31},{8,16},{9,... | collective-permute-start | bytes 208904 | tf_op jit(solution)/shard_map/ppermute | solution.py:298
  12.5 4.1 %collective-permute-start.6 = (f32[136,128]{1,0:T(8,128)S(1)}, f32[136,128]{1,0:T(8,128)S(1)}, u32[]{:S(2)}, u32[]{:S(2)}) collective-permute-start(f32[136,128]{1,0:T(8,128)S(1)} %block_products.1.refs_0_), channel_id=1, source_target_pairs={{0,9},{1,16},{2,11},{3,18},{4,13},{5,20},{6,15},{7,22},{8,25},{9,0... | collective-permute-start | bytes 208904 | tf_op jit(solution)/shard_map/ppermute | solution.py:298
  12.8 9.4 %collective-permute-start.3 = (f32[2,128,128]{2,1,0:T(8,128)S(1)}, f32[2,128,128]{2,1,0:T(8,128)S(1)}, u32[]{:S(2)}, u32[]{:S(2)}) collective-permute-start(f32[2,128,128]{2,1,0:T(8,128)S(1)} %chip_gram.1.refs_0_), channel_id=1, source_target_pairs={{0,24},{1,25},{2,26},{3,27},{4,28},{5,29},{6,30},{7,31},{8,16},{9,... | collective-permute-start | bytes 393224 | tf_op jit(solution)/shard_map/ppermute | solution.py:228
  14.2 2.8 %collective-permute-start.5 = (f32[136,128]{1,0:T(8,128)S(1)}, f32[136,128]{1,0:T(8,128)S(1)}, u32[]{:S(2)}, u32[]{:S(2)}) collective-permute-start(f32[136,128]{1,0:T(8,128)S(1)} %block_products.1.refs_0_), channel_id=1, source_target_pairs={{0,8},{1,9},{2,10},{3,11},{4,12},{5,13},{6,14},{7,15},{8,0},{9,1},... | collective-permute-start | bytes 208904 | tf_op jit(solution)/shard_map/ppermute | solution.py:228
  15.5 1.6 %collective-permute-start.11 = (f32[136,128]{1,0:T(8,128)S(1)}, f32[136,128]{1,0:T(8,128)S(1)}, u32[]{:S(2)}, u32[]{:S(2)}) collective-permute-start(f32[136,128]{1,0:T(8,128)S(1)} %collective-permute-done.8.refs_4_), channel_id=1, source_target_pairs={{0,8},{1,9},{2,10},{3,11},{4,12},{5,13},{6,14},{7,15},{8,0},{9,1},... | collective-permute-start | bytes 208904 | tf_op jit(solution)/shard_map/ppermute | solution.py:228
  16.5 1.3 %collective-permute-start.10 = (f32[136,128]{1,0:T(8,128)S(1)}, f32[136,128]{1,0:T(8,128)S(1)}, u32[]{:S(2)}, u32[]{:S(2)}) collective-permute-start(f32[136,128]{1,0:T(8,128)S(1)} %collective-permute-done.7.refs_3_), channel_id=1, source_target_pairs={{0,8},{1,9},{2,10},{3,11},{4,12},{5,13},{6,14},{7,15},{8,0},{9,1},... | collective-permute-start | bytes 208904 | tf_op jit(solution)/shard_map/ppermute | solution.py:228
  16.5 1.4 %collective-permute-start.9 = (f32[136,128]{1,0:T(8,128)S(1)}, f32[136,128]{1,0:T(8,128)S(1)}, u32[]{:S(2)}, u32[]{:S(2)}) collective-permute-start(f32[136,128]{1,0:T(8,128)S(1)} %collective-permute-done.6.refs_2_), channel_id=1, source_target_pairs={{0,8},{1,9},{2,10},{3,11},{4,12},{5,13},{6,14},{7,15},{8,0},{9,1},... | collective-permute-start | bytes 208904 | tf_op jit(solution)/shard_map/ppermute | solution.py:228
  18.1 5.9 %collective-permute-start.12 = (f32[64,128]{1,0:T(8,128)S(1)}, f32[64,128]{1,0:T(8,128)S(1)}, u32[]{:S(2)}, u32[]{:S(2)}) collective-permute-start(f32[64,128]{1,0:T(8,128)S(1)} %get-tuple-element.60), channel_id=1, source_target_pairs={{0,14},{1,15},{2,12},{3,13},{4,10},{5,11},{6,8},{7,9},{8,6},{9,7},... | collective-permute-start | bytes 98312 | tf_op jit(solution)/shard_map/ppermute | solution.py:228
  21.7 4.2 %collective-permute-start.13 = (f32[64,128]{1,0:T(8,128)S(1)}, f32[64,128]{1,0:T(8,128)S(1)}, u32[]{:S(2)}, u32[]{:S(2)}) collective-permute-start(f32[64,128]{1,0:T(8,128)S(1)} %get-tuple-element.61), channel_id=1, source_target_pairs={{0,12},{1,13},{2,14},{3,15},{4,8},{5,9},{6,10},{7,11},{8,4},{9,5},... | collective-permute-start | bytes 98312 | tf_op jit(solution)/shard_map/ppermute | solution.py:228
  21.7 4.2 %collective-permute-start.14 = (f32[64,128]{1,0:T(8,128)S(1)}, f32[64,128]{1,0:T(8,128)S(1)}, u32[]{:S(2)}, u32[]{:S(2)}) collective-permute-start(f32[64,128]{1,0:T(8,128)S(1)} %get-tuple-element.62), channel_id=1, source_target_pairs={{0,10},{1,11},{2,8},{3,9},{4,14},{5,15},{6,12},{7,13},{8,2},{9,3},... | collective-permute-start | bytes 98312 | tf_op jit(solution)/shard_map/ppermute | solution.py:228
